TPU v7x, 32 devices: a whole 2x2x4 slice. The times are simulated.
32 devices in a mesh: dp: 8 (over y, x, core), fsdp: 4 (over z).
Axes of the slice: x: 2, y: 2, z: 4, core: 2. Of those that a mesh axis runs over, the one named last changes fastest.
Arguments:
- tokens: bfloat16 [32, 512, 1536], P(('dp', 'fsdp')), may hold values from -50 to 50
- conv_weight: bfloat16 [5, 1536, 1536], P(None, 'fsdp'), may hold values from -0.0625 to 0.0625
- query_weight: bfloat16 [1536, 512], P('fsdp'), may hold values from -0.15625 to 0.15625
- key_weight: bfloat16 [1536, 512], P('fsdp'), may hold values from -0.15625 to 0.15625
- value_weight: bfloat16 [1536, 1536], P('fsdp'), may hold values from -0.15625 to 0.15625
- out_weight: bfloat16 [1536, 1536], P('fsdp'), may hold values from -0.875 to 0.875
- rel_weight: bfloat16 [192, 512], P(None, 'fsdp'), may hold values from -1.25 to 1.25
- up_weight: bfloat16 [1536, 3072], P('fsdp'), may hold values from -0.15625 to 0.15625
- down_weight: bfloat16 [3072, 1536], P('fsdp'), may hold values from -0.109375 to 0.109375
- gains: float32 [3, 1536], P(None, 'fsdp'), may hold values from 0.5 to 1.5
- biases: float32 [6, 1536], P(None, 'fsdp'), may hold values from -2 to 2
- up_bias: float32 [3072], P('fsdp'), may hold values from -2 to 2
- rel_bias: float32 [2, 512], P(None, 'fsdp'), may hold values from -1 to 1
- target_table: float32 [64, 1536], replicated, may hold values from -6 to 6
- clip_levels: float32 [16], replicated, may hold values from 0.5 to 8
- window_ids: int32 [32], P(('dp', 'fsdp')), may hold values from 0 to 63
- clip_index: int32 [32, 512], P(('dp', 'fsdp')), may hold values from 0 to 15
Outputs:
- mixed: bfloat16 [32, 512, 1536], P(('dp', 'fsdp'))
- tokens_grad: bfloat16 [32, 512, 1536], P(('dp', 'fsdp'))
- conv_weight_grad: float32 [5, 1536, 1536], P(None, 'fsdp')
- query_weight_grad: float32 [1536, 512], P('fsdp')
- key_weight_grad: float32 [1536, 512], P('fsdp')
- value_weight_grad: float32 [1536, 1536], P('fsdp')
- out_weight_grad: float32 [1536, 1536], P('fsdp')
- rel_weight_grad: float32 [192, 512], P(None, 'fsdp')
- up_weight_grad: float32 [1536, 3072], P('fsdp')
- down_weight_grad: float32 [3072, 1536], P('fsdp')
- gains_grad: float32 [3, 1536], P(None, 'fsdp')
- biases_grad: float32 [6, 1536], P(None, 'fsdp')
- up_bias_grad: float32 [3072], P('fsdp')
- rel_bias_grad: float32 [2, 512], P(None, 'fsdp')
All inputs are finite; a program needn't handle non-finite values.
Results may differ from a plain program's by a relative error of at most 0.04.
Values may be sent and summed in bfloat16 or wider, within the bound.
A program may use at most 384 MiB of HBM per device.

v0:
```python
import math

import jax
import jax.numpy as jnp
from jax import lax
from jax.sharding import PartitionSpec as P

HEADS = 8
KEY = 64


EPSILON = 1e-05


def position_table(length, features):
    basis_count = features // 6
    offsets = jnp.arange(2 * length - 1, dtype=jnp.float32) - (length - 1)
    distance = jnp.abs(offsets)[:, None]
    max_range = math.log(length) / math.log(2.0)
    half_life = 2.0 ** jnp.linspace(3.0, max_range, basis_count, dtype=jnp.float32)
    decaying = jnp.exp(-math.log(2.0) / half_life[None, :] * distance)
    widths = 2.0 ** jnp.arange(1, basis_count + 1, dtype=jnp.float32) - 1.0
    central = (widths[None, :] > distance).astype(jnp.float32)
    stddev = length / (2.0 * basis_count)
    centres = jnp.linspace(length / basis_count, length, basis_count, dtype=jnp.float32)
    shape_par = (centres / stddev) ** 2
    rate_par = centres / stddev**2
    safe_dist = jnp.maximum(distance, 1.0)
    log_prob = (shape_par - 1.0) * jnp.log(safe_dist) - rate_par * safe_dist
    log_prob = log_prob - jnp.max(log_prob, axis=0, keepdims=True)
    gamma_feat = jnp.where(distance > 0.5, jnp.exp(log_prob), 0.0)
    symmetric = jnp.concatenate([decaying, central, gamma_feat], 1)
    sign_row = jnp.sign(offsets)[:, None]
    return jnp.concatenate([symmetric, sign_row * symmetric], 1)


def relative_shift(scores):
    row_count = scores.shape[-2]
    span_width = scores.shape[-1]
    leading = scores.shape[:-2]
    padded = jnp.pad(scores, [(0, 0)] * (scores.ndim - 1) + [(1, 0)])
    folded = padded.reshape(leading + (span_width + 1, row_count))[..., 1:, :]
    return folded.reshape(leading + (row_count, span_width))[..., :row_count]


def normalize(values):
    centred = values - jnp.mean(values, -1, keepdims=True)
    inverse = lax.rsqrt(jnp.mean(centred * centred, -1, keepdims=True) + EPSILON)
    return (centred * inverse, inverse)


def norm_back(grad_std, standard, inverse):
    return inverse * (
        grad_std
        - jnp.mean(grad_std, -1, keepdims=True)
        - standard * jnp.mean(grad_std * standard, -1, keepdims=True)
    )


def dot_leading(left_side, right_side):
    return lax.dot_general(
        left_side, right_side, (((0,), (0,)), ((), ())), preferred_element_type=jnp.float32
    )


def dot_trailing(left_side, right_side):
    return lax.dot_general(
        left_side, right_side, (((1,), (1,)), ((), ())), preferred_element_type=jnp.float32
    )


def attention_scores(content_query, key_heads, position_query, position_keys):
    content = jnp.einsum(
        "ihk,jhk->hij", content_query, key_heads, preferred_element_type=jnp.float32
    )
    relative = jnp.einsum(
        "ihk,mhk->him", position_query, position_keys, preferred_element_type=jnp.float32
    )
    return content + relative_shift(relative)


def on_device(
    tokens,
    conv_weight,
    query_weight,
    key_weight,
    value_weight,
    out_weight,
    rel_weight,
    up_weight,
    down_weight,
    gains,
    biases,
    up_bias,
    rel_bias,
    target_table,
    clip_levels,
    window_ids,
    clip_index,
):
    gathered = (
        lax.all_gather(conv_weight, "fsdp", axis=1, tiled=True),
        lax.all_gather(query_weight, "fsdp", axis=0, tiled=True),
        lax.all_gather(key_weight, "fsdp", axis=0, tiled=True),
        lax.all_gather(value_weight, "fsdp", axis=0, tiled=True),
        lax.all_gather(out_weight, "fsdp", axis=0, tiled=True),
        lax.all_gather(rel_weight, "fsdp", axis=1, tiled=True),
        lax.all_gather(up_weight, "fsdp", axis=0, tiled=True),
        lax.all_gather(down_weight, "fsdp", axis=0, tiled=True),
        lax.all_gather(gains.astype(jnp.bfloat16), "fsdp", axis=1, tiled=True).astype(gains.dtype),
        lax.all_gather(biases.astype(jnp.bfloat16), "fsdp", axis=1, tiled=True).astype(
            biases.dtype
        ),
        lax.all_gather(up_bias.astype(jnp.bfloat16), "fsdp", axis=0, tiled=True).astype(
            up_bias.dtype
        ),
        lax.all_gather(rel_bias.astype(jnp.bfloat16), "fsdp", axis=1, tiled=True).astype(
            rel_bias.dtype
        ),
    )
    (
        conv_full,
        query_full,
        key_full,
        value_full,
        out_full,
        rel_full,
        up_full,
        down_full,
        gain_rows,
        bias_rows,
        up_offset,
        rel_offset,
    ) = gathered
    inputs = tokens[0].astype(jnp.float32)
    length = inputs.shape[0]
    model_width = inputs.shape[1]
    tap_count = conv_full.shape[0]
    half_taps = tap_count // 2
    token_total = length * lax.axis_size("dp") * lax.axis_size("fsdp")
    batch_sums = lax.psum((jnp.sum(inputs, 0), jnp.sum(inputs * inputs, 0)), ("dp", "fsdp"))
    centre = batch_sums[0] / token_total
    variance = batch_sums[1] / token_total - centre * centre
    inverse = lax.rsqrt(variance + EPSILON)
    standard = (inputs - centre) * inverse
    normed = standard * gain_rows[0] + bias_rows[0]
    activated = jax.nn.gelu(normed).astype(jnp.bfloat16)
    padded = jnp.pad(activated, ((half_taps, half_taps), (0, 0)))
    stacked = jnp.concatenate(
        [padded[tap_index : tap_index + length] for tap_index in range(tap_count)], 1
    )
    after_conv = (
        inputs
        + jnp.dot(
            stacked,
            conv_full.reshape(tap_count * model_width, model_width),
            preferred_element_type=jnp.float32,
        )
        + bias_rows[1]
    )
    standard_one, inverse_one = normalize(after_conv)
    normed_one = (standard_one * gain_rows[1] + bias_rows[2]).astype(jnp.bfloat16)
    query_raw = jnp.dot(normed_one, query_full, preferred_element_type=jnp.float32)
    key_scale = KEY ** (-0.5)
    content_query = (
        (query_raw * key_scale + rel_offset[0]).astype(jnp.bfloat16).reshape(length, HEADS, -1)
    )
    position_query = (
        (query_raw * key_scale + rel_offset[1]).astype(jnp.bfloat16).reshape(length, HEADS, -1)
    )
    key_heads = (
        jnp.dot(normed_one, key_full, preferred_element_type=jnp.float32)
        .astype(jnp.bfloat16)
        .reshape(length, HEADS, -1)
    )
    value_heads = (
        jnp.dot(normed_one, value_full, preferred_element_type=jnp.float32)
        .astype(jnp.bfloat16)
        .reshape(length, HEADS, -1)
    )
    table = position_table(length, rel_full.shape[0]).astype(jnp.bfloat16)
    position_keys = (
        jnp.dot(table, rel_full, preferred_element_type=jnp.float32)
        .astype(jnp.bfloat16)
        .reshape(table.shape[0], HEADS, -1)
    )
    scores = attention_scores(content_query, key_heads, position_query, position_keys)
    row_peak = jnp.max(scores, -1, keepdims=True)
    normalizer = row_peak + jnp.log(jnp.sum(jnp.exp(scores - row_peak), -1, keepdims=True))
    attention_probs = jnp.exp(scores - normalizer)
    attended = jnp.einsum(
        "hij,jhv->ihv",
        attention_probs.astype(jnp.bfloat16),
        value_heads,
        preferred_element_type=jnp.float32,
    )
    attended = attended.reshape(length, model_width).astype(jnp.bfloat16)
    after_attention = (
        after_conv + jnp.dot(attended, out_full, preferred_element_type=jnp.float32) + bias_rows[3]
    )
    standard_two, inverse_two = normalize(after_attention)
    normed_two = (standard_two * gain_rows[2] + bias_rows[4]).astype(jnp.bfloat16)
    hidden_pre = jnp.dot(normed_two, up_full, preferred_element_type=jnp.float32) + up_offset
    hidden = jax.nn.gelu(hidden_pre).astype(jnp.bfloat16)
    outputs = (
        after_attention
        + jnp.dot(hidden, down_full, preferred_element_type=jnp.float32)
        + bias_rows[5]
    )
    target_row = lax.dynamic_index_in_dim(target_table, window_ids[0], 0, keepdims=False)
    levels = jnp.arange(clip_levels.shape[0], dtype=jnp.int32)
    selector = (clip_index[0][:, None] == levels[None, :]).astype(jnp.float32)
    limits = jnp.sum(selector * clip_levels[None, :], 1)[:, None]
    cotangent = jnp.clip(outputs - target_row, -limits, limits).astype(jnp.bfloat16)
    cot_value = cotangent.astype(jnp.float32)
    conv_back, query_back, key_back, value_back, out_back, up_back, down_back = (
        lax.all_gather(conv_weight, "fsdp", axis=1, tiled=True),
        lax.all_gather(query_weight, "fsdp", axis=0, tiled=True),
        lax.all_gather(key_weight, "fsdp", axis=0, tiled=True),
        lax.all_gather(value_weight, "fsdp", axis=0, tiled=True),
        lax.all_gather(out_weight, "fsdp", axis=0, tiled=True),
        lax.all_gather(up_weight, "fsdp", axis=0, tiled=True),
        lax.all_gather(down_weight, "fsdp", axis=0, tiled=True),
    )
    hidden_grad = dot_trailing(cotangent, down_back)
    grad_down_bias = jnp.sum(cot_value, 0)
    gelu_pull = jax.vjp(jax.nn.gelu, hidden_pre)[1]
    pre_grad = gelu_pull(hidden_grad)[0].astype(jnp.bfloat16)
    grad_up_bias = jnp.sum(pre_grad.astype(jnp.float32), 0)
    normed_two_grad = dot_trailing(pre_grad, up_back)
    grad_gain_two = jnp.sum(normed_two_grad * standard_two, 0)
    grad_bias_two = jnp.sum(normed_two_grad, 0)
    attention_grad = cot_value + norm_back(
        normed_two_grad * gain_rows[2], standard_two, inverse_two
    )
    branch_grad = attention_grad.astype(jnp.bfloat16)
    grad_out_bias = jnp.sum(branch_grad.astype(jnp.float32), 0)
    attended_grad = (
        dot_trailing(branch_grad, out_back).astype(jnp.bfloat16).reshape(length, HEADS, -1)
    )
    scores = attention_scores(content_query, key_heads, position_query, position_keys)
    attention_probs = jnp.exp(scores - normalizer)
    value_grad = jnp.einsum(
        "hij,ihv->jhv",
        attention_probs.astype(jnp.bfloat16),
        attended_grad,
        preferred_element_type=jnp.float32,
    )
    value_grad = value_grad.reshape(length, model_width).astype(jnp.bfloat16)
    prob_grad = jnp.einsum(
        "ihv,jhv->hij", attended_grad, value_heads, preferred_element_type=jnp.float32
    )
    row_dot = jnp.sum(attention_probs * prob_grad, -1, keepdims=True)
    score_grad = (attention_probs * (prob_grad - row_dot)).astype(jnp.bfloat16)
    content_grad = jnp.einsum(
        "hij,jhk->ihk", score_grad, key_heads, preferred_element_type=jnp.float32
    )
    key_grad = jnp.einsum(
        "hij,ihk->jhk", score_grad, content_query, preferred_element_type=jnp.float32
    )
    key_grad = key_grad.reshape(length, -1).astype(jnp.bfloat16)
    band_zeros = jnp.zeros((HEADS, length, position_keys.shape[0]), jnp.float32)
    shift_pull = jax.vjp(relative_shift, band_zeros)[1]
    band_grad = shift_pull(score_grad.astype(jnp.float32))[0].astype(jnp.bfloat16)
    position_grad = jnp.einsum(
        "him,mhk->ihk", band_grad, position_keys, preferred_element_type=jnp.float32
    )
    table_grad = jnp.einsum(
        "him,ihk->mhk", band_grad, position_query, preferred_element_type=jnp.float32
    )
    table_grad = table_grad.reshape(table.shape[0], -1).astype(jnp.bfloat16)
    grad_rel_bias = jnp.stack(
        [jnp.sum(content_grad, 0).reshape(-1), jnp.sum(position_grad, 0).reshape(-1)]
    )
    query_grad = (
        ((content_grad + position_grad) * key_scale).reshape(length, -1).astype(jnp.bfloat16)
    )
    normed_one_grad = (
        dot_trailing(query_grad, query_back)
        + dot_trailing(key_grad, key_back)
        + dot_trailing(value_grad, value_back)
    )
    grad_gain_one = jnp.sum(normed_one_grad * standard_one, 0)
    grad_bias_one = jnp.sum(normed_one_grad, 0)
    conv_side_grad = attention_grad + norm_back(
        normed_one_grad * gain_rows[1], standard_one, inverse_one
    )
    conv_grad = conv_side_grad.astype(jnp.bfloat16)
    grad_conv_bias = jnp.sum(conv_grad.astype(jnp.float32), 0)
    stacked_grad = dot_trailing(conv_grad, conv_back.reshape(tap_count * model_width, model_width))
    stacked_grad = stacked_grad.reshape(length, tap_count, model_width)
    padded_grad = jnp.zeros((length + 2 * half_taps, model_width), jnp.float32)
    for tap_index in range(tap_count):
        padded_grad = padded_grad.at[tap_index : tap_index + length].add(stacked_grad[:, tap_index])
    activated_grad = padded_grad[half_taps : half_taps + length]
    act_pull = jax.vjp(jax.nn.gelu, normed)[1]
    normed_grad = act_pull(activated_grad)[0]
    totals = lax.psum((jnp.sum(normed_grad * standard, 0), jnp.sum(normed_grad, 0)), ("dp", "fsdp"))
    grad_bn_gain = totals[0]
    grad_bn_bias = totals[1]
    input_grad = conv_side_grad + inverse * (
        normed_grad * gain_rows[0]
        - gain_rows[0] * (grad_bn_bias + standard * grad_bn_gain) / token_total
    )
    ln_gains = jnp.stack([grad_gain_one, grad_gain_two])
    bias_five = jnp.stack(
        [grad_conv_bias, grad_bias_one, grad_out_bias, grad_bias_two, grad_down_bias]
    )
    grad_down = dot_leading(hidden, cotangent)
    grad_up = dot_leading(normed_two, pre_grad)
    grad_out = dot_leading(attended, branch_grad)
    grad_query = dot_leading(normed_one, query_grad)
    grad_key = dot_leading(normed_one, key_grad)
    grad_value = dot_leading(normed_one, value_grad)
    grad_rel = dot_leading(table, table_grad)
    grad_conv = dot_leading(stacked, conv_grad).reshape(tap_count, model_width, model_width)
    parts = (
        lax.psum_scatter(
            grad_conv.astype(jnp.bfloat16), "fsdp", scatter_dimension=1, tiled=True
        ).astype(jnp.float32),
        lax.psum_scatter(
            grad_query.astype(jnp.bfloat16), "fsdp", scatter_dimension=0, tiled=True
        ).astype(jnp.float32),
        lax.psum_scatter(
            grad_key.astype(jnp.bfloat16), "fsdp", scatter_dimension=0, tiled=True
        ).astype(jnp.float32),
        lax.psum_scatter(
            grad_value.astype(jnp.bfloat16), "fsdp", scatter_dimension=0, tiled=True
        ).astype(jnp.float32),
        lax.psum_scatter(
            grad_out.astype(jnp.bfloat16), "fsdp", scatter_dimension=0, tiled=True
        ).astype(jnp.float32),
        lax.psum_scatter(
            grad_rel.astype(jnp.bfloat16), "fsdp", scatter_dimension=1, tiled=True
        ).astype(jnp.float32),
        lax.psum_scatter(
            grad_up.astype(jnp.bfloat16), "fsdp", scatter_dimension=0, tiled=True
        ).astype(jnp.float32),
        lax.psum_scatter(
            grad_down.astype(jnp.bfloat16), "fsdp", scatter_dimension=0, tiled=True
        ).astype(jnp.float32),
        lax.psum_scatter(
            ln_gains.astype(jnp.bfloat16), "fsdp", scatter_dimension=1, tiled=True
        ).astype(jnp.float32),
        lax.psum_scatter(
            bias_five.astype(jnp.bfloat16), "fsdp", scatter_dimension=1, tiled=True
        ).astype(jnp.float32),
        lax.psum_scatter(
            grad_up_bias.astype(jnp.bfloat16), "fsdp", scatter_dimension=0, tiled=True
        ).astype(jnp.float32),
        lax.psum_scatter(
            grad_rel_bias.astype(jnp.bfloat16), "fsdp", scatter_dimension=1, tiled=True
        ).astype(jnp.float32),
    )
    reduced = (
        lax.psum(parts[0].astype(jnp.bfloat16), "dp").astype(jnp.float32),
        lax.psum(parts[1].astype(jnp.bfloat16), "dp").astype(jnp.float32),
        lax.psum(parts[2].astype(jnp.bfloat16), "dp").astype(jnp.float32),
        lax.psum(parts[3].astype(jnp.bfloat16), "dp").astype(jnp.float32),
        lax.psum(parts[4].astype(jnp.bfloat16), "dp").astype(jnp.float32),
        lax.psum(parts[5].astype(jnp.bfloat16), "dp").astype(jnp.float32),
        lax.psum(parts[6].astype(jnp.bfloat16), "dp").astype(jnp.float32),
        lax.psum(parts[7].astype(jnp.bfloat16), "dp").astype(jnp.float32),
        lax.psum(parts[8].astype(jnp.bfloat16), "dp").astype(jnp.float32),
        lax.psum(parts[9].astype(jnp.bfloat16), "dp").astype(jnp.float32),
        lax.psum(parts[10].astype(jnp.bfloat16), "dp").astype(jnp.float32),
        lax.psum(parts[11].astype(jnp.bfloat16), "dp").astype(jnp.float32),
    )
    shard_width = gains.shape[1]
    shard_start = lax.axis_index("fsdp") * shard_width
    bn_gain_shard = lax.dynamic_slice_in_dim(grad_bn_gain, shard_start, shard_width)
    bn_bias_shard = lax.dynamic_slice_in_dim(grad_bn_bias, shard_start, shard_width)
    gains_out = jnp.concatenate([bn_gain_shard[None], reduced[8]], 0)
    biases_out = jnp.concatenate([bn_bias_shard[None], reduced[9]], 0)
    return (
        outputs.astype(jnp.bfloat16)[None],
        input_grad.astype(jnp.bfloat16)[None],
        reduced[0],
        reduced[1],
        reduced[2],
        reduced[3],
        reduced[4],
        reduced[5],
        reduced[6],
        reduced[7],
        gains_out,
        biases_out,
        reduced[10],
        reduced[11],
    )


def solution(mesh):
    placed = (
        P(("dp", "fsdp"), None, None),
        P(None, "fsdp", None),
        P("fsdp", None),
        P("fsdp", None),
        P("fsdp", None),
        P("fsdp", None),
        P(None, "fsdp"),
        P("fsdp", None),
        P("fsdp", None),
        P(None, "fsdp"),
        P(None, "fsdp"),
        P("fsdp"),
        P(None, "fsdp"),
        P(),
        P(),
        P(("dp", "fsdp")),
        P(("dp", "fsdp"), None),
    )
    return jax.shard_map(
        on_device,
        mesh=mesh,
        in_specs=placed,
        out_specs=(
            P(("dp", "fsdp"), None, None),
            P(("dp", "fsdp"), None, None),
            P(None, "fsdp", None),
            P("fsdp", None),
            P("fsdp", None),
            P("fsdp", None),
            P("fsdp", None),
            P(None, "fsdp"),
            P("fsdp", None),
            P("fsdp", None),
            P(None, "fsdp"),
            P(None, "fsdp"),
            P("fsdp"),
            P(None, "fsdp"),
        ),
        check_vma=False,
    )
```

profile of v0, /device:TPU:0, one launch (start us, length us, event | category | flops | bytes accessed | tf_op | source)
XLA Modules:
  0.0 2400.9 jit_solution(6179457475343786586)
XLA Ops:
  14.7 14.7 all_gather.43
  29.5 10.9 all_gather.48
  41.0 31.1 %all_gather.50 = bf16[192,512]{1,0:T(8,128)(2,1)S(1)} all-gather(bf16[192,128]{1,0:T(8,128)(2,1)S(1)} %copy-done.55), channel_id=1, replica_groups=mesh['dp'=8,'fsdp'=4] {'fsdp'}, dimensions={1}, use_global_device_ids=true | all-gather | bytes 245760 | tf_op jit(solution)/shard_map/all_gather | solution.py:107
  72.3 69.4 %all-reduce.7 = (f32[1536]{0:T(1024)S(1)}, f32[1536]{0:T(1024)S(1)}) all-reduce(f32[1536]{0:T(1024)S(1)} %fusion.40, f32[1536]{0:T(1024)S(1)} %convert_reduce_fusion), channel_id=1, replica_groups=mesh['dp'=8,'fsdp'=4] {'dp','fsdp'}, use_global_device_ids=true, to_apply=%region_3.0 | all-reduce | flops 3072 | bytes 24576 | tf_op jit(solution)/shard_map/psum | solution.py:141
  144.3 20.1 all_gather.44
  164.5 29.8 %all-gather = bf16[4,1,768]{2,1,0:T(2,128)(2,1)S(1)} all-gather(bf16[1,1,768]{2,1,0:T(2,128)(2,1)S(1)} %reshape.370), channel_id=1, replica_groups=mesh['dp'=8,'fsdp'=4] {'fsdp'}, dimensions={0}, use_global_device_ids=true | all-gather | bytes 7680 | tf_op jit(solution)/shard_map/all_gather | solution.py:114
  206.1 210.0 %all-gather.9.cloned.1.call-done = bf16[5,1536,1536]{2,1,0:T(8,128)(2,1)} async-done(((bf16[5,384,1536]{2,1,0:T(8,128)(2,1)}), bf16[5,1536,1536]{2,1,0:T(8,128)(2,1)}) %all-gather.9.cloned.1.call-update) | async-done | bytes 23592976 | tf_op jit(solution)/shard_map/all_gather | solution.py:102
  416.1 18.8 fusion.87
  437.1 68.2 %all-gather.11.cloned.1.call-done = bf16[1536,1536]{1,0:T(8,128)(2,1)} async-done(((bf16[384,1536]{1,0:T(8,128)(2,1)}), bf16[1536,1536]{1,0:T(8,128)(2,1)}) %all-gather.11.cloned.1.call-update) | async-done | bytes 4718608 | tf_op jit(solution)/shard_map/all_gather | solution.py:105
  505.3 6.6 convolution_convert_fusion.8
  514.5 27.9 %all-gather.13.cloned.1.call-done = bf16[1536,512]{1,0:T(8,128)(2,1)} async-done(((bf16[384,512]{1,0:T(8,128)(2,1)}), bf16[1536,512]{1,0:T(8,128)(2,1)}) %all-gather.13.cloned.1.call-update) | async-done | bytes 1572880 | tf_op jit(solution)/shard_map/all_gather | solution.py:103
  542.5 3.8 add_convert_fusion.3
  548.7 7.6 pad.34
  556.3 18.1 reshape.361
  574.4 12.1 slice.204
  586.5 19.8 reshape.362
  606.3 7.8 slice.205
  614.2 9.2 copy.75
  626.3 5.0 fusion.88
  637.5 32.1 %all-gather.17.cloned.1.call-done = bf16[1536,1536]{1,0:T(8,128)(2,1)} async-done(((bf16[384,1536]{1,0:T(8,128)(2,1)}), bf16[1536,1536]{1,0:T(8,128)(2,1)}) %all-gather.17.cloned.1.call-update) | async-done | bytes 4718608 | tf_op jit(solution)/shard_map/all_gather | solution.py:106
  669.6 5.3 fusion.89
  677.0 159.3 %all-gather.19.cloned.1.call-done = bf16[1536,3072]{1,0:T(8,128)(2,1)} async-done(((bf16[384,3072]{1,0:T(8,128)(2,1)}), bf16[1536,3072]{1,0:T(8,128)(2,1)}) %all-gather.19.cloned.1.call-update) | async-done | bytes 9437200 | tf_op jit(solution)/shard_map/all_gather | solution.py:108
  836.3 11.6 fusion.79
  847.9 154.9 %all-gather.21.cloned.1.call-done = bf16[3072,1536]{1,0:T(8,128)(2,1)} async-done(((bf16[768,1536]{1,0:T(8,128)(2,1)}), bf16[3072,1536]{1,0:T(8,128)(2,1)}) %all-gather.21.cloned.1.call-update) | async-done | bytes 9437200 | tf_op jit(solution)/shard_map/all_gather | solution.py:109
  1002.9 13.3 fusion.83
  1016.2 13.5 fusion.81
  1029.6 9.4 multiply_reduce_fusion.1
  1042.2 4.0 convolution_convert_fusion.7
  1048.7 6.5 multiply_reduce_fusion
  1055.5 3.8 multiply_convert_fusion
  1059.4 6.4 copy.76
  1065.8 6.6 pad.35.clone
  1072.4 21.9 reshape.364
  1094.2 8.8 pad.36
  1103.0 13.3 reshape.365
  1116.3 6.8 fusion.54
  1127.2 3.8 convolution_convert_fusion.12
  1134.1 5.5 convolution_convert_fusion.9
  1140.8 4.3 convolution_convert_fusion.4
  1145.2 7.2 convolution_convert_fusion.3
  1152.5 10.0 convolution_convert_fusion.2
  1163.9 12.4 convolution_convert_fusion.1
  1179.3 5.0 fusion.92
  1188.1 20.6 convolution_convert_fusion
  1210.9 7.3 fusion.51
  1223.8 60.5 %reduce-scatter.26.cloned.1.call-done = bf16[384,1536]{1,0:T(8,128)(2,1)} async-done(((bf16[1536,1536]{1,0:T(8,128)(2,1)}), bf16[384,1536]{1,0:T(8,128)(2,1)}) %reduce-scatter.26.cloned.1.call-update) | async-done | bytes 1179664 | tf_op jit(solution)/shard_map/reduce_scatter | solution.py:327
  1284.3 88.7 %reduce-scatter.28.cloned.1.call-done = bf16[384,1536]{1,0:T(8,128)(2,1)} async-done(((bf16[1536,1536]{1,0:T(8,128)(2,1)}), bf16[384,1536]{1,0:T(8,128)(2,1)}) %reduce-scatter.28.cloned.1.call-update) | async-done | bytes 1179664 | tf_op jit(solution)/shard_map/reduce_scatter | solution.py:330
  1373.0 164.6 %reduce-scatter.30.cloned.1.call-done = bf16[384,3072]{1,0:T(8,128)(2,1)} async-done(((bf16[1536,3072]{1,0:T(8,128)(2,1)}), bf16[384,3072]{1,0:T(8,128)(2,1)}) %reduce-scatter.30.cloned.1.call-update) | async-done | bytes 2359312 | tf_op jit(solution)/shard_map/reduce_scatter | solution.py:336
  1537.6 164.5 %reduce-scatter.32.cloned.1.call-done = bf16[768,1536]{1,0:T(8,128)(2,1)} async-done(((bf16[3072,1536]{1,0:T(8,128)(2,1)}), bf16[768,1536]{1,0:T(8,128)(2,1)}) %reduce-scatter.32.cloned.1.call-update) | async-done | bytes 2359312 | tf_op jit(solution)/shard_map/reduce_scatter | solution.py:339
  1702.1 392.1 %reduce-scatter.20.cloned.1.call-done = bf16[5,384,1536]{2,1,0:T(8,128)(2,1)} async-done(((bf16[5,1536,1536]{2,1,0:T(8,128)(2,1)}), bf16[5,384,1536]{2,1,0:T(8,128)(2,1)}) %reduce-scatter.20.cloned.1.call-update) | async-done | bytes 5898256 | tf_op jit(solution)/shard_map/reduce_scatter | solution.py:318
  2094.3 19.3 fusion.48
  2120.1 7.7 scatter-add.19
  2131.4 7.7 scatter-add.20
  2139.1 3.5 fusion.45
  2142.6 7.7 scatter-add.21
  2150.3 5.2 fusion.44
  2155.6 8.5 scatter-add.24
  2164.1 5.7 fusion.80
  2169.8 42.9 %all-reduce.6 = (f32[1536]{0:T(1024)S(1)}, f32[1536]{0:T(1024)S(1)}) all-reduce(f32[1536]{0:T(1024)S(1)} %get-tuple-element.83, f32[1536]{0:T(1024)S(1)} %get-tuple-element.82), channel_id=1, replica_groups=mesh['dp'=8,'fsdp'=4] {'dp','fsdp'}, use_global_device_ids=true, to_apply=%region_20.21 | all-reduce | flops 3072 | bytes 24576 | tf_op jit(solution)/shard_map/psum | solution.py:298
  2212.9 10.8 all-reduce.5
  2223.8 5.3 fusion.50
  2232.9 24.4 %all-reduce.8 = (bf16[192,128]{1,0:T(8,128)(2,1)S(1)}, bf16[2,384]{1,0:T(2,128)(2,1)S(1)}, bf16[5,384]{1,0:T(8,128)(2,1)S(1)}, bf16[768]{0:T(1024)(128)(2,1)S(1)}, bf16[2,128]{1,0:T(2,128)(2,1)S(1)}) all-reduce(bf16[192,128]{1,0:T(8,128)(2,1)S(1)} %copy.68, bf16[2,384]{1,0:T(2,128)(2,1)S(1)} %copy.70, ...), channel_id=1, replica_groups=mesh['dp'=8,'fsdp'=4] {'dp'}, use_global_device_ids=true, to_apply=%region_32.33 | all-reduce | flops 28288 | bytes 113152 | tf_op jit(solution)/shard_map/psum | solution.py:361
  2260.4 113.6 %all-reduce.12.cloned.1.call-done = (bf16[5,384,1536]{2,1,0:T(8,128)(2,1)}, bf16[384,512]{1,0:T(8,128)(2,1)}, bf16[384,512]{1,0:T(8,128)(2,1)}, bf16[384,1536]{1...) async-done(((bf16[5,384,1536]{2,1,0:T(8,128)(2,1)}, bf16[384,512]{1,0:T(8,128)(2,1)}, bf16[384,512]{1,0:T(8,128)(2,1)}, ...) | async-done | bytes 13762576 | tf_op jit(solution)/shard_map/psum | solution.py:356
  2374.0 8.9 convert_element_type.287
  (312 shorter events, 97.8 us)
Async XLA Ops:
  7.2 187.7 %copy-start = (f32[64,1536]{1,0:T(8,128)S(1)}, f32[64,1536]{1,0:T(8,128)}, u32[]{:S(2)}) copy-start(f32[64,1536]{1,0:T(8,128)} %param.40) | copy-start | bytes 1179652
  7.2 408.9 %all-gather.9.cloned.1.call-start = ((), (), s32[]{:S(2)}) async-start(), calls=%async_computation.11 | async-start | bytes 29491200 | tf_op jit(solution)/shard_map/all_gather | solution.py:102
  7.9 497.4 %all-gather.11.cloned.1.call-start = ((), (), s32[]{:S(2)}) async-start(), calls=%async_computation.12 | async-start | bytes 5898240 | tf_op jit(solution)/shard_map/all_gather | solution.py:105
  8.7 533.8 %all-gather.13.cloned.1.call-start = ((), (), s32[]{:S(2)}) async-start(), calls=%async_computation.13 | async-start | bytes 1966080 | tf_op jit(solution)/shard_map/all_gather | solution.py:103
  9.4 613.9 %all-gather.15.cloned.1.call-start = ((), (), s32[]{:S(2)}) async-start(), calls=%async_computation.14 | async-start | bytes 1966080 | tf_op jit(solution)/shard_map/all_gather | solution.py:104
  10.0 659.6 %all-gather.17.cloned.1.call-start = ((), (), s32[]{:S(2)}) async-start(), calls=%async_computation.15 | async-start | bytes 5898240 | tf_op jit(solution)/shard_map/all_gather | solution.py:106
  10.6 825.7 %all-gather.19.cloned.1.call-start = ((), (), s32[]{:S(2)}) async-start(), calls=%async_computation.16 | async-start | bytes 11796480 | tf_op jit(solution)/shard_map/all_gather | solution.py:108
  11.2 18.2 copy-start.72
  11.2 29.8 %copy-start.55 = (bf16[192,128]{1,0:T(8,128)(2,1)S(1)}, bf16[192,128]{1,0:T(8,128)(2,1)}, u32[]{:S(2)}) copy-start(bf16[192,128]{1,0:T(8,128)(2,1)} %param.33) | copy-start | bytes 147460
  11.2 991.6 %all-gather.21.cloned.1.call-start = ((), (), s32[]{:S(2)}) async-start(), calls=%async_computation.17 | async-start | bytes 11796480 | tf_op jit(solution)/shard_map/all_gather | solution.py:109
  12.0 1211.8 %reduce-scatter.22.cloned.1.call-start = ((), (), s32[]{:S(2)}) async-start(), calls=%async_computation.19 | async-start | bytes 1966080 | tf_op jit(solution)/shard_map/reduce_scatter | solution.py:321
  12.4 152.1 %copy-start.65 = (f32[768]{0:T(1024)S(1)}, f32[768]{0:T(1024)}, u32[]{:S(2)}) copy-start(f32[768]{0:T(1024)} %param.38) | copy-start | bytes 9220
  29.5 170.9 %copy-start.38 = (f32[1536]{0:T(1024)}, f32[1536]{0:T(1024)S(1)}, u32[]{:S(2)}) copy-start(f32[1536]{0:T(1024)S(1)} %get-tuple-element.92) | copy-start | bytes 18436
  29.5 405.9 %copy-start.46 = (f32[1536]{0:T(1024)}, f32[1536]{0:T(1024)S(1)}, u32[]{:S(2)}) copy-start(f32[1536]{0:T(1024)S(1)} %get-tuple-element.91) | copy-start | bytes 18436
  72.1 125.0 %copy-start.50 = (bf16[1023,32]{0,1:T(8,128)(2,1)}, bf16[1023,32]{0,1:T(8,128)(2,1)S(1)}, u32[]{:S(2)}) copy-start(bf16[1023,32]{0,1:T(8,128)(2,1)S(1)} %get-tuple-element.129) | copy-start | bytes 196420
  72.3 124.8 %copy-start.51 = (bf16[1023,32]{0,1:T(8,128)(2,1)}, bf16[1023,32]{0,1:T(8,128)(2,1)S(1)}, u32[]{:S(2)}) copy-start(bf16[1023,32]{0,1:T(8,128)(2,1)S(1)} %get-tuple-element.127) | copy-start | bytes 196420
  141.7 58.6 %copy-start.40 = (f32[1536]{0:T(1024)}, f32[1536]{0:T(1024)S(1)}, u32[]{:S(2)}) copy-start(f32[1536]{0:T(1024)S(1)} %get-tuple-element.125) | copy-start | bytes 18436
  141.7 58.6 %copy-start.42 = (f32[1536]{0:T(1024)}, f32[1536]{0:T(1024)S(1)}, u32[]{:S(2)}) copy-start(f32[1536]{0:T(1024)S(1)} %get-tuple-element.126) | copy-start | bytes 18436
  142.1 55.0 %copy-start.52 = (bf16[1023,32]{0,1:T(8,128)(2,1)}, bf16[1023,32]{0,1:T(8,128)(2,1)S(1)}, u32[]{:S(2)}) copy-start(bf16[1023,32]{0,1:T(8,128)(2,1)S(1)} %get-tuple-element.123) | copy-start | bytes 196420
  434.9 234.7 %copy-start.3 = (f32[512,1536]{1,0:T(8,128)}, f32[512,1536]{1,0:T(8,128)S(1)}, u32[]{:S(2)}) copy-start(f32[512,1536]{1,0:T(8,128)S(1)} %get-tuple-element.136) | copy-start | bytes 9437188
  435.4 76.5 %copy-start.56 = (f32[512]{0:T(512)}, f32[512]{0:T(512)S(1)}, u32[]{:S(2)}) copy-start(f32[512]{0:T(512)S(1)} %add_rsqrt_fusion.2) | copy-start | bytes 6148
  511.9 30.6 %copy-start.68 = (f32[1,512]{1,0:T(1,128)S(1)}, f32[1,512]{1,0:T(1,128)}, u32[]{:S(2)}) copy-start(f32[1,512]{1,0:T(1,128)} %get-tuple-element.131) | copy-start | bytes 6148
  511.9 30.6 %copy-start.69 = (f32[1,512]{1,0:T(1,128)S(1)}, f32[1,512]{1,0:T(1,128)}, u32[]{:S(2)}) copy-start(f32[1,512]{1,0:T(1,128)} %get-tuple-element.132) | copy-start | bytes 6148
  836.3 166.6 %copy-start.9 = (f32[512,1536]{1,0:T(8,128)S(1)}, f32[512,1536]{1,0:T(8,128)}, u32[]{:S(2)}) copy-start(f32[512,1536]{1,0:T(8,128)} %copy-done.8) | copy-start | bytes 9437188
  836.3 166.6 %copy-start.59 = (f32[4,1,768]{2,1,0:T(1,128)S(1)}, f32[4,1,768]{2,1,0:T(1,128)}, u32[]{:S(2)}) copy-start(f32[4,1,768]{2,1,0:T(1,128)} %convert_element_type.311) | copy-start | bytes 36868
  836.3 166.6 %copy-start.60 = (f32[1536]{0:T(1024)S(1)}, f32[1536]{0:T(1024)}, u32[]{:S(2)}) copy-start(f32[1536]{0:T(1024)} %dynamic-slice_reduce_fusion) | copy-start | bytes 18436
  836.3 166.6 %copy-start.62 = (f32[512]{0:T(512)S(1)}, f32[512]{0:T(512)}, u32[]{:S(2)}) copy-start(f32[512]{0:T(512)} %copy-done.61) | copy-start | bytes 6148
  836.3 166.6 %copy-start.70 = (bf16[512]{0:T(512)(128)(2,1)S(1)}, bf16[512]{0:T(512)(128)(2,1)}, u32[]{:S(2)}) copy-start(bf16[512]{0:T(512)(128)(2,1)} %neg.8) | copy-start | bytes 3076
  1002.9 13.3 copy-start.74
  1002.9 39.3 %slice-start.2 = ((s8[4718592]{0:T(1024)(128)(4,1)}), s8[4194304]{0:T(1024)(128)(4,1)S(1)}, s32[]{:S(2)}) async-start(s8[4718592]{0:T(1024)(128)(4,1)} %bitcast.202), calls=%async_computation.32 | async-start | bytes 8388608
  1016.2 22.9 copy-start.26
  1016.2 26.0 %slice-start.3 = ((s8[4718592]{0:T(1024)(128)(4,1)}), s8[524288]{0:T(1024)(128)(4,1)S(1)}, s32[]{:S(2)}) async-start(s8[4718592]{0:T(1024)(128)(4,1)} %bitcast.202), calls=%async_computation.33 | async-start | bytes 1048576
  1048.7 6.5 slice-start
  1048.7 6.8 slice-start.1
  1116.3 6.8 copy-start.5
  1116.3 6.8 copy-start.23
  1127.1 96.7 %reduce-scatter.24.cloned.1.call-start = ((), (), s32[]{:S(2)}) async-start(), calls=%async_computation.20 | async-start | bytes 1966080 | tf_op jit(solution)/shard_map/reduce_scatter | solution.py:324
  1134.1 150.2 %reduce-scatter.26.cloned.1.call-start = ((), (), s32[]{:S(2)}) async-start(), calls=%async_computation.21 | async-start | bytes 5898240 | tf_op jit(solution)/shard_map/reduce_scatter | solution.py:327
  1134.1 6.7 copy-start.30
  1145.1 227.9 %reduce-scatter.28.cloned.1.call-start = ((), (), s32[]{:S(2)}) async-start(), calls=%async_computation.22 | async-start | bytes 5898240 | tf_op jit(solution)/shard_map/reduce_scatter | solution.py:330
  1152.4 385.2 %reduce-scatter.30.cloned.1.call-start = ((), (), s32[]{:S(2)}) async-start(), calls=%async_computation.23 | async-start | bytes 11796480 | tf_op jit(solution)/shard_map/reduce_scatter | solution.py:336
  1162.5 539.6 %reduce-scatter.32.cloned.1.call-start = ((), (), s32[]{:S(2)}) async-start(), calls=%async_computation.24 | async-start | bytes 11796480 | tf_op jit(solution)/shard_map/reduce_scatter | solution.py:339
  1176.3 917.9 %reduce-scatter.20.cloned.1.call-start = ((), (), s32[]{:S(2)}) async-start(), calls=%async_computation.18 | async-start | bytes 29491200 | tf_op jit(solution)/shard_map/reduce_scatter | solution.py:318
  1179.3 5.1 copy-start.21
  1179.3 5.1 copy-start.31
  1179.3 5.1 copy-start.47
  1179.3 5.1 copy-start.54
  1179.3 5.1 copy-start.57
  1188.1 906.2 %copy-start.11 = (f32[512,1536]{1,0:T(8,128)}, f32[512,1536]{1,0:T(8,128)S(1)}, u32[]{:S(2)}) copy-start(f32[512,1536]{1,0:T(8,128)S(1)} %get-tuple-element.116) | copy-start | bytes 9437188
  1208.7 1020.4 %reduce-scatter.40.cloned.1.call-start = ((), (), s32[]{:S(2)}) async-start(), calls=%async_computation.28 | async-start | bytes 163840
  1209.8 1020.1 %reduce-scatter.36.cloned.1.call-start = ((), (), s32[]{:S(2)}) async-start(), calls=%async_computation.26 | async-start | bytes 491520
  1210.8 7.5 copy-start.66
  1210.9 8.8 copy-start.45
  1210.9 1020.1 %reduce-scatter.38.cloned.1.call-start = ((), (), s32[]{:S(2)}) async-start(), calls=%async_computation.27 | async-start | bytes 491520
  1219.4 1012.5 %reduce-scatter.34.cloned.1.call-start = ((), (), s32[]{:S(2)}) async-start(), calls=%async_computation.25 | async-start | bytes 327680
  1222.4 1151.6 %all-reduce.12.cloned.1.call-start = ((), (), s32[]{:S(2)}) async-start(), calls=%async_computation.29 | async-start | bytes 27525120 | tf_op jit(solution)/shard_map/psum | solution.py:356
  2155.5 8.5 copy-start.7
  2155.5 8.5 copy-start.39
  2155.5 8.5 copy-start.41
  2155.5 8.5 copy-start.43
  2155.5 8.5 copy-start.49
  2164.1 48.8 %copy-start.64 = (bf16[3072]{0:T(1024)(128)(2,1)S(1)}, bf16[3072]{0:T(1024)(128)(2,1)}, u32[]{:S(2)}) copy-start(bf16[3072]{0:T(1024)(128)(2,1)} %get-tuple-element.109) | copy-start | bytes 18436
  2374.0 8.9 copy-start.37
  2374.0 9.9 copy-start.36
  (34 other events, 87.3 us)
Sparse Core Ops, SparseCore 0:
  9.6 406.4 all-gather.8
  417.7 87.5 all-gather.10
  506.9 35.5 all-gather.12
  543.9 35.9 all-gather.14
  581.3 88.2 all-gather.16
  671.0 165.2 all-gather.18
  837.8 164.9 all-gather.20
  1127.2 33.4 reduce-scatter.21
  1163.1 34.2 reduce-scatter.23
  1200.1 84.1 reduce-scatter.25
  1287.2 85.7 reduce-scatter.27
  1375.8 161.8 reduce-scatter.29
  1540.0 162.1 reduce-scatter.31
  1704.4 389.8 reduce-scatter.19
  2096.9 21.0 reduce-scatter.39
  2120.8 18.7 reduce-scatter.35
  2142.3 18.8 reduce-scatter.37
  2164.0 17.8 reduce-scatter.33
  2186.7 187.2 all-reduce.11
where the time goes:
time: 2410 us; the launch traced here: 2400 us
  waiting for transfers between devices  1640 us (68%)
  blocking collectives  254 us (11%)
  matrix products  220 us (9%)
  local copies, waits for them, and re-layouts  202 us (8%)
  other arithmetic  65.9 us (3%)
    reduce_scatter x1, waiting for transfers between devices, on_device(): lax.psum_scatter(grad_conv.astype(jnp.bfloat16), 'fsdp', scatter_dimensio...  392 us
    all_gather x1, waiting for transfers between devices, on_device(): lax.all_gather(conv_weight, 'fsdp', axis=1, tiled=True)  210 us
    reduce_scatter x1, waiting for transfers between devices, on_device(): lax.psum_scatter(grad_up.astype(jnp.bfloat16), 'fsdp', scatter_dimension=...  165 us
    reduce_scatter x1, waiting for transfers between devices, on_device(): lax.psum_scatter(grad_down.astype(jnp.bfloat16), 'fsdp', scatter_dimensio...  165 us
    all_gather x1, waiting for transfers between devices, on_device(): lax.all_gather(up_weight, 'fsdp', axis=0, tiled=True)  159 us
    all_gather x1, waiting for transfers between devices, on_device(): lax.all_gather(down_weight, 'fsdp', axis=0, tiled=True)  155 us
    psum x1, waiting for transfers between devices, on_device(): lax.psum(parts[0].astype(jnp.bfloat16), 'dp').astype(jnp.float32)  114 us
    reduce_scatter x1, waiting for transfers between devices, on_device(): lax.psum_scatter(grad_out.astype(jnp.bfloat16), 'fsdp', scatter_dimension...  88.7 us
  transfers between devices with their start and end apart: 19, of which 12 were waited for; matrix products, arithmetic and copies ran while one was open for 14% of the time, Pallas kernels for 0%

commit v1 on v0

--- a/solution.py
+++ b/solution.py
@@ -1,12 +1,209 @@
+import functools
 import math
 
 import jax
 import jax.numpy as jnp
 from jax import lax
+from jax.experimental import pallas as pl
+from jax.experimental.pallas import tpu as pltpu
 from jax.sharding import PartitionSpec as P
 
 HEADS = 8
 KEY = 64
+MESH = pl.DeviceIdType.MESH
+PIECES = 12
+AHEAD = 2
+LAG = 1
+
+def neighbours(dp):
+    core = dp % 2
+    along_x = dp // 2 % 2
+    along_y = dp // 4 % 2
+    return dp + 1 - 2 * core, dp + 2 - 4 * along_x, dp + 4 - 8 * along_y
+
+def gather_kernel(groups, conv, query, key, value, out, rel, up, down, small,
+                  full, small_full, hold, local_sem, write_sem, z_sem, x_sem, y_sem, d_sem, sib_sem, send_sem, right_send, left_send, small_send, small_recv):
+    dp = lax.axis_index("dp")
+    me = lax.axis_index("fsdp")
+    sib, along_x, along_y = neighbours(dp)
+    rows = full.shape[2]
+    part = rows // 8
+    others = groups - 1
+
+    locals_ = []
+    def local(src, dst, piece):
+        c = pltpu.make_async_copy(src, dst, local_sem.at[len(locals_)])
+        c.start()
+        locals_.append((piece, c))
+    for tap in range(5):
+        local(conv.at[tap], hold.at[tap], tap)
+    qk = query.shape[1]
+    local(query, hold.at[5, :, pl.ds(0, qk)], 5)
+    local(key, hold.at[5, :, pl.ds(qk, qk)], 5)
+    local(rel, hold.at[5, pl.ds(0, rel.shape[0]), pl.ds(2 * qk, rel.shape[1])], 5)
+    local(value, hold.at[6], 6)
+    local(out, hold.at[7], 7)
+    for half in range(2):
+        for shard in range(groups):
+            local(up.at[:, pl.ds((shard * 2 + half) * rows, rows)], hold.at[8 + half, :, pl.ds(shard * rows, rows)], 8 + half)
+    for half in range(2):
+        local(down.at[pl.ds(half * rows, rows)], hold.at[10 + half], 10 + half)
+    local(small, small_full.at[me], 12)
+
+    peers = [(sib, me), (along_x, me), (along_y, me)] + [(dp, (me + 1 + j) % groups) for j in range(others)]
+    barrier = pltpu.get_barrier_semaphore()
+    for peer in peers:
+        pl.semaphore_signal(barrier, inc=1, device_id=peer, device_id_type=MESH)
+    pl.semaphore_wait(barrier, len(peers))
+
+    def remote(src, dst, ssem, rsem, dev):
+        return pltpu.make_async_remote_copy(src_ref=src, dst_ref=dst, send_sem=ssem, recv_sem=rsem, device_id=dev, device_id_type=MESH)
+
+    smalls = []
+    for j in range(others):
+        c = remote(small, small_full.at[me], small_send.at[j], small_recv.at[me], (dp, (me + 1 + j) % groups))
+        c.start()
+        smalls.append(c)
+
+    def piece_slice(piece, shard, owner):
+        return full.at[piece, shard, pl.ds(pl.multiple_of(owner % 8 * part, 16), part)]
+
+    def copy(piece, shard, owner, rsem, dev):
+        ref = piece_slice(piece, shard, owner)
+        return remote(ref, ref, send_sem, rsem, dev)
+
+    order = []
+    for j in range(others):
+        pick = 0
+        for m in range(groups):
+            near = sorted((t for t in range(groups) if t != m), key=lambda t: abs(t - m))
+            pick = pick + jnp.where(me == m, near[j], 0)
+        order.append(pick)
+
+    def right_copy(piece, shard, src=None):
+        dst = piece_slice(piece, shard, dp)
+        return remote(dst if src is None else src, dst, right_send.at[piece, shard], z_sem.at[piece, shard], (dp, (me + 1) % groups))
+
+    def left_copy(piece, shard, src=None):
+        dst = piece_slice(piece, shard, dp)
+        return remote(dst if src is None else src, dst, left_send.at[piece, shard], z_sem.at[piece, shard], (dp, (me + groups - 1) % groups))
+
+    def z_send(piece):
+        src = hold.at[piece, pl.ds(pl.multiple_of(dp % 8 * part, 16), part)]
+        @pl.when(me + 1 < groups)
+        def _():
+            right_copy(piece, me, src).start()
+        @pl.when(me > 0)
+        def _():
+            left_copy(piece, me, src).start()
+
+    def route(piece, shard):
+        return (piece + shard) % 2
+
+    diag = neighbours(along_x)[2]
+
+    def stage_a(piece):
+        for shard in order:
+            copy(piece, shard, dp, z_sem.at[piece, shard], (dp, me)).wait_recv()
+
+            @pl.when(jnp.logical_and(shard < me, me + 1 < groups))
+            def _():
+                right_copy(piece, shard).start()
+
+            @pl.when(jnp.logical_and(shard > me, me > 0))
+            def _():
+                left_copy(piece, shard).start()
+
+            copy(piece, shard, dp, x_sem.at[piece, shard], (along_x, me)).start()
+            copy(piece, shard, dp, y_sem.at[piece, shard], (along_y, me)).start()
+            copy(piece, shard, dp, sib_sem, (sib, me)).start()
+
+    def stage_b(piece):
+        for shard in order:
+            r = route(piece, shard)
+            copy(piece, shard, along_x, x_sem.at[piece, shard], (dp, me)).wait_recv()
+            copy(piece, shard, along_y, y_sem.at[piece, shard], (dp, me)).wait_recv()
+            owner = r * along_x + (1 - r) * along_y
+            target = r * along_y + (1 - r) * along_x
+            copy(piece, shard, owner, d_sem.at[piece, shard], (target, me)).start()
+            copy(piece, shard, along_x, sib_sem, (sib, me)).start()
+            copy(piece, shard, along_y, sib_sem, (sib, me)).start()
+
+    def stage_c(piece):
+        for shard in order:
+            copy(piece, shard, diag, d_sem.at[piece, shard], (dp, me)).wait_recv()
+            copy(piece, shard, diag, sib_sem, (sib, me)).start()
+
+    def wait_local(piece):
+        for p, c in locals_:
+            if p == piece:
+                c.wait()
+    writes = []
+    for piece in range(PIECES):
+        wait_local(piece)
+        c = pltpu.make_async_copy(hold.at[piece], full.at[piece, me], write_sem.at[piece])
+        c.start()
+        writes.append(c)
+        if piece < AHEAD:
+            z_send(piece)
+
+    def body(n, carry):
+        @pl.when(n + AHEAD < PIECES)
+        def _():
+            z_send(n + AHEAD)
+        @pl.when(n < PIECES)
+        def _():
+            stage_a(n)
+        @pl.when(jnp.logical_and(n >= LAG, n < PIECES + LAG))
+        def _():
+            stage_b(n - LAG)
+        @pl.when(n >= 2 * LAG)
+        def _():
+            stage_c(n - 2 * LAG)
+        return carry
+    lax.fori_loop(0, PIECES + 2 * LAG, body, 0)
+
+    def drain(piece, carry):
+        for shard in range(groups):
+            @pl.when(jnp.logical_and(shard <= me, me + 1 < groups))
+            def _():
+                right_copy(piece, shard).wait_send()
+            @pl.when(jnp.logical_and(shard >= me, me > 0))
+            def _():
+                left_copy(piece, shard).wait_send()
+        return carry
+    lax.fori_loop(0, PIECES, drain, 0)
+    wait_local(12)
+    for c in writes:
+        c.wait()
+    for c in smalls:
+        c.wait_send()
+    for j in range(others):
+        shard = (me + 1 + j) % groups
+        remote(small, small_full.at[shard], small_send.at[j], small_recv.at[shard], (dp, me)).wait_recv()
+    got = full.at[:, pl.ds(0, others), pl.ds(0, 4 * part)]
+    remote(got, got, send_sem, sib_sem, (sib, me)).wait_recv()
+    sent = full.at[:, pl.ds(0, others), pl.ds(0, 7 * part)]
+    remote(sent, sent, send_sem, sib_sem, (sib, me)).wait_send()
+
+
+def gather(groups, *args):
+    conv = args[0]
+    rows, cols = conv.shape[1:]
+    small = args[-1]
+    any_spec = pl.BlockSpec(memory_space=pl.ANY)
+    return pl.pallas_call(
+        functools.partial(gather_kernel, groups),
+        out_shape=(jax.ShapeDtypeStruct((PIECES, groups, rows, cols), conv.dtype),
+                   jax.ShapeDtypeStruct((groups,) + small.shape, small.dtype)),
+        in_specs=[any_spec] * 9,
+        out_specs=(any_spec, any_spec),
+        scratch_shapes=[pltpu.VMEM((PIECES, rows, cols), conv.dtype), pltpu.SemaphoreType.DMA((5 + 5 + 2 * groups + 2 + 1,)), pltpu.SemaphoreType.DMA((PIECES,))] +
+          [pltpu.SemaphoreType.DMA((PIECES, groups))] * 4 +
+          [pltpu.SemaphoreType.DMA(()), pltpu.SemaphoreType.DMA(()), pltpu.SemaphoreType.DMA((PIECES, groups)), pltpu.SemaphoreType.DMA((PIECES, groups)), pltpu.SemaphoreType.DMA((groups,)), pltpu.SemaphoreType.DMA((groups,))],
+        compiler_params=pltpu.CompilerParams(collective_id=0, has_side_effects=True, vmem_limit_bytes=24 << 20),
+        name="gather",
+    )(*args)
 
 
 EPSILON = 1e-05
@@ -98,40 +295,51 @@
     window_ids,
     clip_index,
 ):
-    gathered = (
-        lax.all_gather(conv_weight, "fsdp", axis=1, tiled=True),
-        lax.all_gather(query_weight, "fsdp", axis=0, tiled=True),
-        lax.all_gather(key_weight, "fsdp", axis=0, tiled=True),
-        lax.all_gather(value_weight, "fsdp", axis=0, tiled=True),
-        lax.all_gather(out_weight, "fsdp", axis=0, tiled=True),
-        lax.all_gather(rel_weight, "fsdp", axis=1, tiled=True),
-        lax.all_gather(up_weight, "fsdp", axis=0, tiled=True),
-        lax.all_gather(down_weight, "fsdp", axis=0, tiled=True),
-        lax.all_gather(gains.astype(jnp.bfloat16), "fsdp", axis=1, tiled=True).astype(gains.dtype),
-        lax.all_gather(biases.astype(jnp.bfloat16), "fsdp", axis=1, tiled=True).astype(
-            biases.dtype
-        ),
-        lax.all_gather(up_bias.astype(jnp.bfloat16), "fsdp", axis=0, tiled=True).astype(
-            up_bias.dtype
-        ),
-        lax.all_gather(rel_bias.astype(jnp.bfloat16), "fsdp", axis=1, tiled=True).astype(
-            rel_bias.dtype
-        ),
-    )
-    (
-        conv_full,
-        query_full,
-        key_full,
-        value_full,
-        out_full,
-        rel_full,
-        up_full,
-        down_full,
-        gain_rows,
-        bias_rows,
-        up_offset,
-        rel_offset,
-    ) = gathered
+    groups = lax.axis_size("fsdp")
+    piece_rows = conv_weight.shape[1]
+    small_parts = [gains, biases, up_bias, rel_bias]
+    small = jnp.concatenate([part.reshape(-1) for part in small_parts])
+    small = jnp.pad(small, (0, -small.shape[0] % 1024)).reshape(-1, 128)
+    full, small_full = gather(
+        groups,
+        conv_weight,
+        query_weight,
+        key_weight,
+        value_weight,
+        out_weight,
+        rel_weight,
+        up_weight,
+        down_weight,
+        small,
+    )
+    pieces = full.reshape(PIECES, groups * piece_rows, conv_weight.shape[2])
+    key_width = query_weight.shape[1]
+    conv_full = pieces[:5]
+    query_full = pieces[5, :, :key_width]
+    key_full = pieces[5, :, key_width : 2 * key_width]
+    rel_rows, rel_columns = rel_weight.shape
+    rel_full = jnp.concatenate(
+        [
+            full[5, shard, :rel_rows, 2 * key_width : 2 * key_width + rel_columns]
+            for shard in range(groups)
+        ],
+        1,
+    )
+    value_full = pieces[6]
+    out_full = pieces[7]
+    up_full = pieces[8:10]
+    down_full = pieces[10:12]
+    flat = small_full.reshape(groups, -1)
+    taken = 0
+    unpacked = []
+    for part in small_parts:
+        chosen = flat[:, taken : taken + part.size].reshape((groups,) + part.shape)
+        unpacked.append(chosen)
+        taken += part.size
+    gain_rows = jnp.moveaxis(unpacked[0], 0, 1).reshape(gains.shape[0], -1)
+    bias_rows = jnp.moveaxis(unpacked[1], 0, 1).reshape(biases.shape[0], -1)
+    up_offset = jnp.moveaxis(unpacked[2].reshape(groups, 2, piece_rows), 0, 1).reshape(2, -1)
+    rel_offset = jnp.moveaxis(unpacked[3], 0, 1).reshape(2, -1)
     inputs = tokens[0].astype(jnp.float32)
     length = inputs.shape[0]
     model_width = inputs.shape[1]
@@ -200,11 +408,15 @@
     )
     standard_two, inverse_two = normalize(after_attention)
     normed_two = (standard_two * gain_rows[2] + bias_rows[4]).astype(jnp.bfloat16)
-    hidden_pre = jnp.dot(normed_two, up_full, preferred_element_type=jnp.float32) + up_offset
-    hidden = jax.nn.gelu(hidden_pre).astype(jnp.bfloat16)
+    hidden_pre = [
+        jnp.dot(normed_two, up_full[half], preferred_element_type=jnp.float32) + up_offset[half]
+        for half in range(2)
+    ]
+    hidden = [jax.nn.gelu(half).astype(jnp.bfloat16) for half in hidden_pre]
     outputs = (
         after_attention
-        + jnp.dot(hidden, down_full, preferred_element_type=jnp.float32)
+        + jnp.dot(hidden[0], down_full[0], preferred_element_type=jnp.float32)
+        + jnp.dot(hidden[1], down_full[1], preferred_element_type=jnp.float32)
         + bias_rows[5]
     )
     target_row = lax.dynamic_index_in_dim(target_table, window_ids[0], 0, keepdims=False)
@@ -213,21 +425,17 @@
     limits = jnp.sum(selector * clip_levels[None, :], 1)[:, None]
     cotangent = jnp.clip(outputs - target_row, -limits, limits).astype(jnp.bfloat16)
     cot_value = cotangent.astype(jnp.float32)
-    conv_back, query_back, key_back, value_back, out_back, up_back, down_back = (
-        lax.all_gather(conv_weight, "fsdp", axis=1, tiled=True),
-        lax.all_gather(query_weight, "fsdp", axis=0, tiled=True),
-        lax.all_gather(key_weight, "fsdp", axis=0, tiled=True),
-        lax.all_gather(value_weight, "fsdp", axis=0, tiled=True),
-        lax.all_gather(out_weight, "fsdp", axis=0, tiled=True),
-        lax.all_gather(up_weight, "fsdp", axis=0, tiled=True),
-        lax.all_gather(down_weight, "fsdp", axis=0, tiled=True),
-    )
-    hidden_grad = dot_trailing(cotangent, down_back)
     grad_down_bias = jnp.sum(cot_value, 0)
-    gelu_pull = jax.vjp(jax.nn.gelu, hidden_pre)[1]
-    pre_grad = gelu_pull(hidden_grad)[0].astype(jnp.bfloat16)
-    grad_up_bias = jnp.sum(pre_grad.astype(jnp.float32), 0)
-    normed_two_grad = dot_trailing(pre_grad, up_back)
+    pre_grad = []
+    for half in range(2):
+        hidden_grad = dot_trailing(cotangent, down_full[half])
+        gelu_pull = jax.vjp(jax.nn.gelu, hidden_pre[half])[1]
+        pre_grad.append(gelu_pull(hidden_grad)[0].astype(jnp.bfloat16))
+    grad_up_bias = jnp.stack([jnp.sum(half.astype(jnp.float32), 0) for half in pre_grad])
+    grad_up_bias = jnp.moveaxis(grad_up_bias.reshape(2, groups, piece_rows), 0, 1).reshape(-1)
+    normed_two_grad = dot_trailing(pre_grad[0], up_full[0]) + dot_trailing(
+        pre_grad[1], up_full[1]
+    )
     grad_gain_two = jnp.sum(normed_two_grad * standard_two, 0)
     grad_bias_two = jnp.sum(normed_two_grad, 0)
     attention_grad = cot_value + norm_back(
@@ -236,7 +444,7 @@
     branch_grad = attention_grad.astype(jnp.bfloat16)
     grad_out_bias = jnp.sum(branch_grad.astype(jnp.float32), 0)
     attended_grad = (
-        dot_trailing(branch_grad, out_back).astype(jnp.bfloat16).reshape(length, HEADS, -1)
+        dot_trailing(branch_grad, out_full).astype(jnp.bfloat16).reshape(length, HEADS, -1)
     )
     scores = attention_scores(content_query, key_heads, position_query, position_keys)
     attention_probs = jnp.exp(scores - normalizer)
@@ -276,9 +484,9 @@
         ((content_grad + position_grad) * key_scale).reshape(length, -1).astype(jnp.bfloat16)
     )
     normed_one_grad = (
-        dot_trailing(query_grad, query_back)
-        + dot_trailing(key_grad, key_back)
-        + dot_trailing(value_grad, value_back)
+        dot_trailing(query_grad, query_full)
+        + dot_trailing(key_grad, key_full)
+        + dot_trailing(value_grad, value_full)
     )
     grad_gain_one = jnp.sum(normed_one_grad * standard_one, 0)
     grad_bias_one = jnp.sum(normed_one_grad, 0)
@@ -287,7 +495,7 @@
     )
     conv_grad = conv_side_grad.astype(jnp.bfloat16)
     grad_conv_bias = jnp.sum(conv_grad.astype(jnp.float32), 0)
-    stacked_grad = dot_trailing(conv_grad, conv_back.reshape(tap_count * model_width, model_width))
+    stacked_grad = dot_trailing(conv_grad, conv_full.reshape(tap_count * model_width, model_width))
     stacked_grad = stacked_grad.reshape(length, tap_count, model_width)
     padded_grad = jnp.zeros((length + 2 * half_taps, model_width), jnp.float32)
     for tap_index in range(tap_count):
@@ -306,39 +514,44 @@
     bias_five = jnp.stack(
         [grad_conv_bias, grad_bias_one, grad_out_bias, grad_bias_two, grad_down_bias]
     )
-    grad_down = dot_leading(hidden, cotangent)
-    grad_up = dot_leading(normed_two, pre_grad)
-    grad_out = dot_leading(attended, branch_grad)
-    grad_query = dot_leading(normed_one, query_grad)
-    grad_key = dot_leading(normed_one, key_grad)
-    grad_value = dot_leading(normed_one, value_grad)
+    half_width = 2 * key_width
+    projection_grad = dot_leading(normed_one, jnp.concatenate([query_grad, key_grad], 1))
     grad_rel = dot_leading(table, table_grad)
-    grad_conv = dot_leading(stacked, conv_grad).reshape(tap_count, model_width, model_width)
+    grad_rel = jnp.moveaxis(grad_rel.reshape(rel_rows, groups, rel_columns), 0, 1)
+    grad_rel = jnp.pad(
+        grad_rel, ((0, 0), (0, piece_rows - rel_rows), (0, model_width - half_width - rel_columns))
+    )
+    mixed_grad = jnp.concatenate(
+        [projection_grad, grad_rel.reshape(model_width, -1)], 1
+    )
+    grad_pieces = [
+        dot_leading(stacked[:, tap * model_width : (tap + 1) * model_width], conv_grad)
+        for tap in range(tap_count)
+    ]
+    grad_pieces += [
+        mixed_grad,
+        dot_leading(normed_one, value_grad),
+        dot_leading(attended, branch_grad),
+        dot_leading(normed_two, pre_grad[0]),
+        dot_leading(normed_two, pre_grad[1]),
+        dot_leading(hidden[0], cotangent),
+        dot_leading(hidden[1], cotangent),
+    ]
+    grad_pieces = jnp.stack([piece.astype(jnp.bfloat16) for piece in grad_pieces])
+    grad_pieces = lax.psum_scatter(grad_pieces, "fsdp", scatter_dimension=1, tiled=True)
+    grad_pieces = lax.psum(grad_pieces, "dp").astype(jnp.float32)
+    up_grad = jnp.moveaxis(grad_pieces[8:10].reshape(2, piece_rows, groups, piece_rows), 0, 2)
+    weight_grads = (
+        grad_pieces[:5],
+        grad_pieces[5, :, :key_width],
+        grad_pieces[5, :, key_width:half_width],
+        grad_pieces[6],
+        grad_pieces[7],
+        grad_pieces[5, :rel_rows, half_width : half_width + rel_columns],
+        up_grad.reshape(piece_rows, -1),
+        grad_pieces[10:12].reshape(2 * piece_rows, -1),
+    )
     parts = (
-        lax.psum_scatter(
-            grad_conv.astype(jnp.bfloat16), "fsdp", scatter_dimension=1, tiled=True
-        ).astype(jnp.float32),
-        lax.psum_scatter(
-            grad_query.astype(jnp.bfloat16), "fsdp", scatter_dimension=0, tiled=True
-        ).astype(jnp.float32),
-        lax.psum_scatter(
-            grad_key.astype(jnp.bfloat16), "fsdp", scatter_dimension=0, tiled=True
-        ).astype(jnp.float32),
-        lax.psum_scatter(
-            grad_value.astype(jnp.bfloat16), "fsdp", scatter_dimension=0, tiled=True
-        ).astype(jnp.float32),
-        lax.psum_scatter(
-            grad_out.astype(jnp.bfloat16), "fsdp", scatter_dimension=0, tiled=True
-        ).astype(jnp.float32),
-        lax.psum_scatter(
-            grad_rel.astype(jnp.bfloat16), "fsdp", scatter_dimension=1, tiled=True
-        ).astype(jnp.float32),
-        lax.psum_scatter(
-            grad_up.astype(jnp.bfloat16), "fsdp", scatter_dimension=0, tiled=True
-        ).astype(jnp.float32),
-        lax.psum_scatter(
-            grad_down.astype(jnp.bfloat16), "fsdp", scatter_dimension=0, tiled=True
-        ).astype(jnp.float32),
         lax.psum_scatter(
             ln_gains.astype(jnp.bfloat16), "fsdp", scatter_dimension=1, tiled=True
         ).astype(jnp.float32),
@@ -357,36 +570,21 @@
         lax.psum(parts[1].astype(jnp.bfloat16), "dp").astype(jnp.float32),
         lax.psum(parts[2].astype(jnp.bfloat16), "dp").astype(jnp.float32),
         lax.psum(parts[3].astype(jnp.bfloat16), "dp").astype(jnp.float32),
-        lax.psum(parts[4].astype(jnp.bfloat16), "dp").astype(jnp.float32),
-        lax.psum(parts[5].astype(jnp.bfloat16), "dp").astype(jnp.float32),
-        lax.psum(parts[6].astype(jnp.bfloat16), "dp").astype(jnp.float32),
-        lax.psum(parts[7].astype(jnp.bfloat16), "dp").astype(jnp.float32),
-        lax.psum(parts[8].astype(jnp.bfloat16), "dp").astype(jnp.float32),
-        lax.psum(parts[9].astype(jnp.bfloat16), "dp").astype(jnp.float32),
-        lax.psum(parts[10].astype(jnp.bfloat16), "dp").astype(jnp.float32),
-        lax.psum(parts[11].astype(jnp.bfloat16), "dp").astype(jnp.float32),
     )
     shard_width = gains.shape[1]
     shard_start = lax.axis_index("fsdp") * shard_width
     bn_gain_shard = lax.dynamic_slice_in_dim(grad_bn_gain, shard_start, shard_width)
     bn_bias_shard = lax.dynamic_slice_in_dim(grad_bn_bias, shard_start, shard_width)
-    gains_out = jnp.concatenate([bn_gain_shard[None], reduced[8]], 0)
-    biases_out = jnp.concatenate([bn_bias_shard[None], reduced[9]], 0)
+    gains_out = jnp.concatenate([bn_gain_shard[None], reduced[0]], 0)
+    biases_out = jnp.concatenate([bn_bias_shard[None], reduced[1]], 0)
     return (
         outputs.astype(jnp.bfloat16)[None],
         input_grad.astype(jnp.bfloat16)[None],
-        reduced[0],
-        reduced[1],
+        *weight_grads,
+        gains_out,
+        biases_out,
         reduced[2],
         reduced[3],
-        reduced[4],
-        reduced[5],
-        reduced[6],
-        reduced[7],
-        gains_out,
-        biases_out,
-        reduced[10],
-        reduced[11],
     )
 
 

time: 2410 us -> 1910 us (0.79)
  waiting for transfers between devices: 1640 us -> 1010 us
  Pallas kernels: 0 us -> 199 us
  blocking collectives: 254 us -> 116 us
  local copies, waits for them, and re-layouts: 202 us -> 293 us
  matrix products: 220 us -> 193 us
    all_gather x7 -> x0, waiting for transfers between devices: 652 us -> none  [the longest x1 210 us: on_device(): lax.all_gather(conv_weight, 'fsdp', axis=1, tiled=True)]
    pallas_call x0 -> x1, Pallas kernels: none -> 199 us  [gather(): pl.pallas_call(functools.partial(gather_kernel, groups), out_shape=(jax.S...]
    all_gather x5 -> x0, blocking collectives: 107 us -> none  [the longest x1 31.1 us: on_device(): lax.all_gather(rel_weight, 'fsdp', axis=1, tiled=True)]
    slice x1 -> x10, local copies, waits for them, and re-layouts: 0.1 us -> 54.5 us  [the longest x1 20.6 us: on_device(): up_full[half]]
    reduce_scatter x7 -> x1, waiting for transfers between devices: 870 us -> 920 us  [on_device(): lax.psum_scatter(grad_pieces, 'fsdp', scatter_dimension=1, tiled=True)]
    psum x1, blocking collectives: 69.4 us -> 38.1 us  [on_device(): lax.psum((jnp.sum(inputs, 0), jnp.sum(inputs * inputs, 0)), ('dp', 'fsdp'))]
    dot_general x8 -> x13, matrix products: 60.8 us -> 50.6 us  [dot_leading(): lax.dot_general(left_side, right_side, (((0,), (0,)), ((), ())), preferre...]
    dot_general x7 -> x9, matrix products: 54.4 us -> 53.8 us  [dot_trailing(): lax.dot_general(left_side, right_side, (((1,), (1,)), ((), ())), preferre...]
  transfers between devices with their start and end apart: 19 -> 5, of which waited for: 12 -> 2; matrix products, arithmetic and copies ran while one was open for 14% -> 5% of each run, Pallas kernels for 0% -> 0%
where the time goes in v1:
time: 1910 us
  waiting for transfers between devices  1010 us (53%)
  local copies, waits for them, and re-layouts  293 us (15%)
  Pallas kernels  199 us (10%)
  matrix products  193 us (10%)
  blocking collectives  116 us (6%)
  other arithmetic  77.2 us (4%)
    reduce_scatter x1, waiting for transfers between devices, on_device(): lax.psum_scatter(grad_pieces, 'fsdp', scatter_dimension=1, tiled=True)  920 us
    pallas_call x1, Pallas kernels, gather(): pl.pallas_call(functools.partial(gather_kernel, groups), out_shape=(jax.S...  199 us
    psum x1, waiting for transfers between devices, on_device(): grad_pieces = lax.psum(grad_pieces, 'dp').astype(jnp.float32)  91 us
    dot_general x9, matrix products, dot_trailing(): lax.dot_general(left_side, right_side, (((1,), (1,)), ((), ())), preferre...  53.8 us
    dot_general x13, matrix products, dot_leading(): lax.dot_general(left_side, right_side, (((0,), (0,)), ((), ())), preferre...  50.6 us
    psum x1, blocking collectives, on_device(): lax.psum((jnp.sum(normed_grad * standard, 0), jnp.sum(normed_grad, 0)), (...  43.5 us
    unnamed x264, local copies, waits for them, and re-layouts  41.5 us
    reshape x2, local copies, waits for them, and re-layouts, relative_shift(): return folded.reshape(leading + (row_count, span_width))[..., :row_count]  41.2 us
  transfers between devices with their start and end apart: 5, of which 2 were waited for; matrix products, arithmetic and copies ran while one was open for 5% of the time, Pallas kernels for 0%

profile of v1, /device:TPU:0, one launch (start us, length us, event | category | flops | bytes accessed | tf_op | source)
XLA Modules:
  0.0 1905.9 jit_solution(16072452060361648050)
XLA Ops:
  25.1 198.7 %gather.1 = (bf16[12,4,384,1536]{3,2,1,0:T(8,128)(2,1)}, f32[4,40,128]{2,1,0:T(8,128)S(1)}) custom-call(bf16[5,384,1536]{2,1,0:T(8,128)(2,1)S(1)} %copy-done.2, bf16[384,512]{1,0:T(8,128)(2,1)S(1)} %copy-done.7, bf16[384,512]{1,0:T(8,128)(2,1)S(1)} %copy-done.8, bf16[384,1536]{1,0:T(8,128)(2,1)S(1)} %copy-done.5, bf16[384,1536]{1,0:T(8,128)(2,1)S(1)} %copy-done.6, ...), custom_call_target="tpu_custom_call" | custom-call | tf_op jit(solution)/shard_map/gather/pallas_call | solution.py:195
  225.4 19.8 %slice.291 = bf16[5,4,384,1536]{3,2,1,0:T(8,128)(2,1)} slice(bf16[12,4,384,1536]{3,2,1,0:T(8,128)(2,1)} %get-tuple-element.77), slice={[0:5], [0:4], [0:384], [0:1536]} | slice | bytes 47185920 | tf_op jit(solution)/shard_map/slice | solution.py:317
  245.3 20.6 %fusion.146 = (bf16[1,4,384,1536]{3,2,1,0:T(8,128)(2,1)}, bf16[1,4,384,1536]{3,2,1,0:T(8,128)(2,1)}, bf16[1,4,384,1536]{3,2,1,0:T(8,128)(2,1)}, bf16[1,4,384,153...) fusion(bf16[12,4,384,1536]{3,2,1,0:T(8,128)(2,1)} %get-tuple-element.77), kind=kLoop, calls=%fused_computation.268 | loop fusion | bytes 56623104 | tf_op jit(solution)/shard_map/slice | solution.py:412
  273.9 38.1 %all-reduce.9 = (f32[1536]{0:T(1024)S(1)}, f32[1536]{0:T(1024)S(1)}) all-reduce(f32[1536]{0:T(1024)S(1)} %copy-done.76, f32[1536]{0:T(1024)S(1)} %copy-done.77), channel_id=1, replica_groups=mesh['dp'=8,'fsdp'=4] {'dp','fsdp'}, use_global_device_ids=true, to_apply=%region_3.4 | all-reduce | flops 3072 | bytes 24576 | tf_op jit(solution)/shard_map/psum | solution.py:349
  317.2 16.3 fusion.151
  335.2 3.8 fusion.95
  345.6 7.6 pad.44
  353.2 18.3 reshape.500
  371.5 12.1 slice.349
  383.5 19.4 %reshape.501 = f32[8,512,1023]{2,1,0:T(8,128)} reshape(f32[8,1023,512]{2,1,0:T(8,128)} %slice.349) | data formatting | bytes 33521664 | tf_op jit(solution)/shard_map/reshape | solution.py:240
  402.9 7.8 slice.350
  410.6 9.3 copy.95
  420.0 5.0 fusion.152
  428.4 6.1 convolution_convert_fusion.13
  437.1 5.4 convolution_convert_fusion.15
  442.5 5.4 fusion.153
  453.4 5.1 convolution_add_fusion.3
  464.6 5.3 fusion.143
  469.9 5.9 fusion.141
  475.7 6.5 fusion.139
  485.0 3.9 multiply_reduce_fusion.1
  492.7 3.8 convolution_convert_fusion.12
  499.3 6.7 convolution_convert_fusion.14
  506.0 4.8 multiply_reduce_fusion
  517.7 6.4 copy.96
  524.1 6.7 pad.45.clone
  530.8 21.9 %reshape.504 = bf16[8,1023,512]{2,1,0:T(8,128)(2,1)} reshape(bf16[8,512,1023]{2,1,0:T(8,128)(2,1)} %pad.45.clone) | data formatting | bytes 16760832 | tf_op jit(solution)/shard_map/transpose(jvp())/reshape | solution.py:240
  552.7 8.9 pad.46
  561.6 13.1 reshape.505
  574.7 6.8 fusion.92
  584.3 5.2 fusion.156
  595.8 3.9 multiply_reduce_fusion.2
  602.2 4.3 fusion.5
  606.6 4.4 fusion.7
  610.9 4.4 fusion.9
  615.3 4.3 fusion.11
  619.6 4.5 fusion.13
  626.7 4.3 fusion.15
  631.0 4.3 fusion.17
  635.3 4.4 fusion.19
  639.7 4.4 fusion.21
  644.2 4.5 fusion.23
  648.6 4.4 fusion.25
  656.7 920.0 %reduce-scatter.11.cloned.1.call-done = bf16[12,384,1536]{2,1,0:T(8,128)(2,1)} async-done(((bf16[12,1536,1536]{2,1,0:T(8,128)(2,1)}), bf16[12,384,1536]{2,1,0:T(8,128)(2,1)}) %reduce-scatter.11.cloned.1.call-update) | async-done | bytes 14155792 | tf_op jit(solution)/shard_map/reduce_scatter | solution.py:541
  1578.1 19.5 %fusion.78 = f32[512,5,1536]{2,0,1:T(8,128)} fusion(bf16[5,1536,1536]{2,1,0:T(8,128)(2,1)} %bitcast.327, bf16[512,1536]{1,0:T(8,128)(2,1)S(1)} %copy-done.35), kind=kOutput, calls=%fused_computation.141 | convolution fusion | flops 12079595520 | bytes 40894464 | tf_op jit(solution)/shard_map/dot_general | solution.py:264
  1601.6 4.2 fusion.77
  1605.8 8.4 scatter-add.19
  1617.7 7.7 scatter-add.20
  1628.9 7.7 scatter-add.21
  1636.7 5.2 fusion.74
  1641.9 8.5 scatter-add.24
  1650.5 6.2 fusion.138
  1656.6 43.5 %all-reduce.8 = (f32[1536]{0:T(1024)S(1)}, f32[1536]{0:T(1024)S(1)}) all-reduce(f32[1536]{0:T(1024)S(1)} %get-tuple-element.87, f32[1536]{0:T(1024)S(1)} %get-tuple-element.86), channel_id=1, replica_groups=mesh['dp'=8,'fsdp'=4] {'dp','fsdp'}, use_global_device_ids=true, to_apply=%region_20.21 | all-reduce | flops 3072 | bytes 24576 | tf_op jit(solution)/shard_map/psum | solution.py:506
  1701.5 10.8 all-reduce.7
  1712.4 5.3 fusion.80
  1720.6 23.2 %all-reduce.10 = (bf16[2,384]{1,0:T(2,128)(2,1)S(1)}, bf16[5,384]{1,0:T(8,128)(2,1)S(1)}, bf16[768]{0:T(1024)(128)(2,1)S(1)}, bf16[2,128]{1,0:T(2,128)(2,1)S(1)}) all-reduce(bf16[2,384]{1,0:T(2,128)(2,1)S(1)} %copy.90, bf16[5,384]{1,0:T(8,128)(2,1)S(1)} %copy.92, ...), channel_id=1, replica_groups=mesh['dp'=8,'fsdp'=4] {'dp'}, use_global_device_ids=true, to_apply=%region_26.27 | all-reduce | flops 3712 | bytes 14848 | tf_op jit(solution)/shard_map/psum | solution.py:569
  1746.2 91.0 %all-reduce.13.cloned.1.call-done = bf16[12,384,1536]{2,1,0:T(8,128)(2,1)} async-done(((bf16[12,384,1536]{2,1,0:T(8,128)(2,1)}), bf16[12,384,1536]{2,1,0:T(8,128)(2,1)}) %all-reduce.13.cloned.1.call-update) | async-done | bytes 14155792 | tf_op jit(solution)/shard_map/psum | solution.py:542
  1837.2 16.8 convert_element_type.274
  1859.0 4.9 slice_bitcast_fusion.5
  1863.9 5.1 fusion.147
  1868.9 6.2 reshape.510
  1875.1 8.1 copy.82
  1883.2 7.0 reshape.511
  1890.2 8.9 slice.367
  (396 shorter events, 113.9 us)
Async XLA Ops:
  7.2 443.5 %copy-start = (f32[64,1536]{1,0:T(8,128)S(1)}, f32[64,1536]{1,0:T(8,128)}, u32[]{:S(2)}) copy-start(f32[64,1536]{1,0:T(8,128)} %param.40) | copy-start | bytes 1179652
  7.2 8.1 copy-start.89
  7.2 10.1 copy-start.3
  7.2 10.1 copy-start.8
  7.2 10.1 copy-start.7
  7.2 1569.4 %reduce-scatter.11.cloned.1.call-start = ((), (), s32[]{:S(2)}) async-start(), calls=%async_computation.4 | async-start | bytes 70778880 | tf_op jit(solution)/shard_map/reduce_scatter | solution.py:541
  245.2 21.3 %copy-start.95 = (s32[1,512]{1,0:T(1,128)S(1)}, s32[1,512]{1,0:T(1,128)}, u32[]{:S(2)}) copy-start(s32[1,512]{1,0:T(1,128)} %param.43) | copy-start | bytes 6148
  245.2 21.3 %copy-start.101 = (f32[16]{0:T(128)S(1)}, f32[16]{0:T(128)}, u32[]{:S(2)}) copy-start(f32[16]{0:T(128)} %param.41) | copy-start | bytes 196
  245.2 22.0 %copy-start.104 = (f32[31]{0:T(128)S(1)}, f32[31]{0:T(128)}, u32[]{:S(2)}) copy-start(f32[31]{0:T(128)} %fusion.126) | copy-start | bytes 376
  245.3 22.0 %copy-start.100 = (f32[32]{0:T(128)S(1)}, f32[32]{0:T(128)}, u32[]{:S(2)}) copy-start(f32[32]{0:T(128)} %power_add_fusion) | copy-start | bytes 388
  245.3 28.6 %copy-start.76 = (f32[1536]{0:T(1024)S(1)}, f32[1536]{0:T(1024)}, u32[]{:S(2)}) copy-start(f32[1536]{0:T(1024)} %fusion.56) | copy-start | bytes 18436
  245.3 28.6 %copy-start.77 = (f32[1536]{0:T(1024)S(1)}, f32[1536]{0:T(1024)}, u32[]{:S(2)}) copy-start(f32[1536]{0:T(1024)} %convert_reduce_fusion) | copy-start | bytes 18436
  245.3 66.8 %copy-start.14 = (bf16[1,512,1536]{2,1,0:T(8,128)(2,1)S(1)}, bf16[1,512,1536]{2,1,0:T(8,128)(2,1)}, u32[]{:S(2)}) copy-start(bf16[1,512,1536]{2,1,0:T(8,128)(2,1)} %param.27) | copy-start | bytes 4718596
  271.3 43.0 %copy-start.46 = (f32[1536]{0:T(1024)}, f32[1536]{0:T(1024)S(1)}, u32[]{:S(2)}) copy-start(f32[1536]{0:T(1024)S(1)} %mul.415) | copy-start | bytes 18436
  271.3 63.3 %copy-start.54 = (f32[1536]{0:T(1024)}, f32[1536]{0:T(1024)S(1)}, u32[]{:S(2)}) copy-start(f32[1536]{0:T(1024)S(1)} %mul.425) | copy-start | bytes 18436
  272.1 42.2 %copy-start.56 = (f32[1536]{0:T(1024)}, f32[1536]{0:T(1024)S(1)}, u32[]{:S(2)}) copy-start(f32[1536]{0:T(1024)S(1)} %add.338) | copy-start | bytes 18436
  334.2 4.9 copy-start.78
  334.6 8.0 copy-start.63
  335.2 7.3 copy-start.38
  335.2 3.8 copy-start.96
  437.1 5.5 copy-start.75
  442.5 5.4 copy-start.25
  450.7 7.8 slice-start.6
  453.3 5.1 copy-start.41
  453.4 5.1 slice-start.7
  453.4 5.1 copy-start.84
  453.4 7.8 slice-start.8
  458.5 11.4 copy-start.109
  458.6 6.0 slice-start.10
  469.9 19.0 copy-start.36
  469.9 15.0 slice-start.4
  475.7 9.2 slice-start.5
  482.2 10.5 slice-start.2
  485.0 7.7 slice-start.3
  499.2 6.8 copy-start.21
  499.3 6.8 copy-start.22
  499.3 11.6 slice-start
  506.0 4.8 slice-start.1
  510.9 4.6 copy-start.29
  574.7 6.8 copy-start.27
  574.7 6.8 copy-start.33
  584.3 5.2 copy-start.13
  584.3 5.2 copy-start.31
  595.8 3.9 copy-start.24
  602.2 17.4 copy-start.34
  626.7 4.3 copy-start.26
  631.0 4.3 copy-start.42
  631.0 4.3 copy-start.108
  635.3 4.4 copy-start.106
  639.7 4.4 copy-start.37
  639.7 4.4 copy-start.112
  644.2 4.5 copy-start.110
  653.1 1064.6 %reduce-scatter.17.cloned.1.call-start = ((), (), s32[]{:S(2)}) async-start(), calls=%async_computation.8 | async-start | bytes 163840
  654.2 1064.4 %reduce-scatter.13.cloned.1.call-start = ((), (), s32[]{:S(2)}) async-start(), calls=%async_computation.6 | async-start | bytes 491520
  655.3 1064.3 %reduce-scatter.15.cloned.1.call-start = ((), (), s32[]{:S(2)}) async-start(), calls=%async_computation.7 | async-start | bytes 491520
  656.5 1180.7 %all-reduce.13.cloned.1.call-start = ((), (), s32[]{:S(2)}) async-start(), calls=%async_computation.5 | async-start | bytes 28311552 | tf_op jit(solution)/shard_map/psum | solution.py:542
  1641.9 8.5 copy-start.16
  1641.9 8.5 copy-start.47
  1641.9 8.5 copy-start.49
  1641.9 8.5 copy-start.51
  1641.9 8.5 copy-start.57
  1650.4 49.8 %copy-start.103 = (u32[32]{0:T(128)S(1)}, u32[32]{0:T(128)}, u32[]{:S(2)}) copy-start(u32[32]{0:T(128)} %constant.271) | copy-start | bytes 388
  1837.2 26.6 %copy-start.11 = (bf16[12,384,1536]{2,1,0:T(8,128)(2,1)S(1)}, bf16[12,384,1536]{2,1,0:T(8,128)(2,1)}, u32[]{:S(2)}) copy-start(bf16[12,384,1536]{2,1,0:T(8,128)(2,1)} %all-reduce.13.cloned.1.call-done) | copy-start | bytes 42467332
  1890.2 8.9 copy-start.1
  (66 other events, 155.8 us)
Sparse Core Ops, SparseCore 0:
  653.3 923.3 reduce-scatter.10
  1579.6 21.1 reduce-scatter.16
  1603.6 18.8 reduce-scatter.12
  1625.3 18.8 reduce-scatter.14
  1647.6 189.6 all-reduce.12

commit v2 on v1

v2 whole, which is shorter than its diff:
```python
import functools
import math

import jax
import jax.numpy as jnp
from jax import lax
from jax.experimental import pallas as pl
from jax.experimental.pallas import tpu as pltpu
from jax.sharding import PartitionSpec as P

HEADS = 8
KEY = 64
MESH = pl.DeviceIdType.MESH
AHEAD = 2


def neighbours(dp):
    core = dp % 2
    along_x = dp // 2 % 2
    along_y = dp // 4 % 2
    return dp + 1 - 2 * core, dp + 2 - 4 * along_x, dp + 4 - 8 * along_y


def remote(src, dst, send_sem, recv_sem, device):
    return pltpu.make_async_remote_copy(
        src_ref=src,
        dst_ref=dst,
        send_sem=send_sem,
        recv_sem=recv_sem,
        device_id=device,
        device_id_type=MESH,
    )


def meet(peers):
    barrier = pltpu.get_barrier_semaphore()
    for peer in peers:
        pl.semaphore_signal(barrier, inc=1, device_id=peer, device_id_type=MESH)
    pl.semaphore_wait(barrier, len(peers))


def peers_of(groups, blocks):
    dp = lax.axis_index("dp")
    me = lax.axis_index("fsdp")
    near = [(device, me) for device in neighbours(dp)]
    shards = [(dp, (me + 1 + j) % groups) for j in range(groups - 1)]
    far = [((dp + 8 * (1 + j)) % (8 * blocks), me) for j in range(blocks - 1)]
    return near, shards, far


def sum_steps(groups, blocks, vector, total, near_got, sums, shard_got, block_got, sems):
    near_send, near_recv, shard_send, shard_recv, block_send, block_recv = sems
    me = lax.axis_index("fsdp")
    block = lax.axis_index("dp") // 8
    near, shards, far = peers_of(groups, blocks)

    def near_copy(step):
        src = vector if step == 0 else sums.at[step - 1]
        return remote(
            src, near_got.at[step], near_send.at[step], near_recv.at[step], near[step]
        )

    def fold(step):
        copy = near_copy(step)
        copy.wait()
        held = vector[...] if step == 0 else sums[step - 1]
        sums[step] = held + near_got[step]

    def shard_copy(j):
        return remote(
            sums.at[2], shard_got.at[me], shard_send.at[j], shard_recv.at[me], shards[j]
        )

    def block_copy(j):
        return remote(
            sums.at[3], block_got.at[block], block_send.at[j], block_recv.at[block], far[j]
        )

    def start():
        near_copy(0).start()

    def second():
        fold(0)
        near_copy(1).start()

    def third():
        fold(1)
        near_copy(2).start()

    def fourth():
        fold(2)
        for j in range(groups - 1):
            shard_copy(j).start()
        shard_got[me] = sums[2]

    def fifth():
        for j in range(groups - 1):
            shard_copy(j).wait_send()
            other = (me + 1 + j) % groups
            remote(
                sums.at[2], shard_got.at[other], shard_send.at[j], shard_recv.at[other], shards[j]
            ).wait_recv()
        added = shard_got[0]
        for shard in range(1, groups):
            added = added + shard_got[shard]
        sums[3] = added
        for j in range(blocks - 1):
            block_copy(j).start()
        block_got[block] = added

    def sixth():
        for j in range(blocks - 1):
            block_copy(j).wait_send()
            other = (block + 1 + j) % blocks
            remote(
                sums.at[3], block_got.at[other], block_send.at[j], block_recv.at[other], far[j]
            ).wait_recv()
        added = block_got[0]
        for other in range(1, blocks):
            added = added + block_got[other]
        total[...] = added

    return [start, second, third, fourth, fifth, sixth]


def sum_scratch(groups, blocks, shape):
    return [
        pltpu.VMEM((3,) + shape, jnp.float32),
        pltpu.VMEM((4,) + shape, jnp.float32),
        pltpu.VMEM((groups,) + shape, jnp.float32),
        pltpu.VMEM((blocks,) + shape, jnp.float32),
        pltpu.SemaphoreType.DMA((3,)),
        pltpu.SemaphoreType.DMA((3,)),
        pltpu.SemaphoreType.DMA((groups,)),
        pltpu.SemaphoreType.DMA((groups,)),
        pltpu.SemaphoreType.DMA((blocks,)),
        pltpu.SemaphoreType.DMA((blocks,)),
    ]


def gather_kernel(groups, blocks, *refs):
    weights = refs[:8]
    conv, query, key, value, out, up, down, rel = weights
    small, stats = refs[8:10]
    outs = refs[10:21]
    rel_full, small_full, stat_total = outs[8:]
    hold, hold_mixed, local_sem, write_sem = refs[21:25]
    z_sem, x_sem, y_sem, d_sem, sib_sem, send_sem, right_send, left_send = refs[25:33]
    rel_send, rel_recv, small_send, small_recv = refs[33:37]
    near_got, sums, shard_got, block_got = refs[37:41]
    sum_sems = refs[41:47]
    dp = lax.axis_index("dp")
    me = lax.axis_index("fsdp")
    near, shards, far = peers_of(groups, blocks)
    sib, along_x, along_y = neighbours(dp)
    rows = conv.shape[1]
    part = rows // 8
    others = groups - 1
    pieces = [outs[0].at[tap] for tap in range(5)] + list(outs[1:8])
    count = len(pieces)
    holds = [hold.at[i] for i in range(5)] + [hold_mixed] + [hold.at[i] for i in range(5, 11)]

    pending = [[] for _ in range(count)]
    started = [0]

    def load(src, dst, piece):
        copy = pltpu.make_async_copy(src, dst, local_sem.at[started[0]])
        copy.start()
        started[0] += 1
        pending[piece].append(copy)

    for tap in range(5):
        load(conv.at[tap], holds[tap], tap)
    width = query.shape[1]
    load(query, hold_mixed.at[:, pl.ds(0, width)], 5)
    load(key, hold_mixed.at[:, pl.ds(width, width)], 5)
    load(value, holds[6], 6)
    load(out, holds[7], 7)
    for half in range(2):
        for shard in range(groups):
            load(
                up.at[:, pl.ds((shard * 2 + half) * rows, rows)],
                holds[8 + half].at[:, pl.ds(shard * rows, rows)],
                8 + half,
            )
    for half in range(2):
        load(down.at[pl.ds(half * rows, rows)], holds[10 + half], 10 + half)

    meet(near + shards + far)

    summing = sum_steps(
        groups, blocks, stats, stat_total, near_got, sums, shard_got, block_got, sum_sems
    )
    summing[0]()

    for j in range(others):
        remote(
            rel, rel_full.at[me], rel_send.at[j], rel_recv.at[me], shards[j]
        ).start()
        remote(
            small, small_full.at[me], small_send.at[j], small_recv.at[me], shards[j]
        ).start()
    rel_full[me] = rel[...]
    small_full[me] = small[...]

    def slice_of(piece, shard, owner):
        return pieces[piece].at[shard, pl.ds(pl.multiple_of(owner % 8 * part, 16), part)]

    def copy_of(piece, shard, owner, recv_sem, device):
        ref = slice_of(piece, shard, owner)
        return remote(ref, ref, send_sem.at[piece], recv_sem, (device, me))

    order = []
    for j in range(others):
        pick = 0
        for m in range(groups):
            nearest = sorted((t for t in range(groups) if t != m), key=lambda t: abs(t - m))
            pick = pick + jnp.where(me == m, nearest[j], 0)
        order.append(pick)

    def right_copy(piece, shard, src=None):
        dst = slice_of(piece, shard, dp)
        return remote(
            dst if src is None else src,
            dst,
            right_send.at[piece, shard],
            z_sem.at[piece, shard],
            (dp, (me + 1) % groups),
        )

    def left_copy(piece, shard, src=None):
        dst = slice_of(piece, shard, dp)
        return remote(
            dst if src is None else src,
            dst,
            left_send.at[piece, shard],
            z_sem.at[piece, shard],
            (dp, (me + groups - 1) % groups),
        )

    def z_send(piece):
        src = holds[piece].at[pl.ds(pl.multiple_of(dp % 8 * part, 16), part)]

        @pl.when(me + 1 < groups)
        def _():
            right_copy(piece, me, src).start()

        @pl.when(me > 0)
        def _():
            left_copy(piece, me, src).start()

    diagonal = neighbours(along_x)[2]

    def stage_a(piece):
        for shard in order:
            copy_of(piece, shard, dp, z_sem.at[piece, shard], dp).wait_recv()

            @pl.when(jnp.logical_and(shard < me, me + 1 < groups))
            def _():
                right_copy(piece, shard).start()

            @pl.when(jnp.logical_and(shard > me, me > 0))
            def _():
                left_copy(piece, shard).start()

            copy_of(piece, shard, dp, x_sem.at[piece, shard], along_x).start()
            copy_of(piece, shard, dp, y_sem.at[piece, shard], along_y).start()
            copy_of(piece, shard, dp, sib_sem.at[piece], sib).start()

    def stage_b(piece):
        for shard in order:
            route = (piece + shard) % 2
            copy_of(piece, shard, along_x, x_sem.at[piece, shard], dp).wait_recv()
            copy_of(piece, shard, along_y, y_sem.at[piece, shard], dp).wait_recv()
            owner = route * along_x + (1 - route) * along_y
            target = route * along_y + (1 - route) * along_x
            copy_of(piece, shard, owner, d_sem.at[piece, shard], target).start()
            copy_of(piece, shard, along_x, sib_sem.at[piece], sib).start()
            copy_of(piece, shard, along_y, sib_sem.at[piece], sib).start()

    def stage_c(piece):
        for shard in order:
            copy_of(piece, shard, diagonal, d_sem.at[piece, shard], dp).wait_recv()
            copy_of(piece, shard, diagonal, sib_sem.at[piece], sib).start()

    writes = []
    for piece in range(count):
        for copy in pending[piece]:
            copy.wait()
        copy = pltpu.make_async_copy(holds[piece], pieces[piece].at[me], write_sem.at[piece])
        copy.start()
        writes.append(copy)
        if piece < AHEAD:
            z_send(piece)

    for n in range(count + 2):
        if n + AHEAD < count:
            z_send(n + AHEAD)
        if n < count:
            stage_a(n)
        if 1 <= n <= count:
            stage_b(n - 1)
        if n >= 2:
            stage_c(n - 2)
        if 1 <= n < len(summing):
            summing[n]()

    for piece in range(count):
        for shard in range(groups):

            @pl.when(jnp.logical_and(shard <= me, me + 1 < groups))
            def _():
                right_copy(piece, shard).wait_send()

            @pl.when(jnp.logical_and(shard >= me, me > 0))
            def _():
                left_copy(piece, shard).wait_send()

        writes[piece].wait()
        got = pieces[piece].at[pl.ds(0, others), pl.ds(0, 4 * part)]
        remote(got, got, send_sem.at[piece], sib_sem.at[piece], (sib, me)).wait_recv()
        sent = pieces[piece].at[pl.ds(0, others), pl.ds(0, 7 * part)]
        remote(sent, sent, send_sem.at[piece], sib_sem.at[piece], (sib, me)).wait_send()
    for j in range(others):
        shard = (me + 1 + j) % groups
        remote(rel, rel_full.at[shard], rel_send.at[j], rel_recv.at[shard], shards[j]).wait()
        remote(
            small, small_full.at[shard], small_send.at[j], small_recv.at[shard], shards[j]
        ).wait()


def gather(groups, blocks, weights, small, stats):
    conv, query = weights[:2]
    rel = weights[7]
    taps, rows, columns = conv.shape
    dtype = conv.dtype
    kept = pl.BlockSpec(memory_space=pl.ANY)
    inside = pl.BlockSpec(memory_space=pltpu.VMEM)
    full = jax.ShapeDtypeStruct((groups, rows, columns), dtype)
    count = taps + 7
    grid_sems = [pltpu.SemaphoreType.DMA((count, groups))] * 4
    return pl.pallas_call(
        functools.partial(gather_kernel, groups, blocks),
        out_shape=(
            jax.ShapeDtypeStruct((taps, groups, rows, columns), dtype),
            jax.ShapeDtypeStruct((groups, rows, 2 * query.shape[1]), dtype),
            *([full] * 6),
            jax.ShapeDtypeStruct((groups,) + rel.shape, dtype),
            jax.ShapeDtypeStruct((groups,) + small.shape, jnp.float32),
            jax.ShapeDtypeStruct(stats.shape, jnp.float32),
        ),
        in_specs=[kept] * 7 + [inside] * 3,
        out_specs=[kept] * 8 + [inside] * 3,
        scratch_shapes=[
            pltpu.VMEM((count - 1, rows, columns), dtype),
            pltpu.VMEM((rows, 2 * query.shape[1]), dtype),
            pltpu.SemaphoreType.DMA((taps + 6 + 2 * groups,)),
            pltpu.SemaphoreType.DMA((count,)),
            *grid_sems,
            pltpu.SemaphoreType.DMA((count,)),
            pltpu.SemaphoreType.DMA((count,)),
            *grid_sems[:2],
            *([pltpu.SemaphoreType.DMA((groups,))] * 4),
            *sum_scratch(groups, blocks, stats.shape),
        ],
        compiler_params=pltpu.CompilerParams(
            collective_id=0, has_side_effects=True, vmem_limit_bytes=24 << 20
        ),
        name="gather",
    )(*weights, small, stats)


def reduce_kernel(groups, blocks, rel_at, *refs):
    lefts = refs[:6]
    lefts_sib = refs[6:12]
    conv_right, conv_right_sib = refs[12:14]
    rights = refs[14:21]
    rights_sib = refs[21:28]
    rel_grad, vector = refs[28:30]
    out, total = refs[30:32]
    left_hold, right_hold, grad, x_one, y_one, x_two, y_two, shard_got, block_got, partial, done = refs[32:43]
    load_sem = refs[43]
    x1s, y1s, x2s, y2s, x1r, y1r, x2r, y2r = refs[44:52]
    shard_send, shard_recv, block_send, block_recv = refs[52:56]
    write_sem, send_sem, ax, ay, ad, sib_sem = refs[56:62]
    sum_bufs = refs[62:66]
    sum_sems = refs[66:72]

    dp = lax.axis_index("dp")
    me = lax.axis_index("fsdp")
    near, shards, far = peers_of(groups, blocks)
    sib, along_x, along_y = neighbours(dp)
    core = dp % 2
    at_x = dp // 2 % 2
    at_y = dp // 4 % 2
    block = dp // 8
    slots = grad.shape[0]
    part = grad.shape[4]
    width = grad.shape[5]
    half = width // 2
    rows = 4 * part
    count = out.shape[0]
    others = groups - 1
    first = pl.ds(0, half)
    last = pl.ds(half, half)
    left_of = [0] * 5 + [1, 1, 2, 3, 3, 4, 5]

    def loads(piece, slot):
        right = conv_right.at[piece] if piece < 5 else rights[piece - 5]
        right_sib = conv_right_sib.at[piece] if piece < 5 else rights_sib[piece - 5]
        pairs = (
            (lefts[left_of[piece]], left_hold.at[slot, 0]),
            (lefts_sib[left_of[piece]], left_hold.at[slot, 1]),
            (right, right_hold.at[slot, 0]),
            (right_sib, right_hold.at[slot, 1]),
        )
        return [
            pltpu.make_async_copy(src, dst, load_sem.at[slot, i])
            for i, (src, dst) in enumerate(pairs)
        ]

    for copy in loads(0, 0):
        copy.start()

    meet(near + shards + far)

    summing = sum_steps(groups, blocks, vector, total, *sum_bufs, sum_sems)

    def one(piece):
        slot = piece % slots
        return (
            remote(
                grad.at[slot, :, :, 1 - at_x, :, first],
                x_one.at[piece],
                x1s.at[piece],
                x1r.at[piece],
                (along_x, me),
            ),
            remote(
                grad.at[slot, :, 1 - at_y, :, :, last],
                y_one.at[piece],
                y1s.at[piece],
                y1r.at[piece],
                (along_y, me),
            ),
        )

    def two(piece):
        slot = piece % slots
        return (
            remote(
                grad.at[slot, :, 1 - at_y, at_x, :, first],
                y_two.at[piece],
                y2s.at[piece],
                y2r.at[piece],
                (along_y, me),
            ),
            remote(
                grad.at[slot, :, at_y, 1 - at_x, :, last],
                x_two.at[piece],
                x2s.at[piece],
                x2r.at[piece],
                (along_x, me),
            ),
        )

    def shard_copy(piece, j):
        other = (me + 1 + j) % groups
        return remote(
            grad.at[piece % slots, other, at_y, at_x],
            shard_got.at[piece, me],
            shard_send.at[piece, j],
            shard_recv.at[piece, me],
            (dp, other),
        )

    def shard_arrival(piece, j):
        other = (me + 1 + j) % groups
        return remote(
            grad.at[piece % slots, other, at_y, at_x],
            shard_got.at[piece, other],
            shard_send.at[piece, j],
            shard_recv.at[piece, other],
            (dp, other),
        )

    def block_copy(piece, j):
        return remote(
            partial.at[piece],
            block_got.at[piece, block],
            block_send.at[piece, j],
            block_recv.at[piece, block],
            far[j],
        )

    def block_arrival(piece, j):
        other = (block + 1 + j) % blocks
        return remote(
            partial.at[piece],
            block_got.at[piece, other],
            block_send.at[piece, j],
            block_recv.at[piece, other],
            far[j],
        )

    def place(piece, owner):
        return out.at[
            piece,
            pl.ds(pl.multiple_of(owner % 8 // 2 * part, 16), part),
            pl.ds(pl.multiple_of(core * width, 128), width),
        ]

    def spread(piece, src, owner, recv_sem, device):
        return remote(src, place(piece, owner), send_sem.at[piece], recv_sem, (device, me))

    def forward(piece, owner, recv_sem, device):
        return spread(piece, place(piece, owner), owner, recv_sem, device)

    diagonal = neighbours(along_x)[2]

    def produce(piece):
        slot = piece % slots
        hold = piece % 2

        def shard_body(shard, carry):
            columns = pl.ds(pl.multiple_of(shard * rows, 128), rows)
            value = dot_leading(left_hold[hold, 0, :, columns], right_hold[hold, 0])
            value = value + dot_leading(left_hold[hold, 1, :, columns], right_hold[hold, 1])
            grad[slot, shard] = value.astype(grad.dtype).reshape(2, 2, part, width)
            return carry

        lax.fori_loop(0, groups, shard_body, 0)

        @pl.when(jnp.logical_and(piece == 5, core == 1))
        def _():
            for shard in range(groups):
                grad[slot, shard, 0, :, :, pl.ds(rel_at, rel_grad.shape[3])] = rel_grad[shard]

    def add(piece_slot, ref, columns, *index):
        ahead = grad[(piece_slot,) + index + (slice(None), columns)]
        return ahead.astype(jnp.float32) + ref.astype(jnp.float32)

    def body(n, carry):
        @pl.when(n < count)
        def _():
            @pl.when(n >= slots)
            def _():
                old = n - slots
                for copy in one(old) + two(old):
                    copy.wait_send()
                for j in range(others):
                    shard_copy(old, j).wait_send()

            for piece in range(count):

                @pl.when(n == piece)
                def _():
                    for copy in loads(piece, piece % 2):
                        copy.wait()
                    if piece + 1 < count:
                        for copy in loads(piece + 1, (piece + 1) % 2):
                            copy.start()

            produce(n)
            for copy in one(n):
                copy.start()

        @pl.when(jnp.logical_and(n >= 1, n < count + 1))
        def _():
            piece = n - 1
            slot = piece % slots
            for copy in one(piece):
                copy.wait_recv()

            def shard_body(shard, carry):
                for other in range(2):
                    value = add(slot, x_one[piece, shard, other], first, shard, other, at_x)
                    grad[slot, shard, other, at_x, :, first] = value.astype(grad.dtype)
                    value = add(slot, y_one[piece, shard, other], last, shard, at_y, other)
                    grad[slot, shard, at_y, other, :, last] = value.astype(grad.dtype)
                return carry

            lax.fori_loop(0, groups, shard_body, 0)
            for copy in two(piece):
                copy.start()

        @pl.when(jnp.logical_and(n >= 2, n < count + 2))
        def _():
            piece = n - 2
            slot = piece % slots
            for copy in two(piece):
                copy.wait_recv()

            def shard_body(shard, carry):
                value = add(slot, y_two[piece, shard], first, shard, at_y, at_x)
                grad[slot, shard, at_y, at_x, :, first] = value.astype(grad.dtype)
                value = add(slot, x_two[piece, shard], last, shard, at_y, at_x)
                grad[slot, shard, at_y, at_x, :, last] = value.astype(grad.dtype)
                return carry

            lax.fori_loop(0, groups, shard_body, 0)
            for j in range(others):
                shard_copy(piece, j).start()

        @pl.when(jnp.logical_and(n >= 3, n < count + 3))
        def _():
            piece = n - 3
            value = grad[piece % slots, me, at_y, at_x].astype(jnp.float32)
            for j in range(others):
                shard_arrival(piece, j).wait_recv()
                value = value + shard_got[piece, (me + 1 + j) % groups].astype(jnp.float32)
            if blocks > 1:
                partial[piece] = value.astype(partial.dtype)
                block_got[piece, block] = value.astype(partial.dtype)
                for j in range(blocks - 1):
                    block_copy(piece, j).start()
                for j in range(blocks - 1):
                    block_copy(piece, j).wait_send()
                    block_arrival(piece, j).wait_recv()
                value = block_got[piece, 0].astype(jnp.float32)
                for other in range(1, blocks):
                    value = value + block_got[piece, other].astype(jnp.float32)
            done[piece] = value.astype(done.dtype)
            pltpu.make_async_copy(done.at[piece], place(piece, dp), write_sem.at[piece]).start()
            spread(piece, done.at[piece], dp, ax.at[piece], along_x).start()
            spread(piece, done.at[piece], dp, ay.at[piece], along_y).start()
            spread(piece, done.at[piece], dp, sib_sem.at[piece], sib).start()

        @pl.when(jnp.logical_and(n >= 4, n < count + 4))
        def _():
            piece = n - 4
            route = piece % 2
            forward(piece, along_x, ax.at[piece], dp).wait_recv()
            forward(piece, along_y, ay.at[piece], dp).wait_recv()
            owner = route * along_x + (1 - route) * along_y
            target = route * along_y + (1 - route) * along_x
            forward(piece, owner, ad.at[piece], target).start()
            forward(piece, along_x, sib_sem.at[piece], sib).start()
            forward(piece, along_y, sib_sem.at[piece], sib).start()

        @pl.when(n >= 5)
        def _():
            piece = n - 5
            forward(piece, diagonal, ad.at[piece], dp).wait_recv()
            forward(piece, diagonal, sib_sem.at[piece], sib).start()

        for step in range(len(summing)):

            @pl.when(n == step)
            def _():
                summing[step]()

        return carry

    lax.fori_loop(0, count + 5, body, 0)

    def drain(piece, carry):
        @pl.when(piece >= count - slots)
        def _():
            for copy in one(piece) + two(piece):
                copy.wait_send()
            for j in range(others):
                shard_copy(piece, j).wait_send()

        pltpu.make_async_copy(done.at[piece], place(piece, dp), write_sem.at[piece]).wait()
        got = out.at[piece, :, pl.ds(0, width)]
        remote(got, got, send_sem.at[piece], sib_sem.at[piece], (sib, me)).wait_recv()
        sent = out.at[piece, pl.ds(0, 7 * part // 2), :]
        remote(sent, sent, send_sem.at[piece], sib_sem.at[piece], (sib, me)).wait_send()
        return carry

    lax.fori_loop(0, count, drain, 0)


def reduce(
    groups,
    blocks,
    rel_at,
    lefts,
    lefts_sib,
    conv_right,
    conv_right_sib,
    rights,
    rights_sib,
    rel_grad,
    vector,
):
    bins, columns = lefts[0].shape
    width = columns // 2
    rows = columns // groups
    part = rows // 4
    dtype = lefts[0].dtype
    taps = conv_right.shape[0]
    count = taps + len(rights)
    slots = 5
    kept = pl.BlockSpec(memory_space=pl.ANY)
    inside = pl.BlockSpec(memory_space=pltpu.VMEM)
    each = pltpu.SemaphoreType.DMA((count,))
    return pl.pallas_call(
        functools.partial(reduce_kernel, groups, blocks, rel_at),
        out_shape=(
            jax.ShapeDtypeStruct((count, rows, columns), dtype),
            jax.ShapeDtypeStruct(vector.shape, jnp.float32),
        ),
        in_specs=[kept] * 28 + [inside] * 2,
        out_specs=[kept, inside],
        scratch_shapes=[
            pltpu.VMEM((2, 2, bins, columns), dtype),
            pltpu.VMEM((2, 2, bins, width), dtype),
            pltpu.VMEM((slots, groups, 2, 2, part, width), dtype),
            pltpu.VMEM((count, groups, 2, part, width // 2), dtype),
            pltpu.VMEM((count, groups, 2, part, width // 2), dtype),
            pltpu.VMEM((count, groups, part, width // 2), dtype),
            pltpu.VMEM((count, groups, part, width // 2), dtype),
            pltpu.VMEM((count, groups, part, width), dtype),
            pltpu.VMEM((count if blocks > 1 else 1, blocks, part, width), dtype),
            pltpu.VMEM((count if blocks > 1 else 1, part, width), dtype),
            pltpu.VMEM((count, part, width), dtype),
            pltpu.SemaphoreType.DMA((2, 4)),
            *([each] * 8),
            pltpu.SemaphoreType.DMA((count, groups)),
            pltpu.SemaphoreType.DMA((count, groups)),
            pltpu.SemaphoreType.DMA((count, blocks)),
            pltpu.SemaphoreType.DMA((count, blocks)),
            *([each] * 6),
            *sum_scratch(groups, blocks, vector.shape),
        ],
        compiler_params=pltpu.CompilerParams(
            collective_id=1, has_side_effects=True, vmem_limit_bytes=60 << 20
        ),
        name="reduce",
    )(*lefts, *lefts_sib, conv_right, conv_right_sib, *rights, *rights_sib, rel_grad, vector)


EPSILON = 1e-05


def position_table(length, features):
    basis_count = features // 6
    offsets = jnp.arange(2 * length - 1, dtype=jnp.float32) - (length - 1)
    distance = jnp.abs(offsets)[:, None]
    max_range = math.log(length) / math.log(2.0)
    half_life = 2.0 ** jnp.linspace(3.0, max_range, basis_count, dtype=jnp.float32)
    decaying = jnp.exp(-math.log(2.0) / half_life[None, :] * distance)
    widths = 2.0 ** jnp.arange(1, basis_count + 1, dtype=jnp.float32) - 1.0
    central = (widths[None, :] > distance).astype(jnp.float32)
    stddev = length / (2.0 * basis_count)
    centres = jnp.linspace(length / basis_count, length, basis_count, dtype=jnp.float32)
    shape_par = (centres / stddev) ** 2
    rate_par = centres / stddev**2
    safe_dist = jnp.maximum(distance, 1.0)
    log_prob = (shape_par - 1.0) * jnp.log(safe_dist) - rate_par * safe_dist
    log_prob = log_prob - jnp.max(log_prob, axis=0, keepdims=True)
    gamma_feat = jnp.where(distance > 0.5, jnp.exp(log_prob), 0.0)
    symmetric = jnp.concatenate([decaying, central, gamma_feat], 1)
    sign_row = jnp.sign(offsets)[:, None]
    return jnp.concatenate([symmetric, sign_row * symmetric], 1)


def relative_shift(scores):
    row_count = scores.shape[-2]
    span_width = scores.shape[-1]
    leading = scores.shape[:-2]
    padded = jnp.pad(scores, [(0, 0)] * (scores.ndim - 1) + [(1, 0)])
    folded = padded.reshape(leading + (span_width + 1, row_count))[..., 1:, :]
    return folded.reshape(leading + (row_count, span_width))[..., :row_count]


def normalize(values):
    centred = values - jnp.mean(values, -1, keepdims=True)
    inverse = lax.rsqrt(jnp.mean(centred * centred, -1, keepdims=True) + EPSILON)
    return (centred * inverse, inverse)


def norm_back(grad_std, standard, inverse):
    return inverse * (
        grad_std
        - jnp.mean(grad_std, -1, keepdims=True)
        - standard * jnp.mean(grad_std * standard, -1, keepdims=True)
    )


def dot_leading(left_side, right_side):
    return lax.dot_general(
        left_side, right_side, (((0,), (0,)), ((), ())), preferred_element_type=jnp.float32
    )


def dot_trailing(left_side, right_side):
    return lax.dot_general(
        left_side, right_side, (((1,), (1,)), ((), ())), preferred_element_type=jnp.float32
    )


def attention_scores(content_query, key_heads, position_query, position_keys):
    content = jnp.einsum(
        "ihk,jhk->hij", content_query, key_heads, preferred_element_type=jnp.float32
    )
    relative = jnp.einsum(
        "ihk,mhk->him", position_query, position_keys, preferred_element_type=jnp.float32
    )
    return content + relative_shift(relative)


def on_device(
    tokens,
    conv_weight,
    query_weight,
    key_weight,
    value_weight,
    out_weight,
    rel_weight,
    up_weight,
    down_weight,
    gains,
    biases,
    up_bias,
    rel_bias,
    target_table,
    clip_levels,
    window_ids,
    clip_index,
):
    groups = lax.axis_size("fsdp")
    blocks = lax.axis_size("dp") // 8
    core = lax.axis_index("dp") % 2
    pairs = [(i, i + 1 - 2 * (i % 2)) for i in range(lax.axis_size("dp"))]
    tap_count, piece_rows, model_width = conv_weight.shape
    half_taps = tap_count // 2
    half_width = model_width // 2
    key_width = query_weight.shape[1]
    rel_rows, rel_columns = rel_weight.shape
    inputs = tokens[0].astype(jnp.float32)
    length = inputs.shape[0]
    token_total = length * lax.axis_size("dp") * lax.axis_size("fsdp")

    def exchange(array):
        return lax.ppermute(array, "dp", pairs)

    def own_half(array):
        return lax.dynamic_slice_in_dim(array, core * half_width, half_width, 1)

    def sib_half(array):
        return exchange(
            lax.dynamic_slice_in_dim(array, (1 - core) * half_width, half_width, 1)
        )

    small_parts = [gains, biases, up_bias, rel_bias]
    small = jnp.concatenate([part.reshape(-1) for part in small_parts])
    small = jnp.pad(small, (0, -small.shape[0] % 1024)).reshape(-1, 128)
    stats = jnp.concatenate([jnp.sum(inputs, 0), jnp.sum(inputs * inputs, 0)]).reshape(-1, 128)
    (
        conv_full,
        mixed_full,
        value_full,
        out_full,
        up_first,
        up_last,
        down_first,
        down_last,
        rel_full,
        small_full,
        stats,
    ) = gather(
        groups,
        blocks,
        [
            conv_weight,
            query_weight,
            key_weight,
            value_weight,
            out_weight,
            up_weight,
            down_weight,
            rel_weight,
        ],
        small,
        stats,
    )
    conv_full = conv_full.reshape(tap_count, model_width, model_width)
    mixed_full = mixed_full.reshape(model_width, -1)
    value_full = value_full.reshape(model_width, -1)
    out_full = out_full.reshape(model_width, -1)
    up_full = [up_first.reshape(model_width, -1), up_last.reshape(model_width, -1)]
    down_full = [down_first.reshape(model_width, -1), down_last.reshape(model_width, -1)]
    rel_full = jnp.concatenate([rel_full[shard] for shard in range(groups)], 1)
    flat = small_full.reshape(groups, -1)
    taken = 0
    unpacked = []
    for part in small_parts:
        chosen = flat[:, taken : taken + part.size].reshape((groups,) + part.shape)
        unpacked.append(chosen)
        taken += part.size
    gain_rows = jnp.moveaxis(unpacked[0], 0, 1).reshape(gains.shape[0], -1)
    bias_rows = jnp.moveaxis(unpacked[1], 0, 1).reshape(biases.shape[0], -1)
    up_offset = jnp.moveaxis(unpacked[2].reshape(groups, 2, piece_rows), 0, 1).reshape(2, -1)
    rel_offset = jnp.moveaxis(unpacked[3], 0, 1).reshape(2, -1)
    batch_sums = stats.reshape(2, -1)
    centre = batch_sums[0] / token_total
    variance = batch_sums[1] / token_total - centre * centre
    inverse = lax.rsqrt(variance + EPSILON)
    standard = (inputs - centre) * inverse
    normed = standard * gain_rows[0] + bias_rows[0]
    activated = jax.nn.gelu(normed).astype(jnp.bfloat16)
    padded = jnp.pad(activated, ((half_taps, half_taps), (0, 0)))
    stacked = jnp.concatenate([padded[tap : tap + length] for tap in range(tap_count)], 1)
    conv_out = jnp.dot(
        stacked, conv_full.reshape(-1, model_width), preferred_element_type=jnp.float32
    )
    after_conv = inputs + conv_out + bias_rows[1]
    standard_one, inverse_one = normalize(after_conv)
    normed_one = (standard_one * gain_rows[1] + bias_rows[2]).astype(jnp.bfloat16)
    mixed_raw = jnp.dot(normed_one, mixed_full, preferred_element_type=jnp.float32)
    query_raw = mixed_raw[:, :key_width]
    key_scale = KEY ** (-0.5)
    content_query = (
        (query_raw * key_scale + rel_offset[0]).astype(jnp.bfloat16).reshape(length, HEADS, -1)
    )
    position_query = (
        (query_raw * key_scale + rel_offset[1]).astype(jnp.bfloat16).reshape(length, HEADS, -1)
    )
    key_heads = mixed_raw[:, key_width:].astype(jnp.bfloat16).reshape(length, HEADS, -1)
    value_heads = (
        jnp.dot(normed_one, value_full, preferred_element_type=jnp.float32)
        .astype(jnp.bfloat16)
        .reshape(length, HEADS, -1)
    )
    table = position_table(length, rel_full.shape[0]).astype(jnp.bfloat16)
    position_keys = (
        jnp.dot(table, rel_full, preferred_element_type=jnp.float32)
        .astype(jnp.bfloat16)
        .reshape(table.shape[0], HEADS, -1)
    )
    scores = attention_scores(content_query, key_heads, position_query, position_keys)
    row_peak = jnp.max(scores, -1, keepdims=True)
    normalizer = row_peak + jnp.log(jnp.sum(jnp.exp(scores - row_peak), -1, keepdims=True))
    attention_probs = jnp.exp(scores - normalizer)
    attended = jnp.einsum(
        "hij,jhv->ihv",
        attention_probs.astype(jnp.bfloat16),
        value_heads,
        preferred_element_type=jnp.float32,
    )
    attended = attended.reshape(length, model_width).astype(jnp.bfloat16)
    after_attention = (
        after_conv + jnp.dot(attended, out_full, preferred_element_type=jnp.float32) + bias_rows[3]
    )
    standard_two, inverse_two = normalize(after_attention)
    normed_two = (standard_two * gain_rows[2] + bias_rows[4]).astype(jnp.bfloat16)
    hidden_pre = [
        jnp.dot(normed_two, up_full[half], preferred_element_type=jnp.float32) + up_offset[half]
        for half in range(2)
    ]
    hidden = [jax.nn.gelu(half).astype(jnp.bfloat16) for half in hidden_pre]
    outputs = (
        after_attention
        + jnp.dot(hidden[0], down_full[0], preferred_element_type=jnp.float32)
        + jnp.dot(hidden[1], down_full[1], preferred_element_type=jnp.float32)
        + bias_rows[5]
    )
    target_row = lax.dynamic_index_in_dim(target_table, window_ids[0], 0, keepdims=False)
    levels = jnp.arange(clip_levels.shape[0], dtype=jnp.int32)
    selector = (clip_index[0][:, None] == levels[None, :]).astype(jnp.float32)
    limits = jnp.sum(selector * clip_levels[None, :], 1)[:, None]
    cotangent = jnp.clip(outputs - target_row, -limits, limits).astype(jnp.bfloat16)
    cot_value = cotangent.astype(jnp.float32)
    grad_down_bias = jnp.sum(cot_value, 0)
    pre_grad = []
    for half in range(2):
        hidden_grad = dot_trailing(cotangent, down_full[half])
        gelu_pull = jax.vjp(jax.nn.gelu, hidden_pre[half])[1]
        pre_grad.append(gelu_pull(hidden_grad)[0].astype(jnp.bfloat16))
    grad_up_bias = jnp.stack([jnp.sum(half.astype(jnp.float32), 0) for half in pre_grad])
    normed_two_grad = dot_trailing(pre_grad[0], up_full[0]) + dot_trailing(
        pre_grad[1], up_full[1]
    )
    grad_gain_two = jnp.sum(normed_two_grad * standard_two, 0)
    grad_bias_two = jnp.sum(normed_two_grad, 0)
    attention_grad = cot_value + norm_back(
        normed_two_grad * gain_rows[2], standard_two, inverse_two
    )
    branch_grad = attention_grad.astype(jnp.bfloat16)
    grad_out_bias = jnp.sum(branch_grad.astype(jnp.float32), 0)
    attended_grad = (
        dot_trailing(branch_grad, out_full).astype(jnp.bfloat16).reshape(length, HEADS, -1)
    )
    scores = attention_scores(content_query, key_heads, position_query, position_keys)
    attention_probs = jnp.exp(scores - normalizer)
    value_grad = jnp.einsum(
        "hij,ihv->jhv",
        attention_probs.astype(jnp.bfloat16),
        attended_grad,
        preferred_element_type=jnp.float32,
    )
    value_grad = value_grad.reshape(length, model_width).astype(jnp.bfloat16)
    prob_grad = jnp.einsum(
        "ihv,jhv->hij", attended_grad, value_heads, preferred_element_type=jnp.float32
    )
    row_dot = jnp.sum(attention_probs * prob_grad, -1, keepdims=True)
    score_grad = (attention_probs * (prob_grad - row_dot)).astype(jnp.bfloat16)
    content_grad = jnp.einsum(
        "hij,jhk->ihk", score_grad, key_heads, preferred_element_type=jnp.float32
    )
    key_grad = jnp.einsum(
        "hij,ihk->jhk", score_grad, content_query, preferred_element_type=jnp.float32
    )
    key_grad = key_grad.reshape(length, -1).astype(jnp.bfloat16)
    band_zeros = jnp.zeros((HEADS, length, position_keys.shape[0]), jnp.float32)
    shift_pull = jax.vjp(relative_shift, band_zeros)[1]
    band_grad = shift_pull(score_grad.astype(jnp.float32))[0].astype(jnp.bfloat16)
    position_grad = jnp.einsum(
        "him,mhk->ihk", band_grad, position_keys, preferred_element_type=jnp.float32
    )
    table_grad = jnp.einsum(
        "him,ihk->mhk", band_grad, position_query, preferred_element_type=jnp.float32
    )
    table_grad = table_grad.reshape(table.shape[0], -1).astype(jnp.bfloat16)
    grad_rel_bias = jnp.stack(
        [jnp.sum(content_grad, 0).reshape(-1), jnp.sum(position_grad, 0).reshape(-1)]
    )
    query_grad = (
        ((content_grad + position_grad) * key_scale).reshape(length, -1).astype(jnp.bfloat16)
    )
    mixed_grad = jnp.concatenate([query_grad, key_grad], 1)
    normed_one_grad = (
        dot_trailing(mixed_grad, mixed_full)
        + dot_trailing(value_grad, value_full)
    )
    grad_gain_one = jnp.sum(normed_one_grad * standard_one, 0)
    grad_bias_one = jnp.sum(normed_one_grad, 0)
    conv_side_grad = attention_grad + norm_back(
        normed_one_grad * gain_rows[1], standard_one, inverse_one
    )
    conv_grad = conv_side_grad.astype(jnp.bfloat16)
    grad_conv_bias = jnp.sum(conv_grad.astype(jnp.float32), 0)
    padded = jnp.pad(conv_grad, ((half_taps, half_taps), (0, 0)))
    activated_grad = 0.0
    for tap in range(tap_count):
        moved = padded[tap_count - 1 - tap : tap_count - 1 - tap + length]
        activated_grad = activated_grad + dot_trailing(moved, conv_full[tap])
    act_pull = jax.vjp(jax.nn.gelu, normed)[1]
    normed_grad = act_pull(activated_grad)[0]
    sum_parts = [
        jnp.sum(normed_grad * standard, 0),
        grad_gain_one,
        grad_gain_two,
        jnp.sum(normed_grad, 0),
        grad_conv_bias,
        grad_bias_one,
        grad_out_bias,
        grad_bias_two,
        grad_down_bias,
        grad_up_bias[0],
        grad_up_bias[1],
        grad_rel_bias.reshape(-1),
    ]
    sums = jnp.concatenate(sum_parts)
    sums = jnp.pad(sums, (0, -sums.shape[0] % 1024)).reshape(-1, 128)
    grad_rel = dot_leading(table, table_grad).astype(jnp.bfloat16)
    grad_rel = grad_rel.astype(jnp.float32) + exchange(grad_rel).astype(jnp.float32)
    grad_rel = jnp.moveaxis(grad_rel.reshape(rel_rows, groups, rel_columns), 0, 1)
    grad_rel = grad_rel.reshape(groups, 2, rel_rows // 2, rel_columns).astype(jnp.bfloat16)
    mixed_wide = jnp.pad(mixed_grad, ((0, 0), (0, model_width - 2 * key_width)))
    lefts = [activated, normed_one, attended, normed_two, hidden[0], hidden[1]]
    rights = [mixed_wide, value_grad, branch_grad, pre_grad[0], pre_grad[1], cotangent]
    lefts_sib = [exchange(left) for left in lefts]
    rights_own = [own_half(right) for right in rights]
    rights_sib = [sib_half(right) for right in rights]

    def shifted(array):
        padded = jnp.pad(array, ((half_taps, half_taps), (0, 0)))
        return jnp.stack([padded[tap : tap + length] for tap in reversed(range(tap_count))])

    pieces, sums = reduce(
        groups,
        blocks,
        2 * key_width - half_width,
        lefts,
        lefts_sib,
        shifted(own_half(conv_grad)),
        shifted(sib_half(conv_grad)),
        rights_own + rights_own[5:],
        rights_sib + rights_sib[5:],
        grad_rel,
        sums,
    )
    flat = sums.reshape(-1)
    bn_sums = flat[: 4 * model_width].reshape(4, model_width)
    input_grad = conv_side_grad + inverse * (
        normed_grad * gain_rows[0]
        - gain_rows[0] * (bn_sums[3] + standard * bn_sums[0]) / token_total
    )
    shard = lax.axis_index("fsdp")
    by_shard = flat[: 11 * model_width].reshape(11, groups, -1)
    by_shard = lax.dynamic_index_in_dim(by_shard, shard, 1, keepdims=False)
    rel_sums = flat[11 * model_width : 11 * model_width + 2 * key_width]
    rel_sums = rel_sums.reshape(2, groups, -1)
    rel_sums = lax.dynamic_index_in_dim(rel_sums, shard, 1, keepdims=False)
    up_grad = jnp.concatenate(
        [
            pieces[8 + half, :, index * piece_rows : (index + 1) * piece_rows]
            for index in range(groups)
            for half in range(2)
        ],
        1,
    )
    mixed_sum = pieces[5].astype(jnp.float32)
    rel_at = 2 * key_width
    return (
        outputs.astype(jnp.bfloat16)[None],
        input_grad.astype(jnp.bfloat16)[None],
        pieces[:5].astype(jnp.float32),
        mixed_sum[:, :key_width],
        mixed_sum[:, key_width:rel_at],
        pieces[6].astype(jnp.float32),
        pieces[7].astype(jnp.float32),
        mixed_sum[:rel_rows, rel_at : rel_at + rel_columns],
        up_grad.astype(jnp.float32),
        pieces[10:12].reshape(2 * piece_rows, -1).astype(jnp.float32),
        by_shard[:3],
        by_shard[3:9],
        by_shard[9:11].reshape(-1),
        rel_sums,
    )


def solution(mesh):
    placed = (
        P(("dp", "fsdp"), None, None),
        P(None, "fsdp", None),
        P("fsdp", None),
        P("fsdp", None),
        P("fsdp", None),
        P("fsdp", None),
        P(None, "fsdp"),
        P("fsdp", None),
        P("fsdp", None),
        P(None, "fsdp"),
        P(None, "fsdp"),
        P("fsdp"),
        P(None, "fsdp"),
        P(),
        P(),
        P(("dp", "fsdp")),
        P(("dp", "fsdp"), None),
    )
    return jax.shard_map(
        on_device,
        mesh=mesh,
        in_specs=placed,
        out_specs=(
            P(("dp", "fsdp"), None, None),
            P(("dp", "fsdp"), None, None),
            P(None, "fsdp", None),
            P("fsdp", None),
            P("fsdp", None),
            P("fsdp", None),
            P("fsdp", None),
            P(None, "fsdp"),
            P("fsdp", None),
            P("fsdp", None),
            P(None, "fsdp"),
            P(None, "fsdp"),
            P("fsdp"),
            P(None, "fsdp"),
        ),
        check_vma=False,
    )
```

time: 1910 us -> 1000 us (0.52)
  waiting for transfers between devices: 1010 us -> 0.04 us
  Pallas kernels: 199 us -> 507 us
  blocking collectives: 116 us -> 0 us
  matrix products: 193 us -> 153 us
  local copies, waits for them, and re-layouts: 293 us -> 260 us
    reduce_scatter x1 -> x0, waiting for transfers between devices: 920 us -> none  [on_device(): lax.psum_scatter(grad_pieces, 'fsdp', scatter_dimension=1, tiled=True)]
    pallas_call x1 -> x2, Pallas kernels: 199 us -> 507 us  [the longest x1 308 us: reduce(): pl.pallas_call(functools.partial(reduce_kernel, groups, blocks, rel_at),...]
    psum x3 -> x0, blocking collectives: 105 us -> none  [the longest x1 43.5 us: on_device(): lax.psum((jnp.sum(normed_grad * standard, 0), jnp.sum(normed_grad, 0)), (...]
    psum x1 -> x0, waiting for transfers between devices: 91 us -> none  [on_device(): grad_pieces = lax.psum(grad_pieces, 'dp').astype(jnp.float32)]
    dot_general x13 -> x1, matrix products: 50.6 us -> 0.51 us  [dot_leading(): lax.dot_general(left_side, right_side, (((0,), (0,)), ((), ())), preferre...]
    unnamed x264 -> x308, local copies, waits for them, and re-layouts: 41.5 us -> 80 us
    slice x4 -> x11, local copies, waits for them, and re-layouts: 54.3 us -> 19.7 us  [the longest x1 17.4 us: on_device(): activated_grad = activated_grad + dot_trailing(moved, conv_full[tap])]
    scatter-add x5 -> x0, local copies, waits for them, and re-layouts: 34.2 us -> none  [on_device(): padded_grad.at[tap_index:tap_index + length].add(stacked_grad[:, tap_index])]
  transfers between devices with their start and end apart: 5 -> 14, of which waited for: 2 -> 0; matrix products, arithmetic and copies ran while one was open for 5% -> 25% of each run, Pallas kernels for 0% -> 0%
where the time goes in v2:
time: 1000 us; the launch traced here: 990 us
  Pallas kernels  507 us (51%)
  local copies, waits for them, and re-layouts  260 us (26%)
  matrix products  153 us (15%)
  other arithmetic  62.3 us (6%)
    pallas_call x1, Pallas kernels, reduce(): pl.pallas_call(functools.partial(reduce_kernel, groups, blocks, rel_at),...  308 us
    pallas_call x1, Pallas kernels, gather(): pl.pallas_call(functools.partial(gather_kernel, groups, blocks), out_shap...  198 us
    unnamed x308, local copies, waits for them, and re-layouts  80 us
    dot_general x12, matrix products, dot_trailing(): lax.dot_general(left_side, right_side, (((1,), (1,)), ((), ())), preferre...  50.5 us
    reshape x2, local copies, waits for them, and re-layouts, relative_shift(): return folded.reshape(leading + (row_count, span_width))[..., :row_count]  41 us
    reshape x2, local copies, waits for them, and re-layouts, relative_shift(): folded = padded.reshape(leading + (span_width + 1, row_count))[..., 1:, :]  31.2 us
  transfers between devices with their start and end apart: 14, of which 0 were waited for; matrix products, arithmetic and copies ran while one was open for 25% of the time, Pallas kernels for 0%

profile of v2, /device:TPU:0, one launch (start us, length us, event | category | flops | bytes accessed | tf_op | source)
XLA Modules:
  0.0 989.8 jit_solution(11269540477962041500)
XLA Ops:
  0.7 2.4 convert_reduce_fusion.1
  3.1 2.3 fusion.11
  14.0 198.2 %gather.1 = (bf16[5,4,384,1536]{3,2,1,0:T(8,128)(2,1)}, bf16[4,384,1024]{2,1,0:T(8,128)(2,1)S(1)}, bf16[4,384,1536]{2,1,0:T(8,128)(2,1)S(1)}, bf16[4,384,1536]{2...) custom-call(bf16[5,384,1536]{2,1,0:T(8,128)(2,1)} %refs_0_.1, ...), custom_call_target="tpu_custom_call" | custom-call | tf_op jit(solution)/shard_map/gather/pallas_call | solution.py:342
  212.2 2.2 copy-done.2
  215.1 2.2 copy-done.12
  217.3 2.1 copy-done.13
  219.4 2.2 copy-done.14
  229.5 2.9 fusion.22.refs_0_
  236.6 3.2 copy-done.64
  239.8 18.9 %fusion.108 = (f32[512]{0:T(512)S(1)}, f32[512,1536]{1,0:T(8,128)S(1)}) fusion(f32[1536]{0:T(1024)S(1)} %add.329, bf16[512,7680]{1,0:T(8,128)(2,1)} %copy-done.64, bf16[7680,1536]{1,0:T(8,128)(2,1)} %bitcast.304, bf16[1,512,1536]{2,1,0:T(8,128)(2,1)S(1)} %copy-done.25), kind=kOutput, calls=%fused_computation.274 | convolution fusion | flops 12082741248 | bytes 36184064 | tf_op jit(solution)/shard_map/dot_general | solution.py:907
  264.8 3.6 add_convert_fusion.1.refs_1_
  268.4 3.2 fusion.111
  273.6 2.4 fusion.112
  276.0 7.5 pad.46
  283.5 18.1 %reshape.394 = f32[8,1024,512]{2,1,0:T(8,128)} reshape(f32[8,512,1024]{2,1,0:T(8,128)} %pad.46) | data formatting | bytes 33554432 | tf_op jit(solution)/shard_map/reshape | solution.py:765
  301.6 12.0 %slice.346 = f32[8,1023,512]{2,1,0:T(8,128)} slice(f32[8,1024,512]{2,1,0:T(8,128)} %reshape.394), slice={[0:8], [1:1024], [0:512]} | slice | bytes 33521664 | tf_op jit(solution)/shard_map/slice | solution.py:765
  313.6 19.2 %reshape.395 = f32[8,512,1023]{2,1,0:T(8,128)} reshape(f32[8,1023,512]{2,1,0:T(8,128)} %slice.346) | data formatting | bytes 33521664 | tf_op jit(solution)/shard_map/reshape | solution.py:766
  332.8 7.8 slice.347
  340.6 9.3 copy.93
  350.4 4.9 fusion.109
  356.6 2.2 copy-done.18
  358.8 4.0 convolution_convert_fusion.1
  364.8 5.1 convolution_convert_fusion.3
  370.0 5.6 fusion.110
  383.8 2.4 add_convert_fusion.refs_3_
  386.3 8.1 multiply_convert_fusion.1
  400.0 8.2 multiply_convert_fusion.2
  408.1 7.0 convolution_add_fusion.8
  415.2 8.6 convert_reduce_fusion
  423.8 7.8 convert_reduce_fusion.2
  432.1 5.0 convert_reduce_fusion.3
  437.2 2.6 fusion.113
  439.9 3.8 multiply_reduce_fusion.1
  443.8 3.3 convert_reduce_fusion.4
  448.3 3.7 convolution_convert_fusion
  453.9 4.8 multiply_reduce_fusion
  459.7 3.8 multiply_convert_fusion
  463.6 6.5 copy.100
  470.0 6.5 pad.47.clone
  476.5 21.9 %reshape.403 = bf16[8,1023,512]{2,1,0:T(8,128)(2,1)} reshape(bf16[8,512,1023]{2,1,0:T(8,128)(2,1)} %pad.47.clone) | data formatting | bytes 16760832 | tf_op jit(solution)/shard_map/transpose(jvp())/reshape | solution.py:766
  498.4 8.7 pad.48
  507.1 13.1 %reshape.404 = bf16[8,512,1024]{2,1,0:T(8,128)(2,1)} reshape(bf16[8,1024,512]{2,1,0:T(8,128)(2,1)} %pad.48) | data formatting | bytes 16777216 | tf_op jit(solution)/shard_map/transpose(jvp())/reshape | solution.py:765
  520.3 6.3 fusion.56
  527.4 3.9 fusion.59
  532.7 4.0 fusion.105
  542.0 5.2 convolution_convert_fusion.2
  549.2 4.6 multiply_reduce_fusion.2
  553.8 3.1 convert_reduce_fusion.5
  560.9 17.4 %fusion.103 = (bf16[1,4,384,1536]{3,2,1,0:T(8,128)(2,1)}, bf16[1,4,384,1536]{3,2,1,0:T(8,128)(2,1)}, bf16[1,4,384,1536]{3,2,1,0:T(8,128)(2,1)}, bf16[1,4,384,1536]{3,2,1,0:T(8,128)(2,1)}, bf16[1,4,384,1536]{3,2,1,0:T(8,128)(2,1)}) fusion(bf16[5,4,384,1536]{3,2,1,0:T(8,128)(2,1)} %get-tuple-element.29), kind=kLoop, calls=%fused_computation.269 | loop fusion | bytes 47185920 | tf_op jit(solution)/shard_map/slice | solution.py:1040
  578.2 4.7 fusion.53
  583.0 2.6 convolution_add_fusion.3
  585.7 2.7 convolution_add_fusion.2
  588.5 2.7 convolution_add_fusion.1
  591.4 8.3 fusion.100
  619.3 2.5 constant_dynamic-slice_fusion.4
  633.9 2.3 copy.94.refs_15_
  636.1 2.1 bitcast_dynamic-update-slice_fusion.7
  638.3 2.2 bitcast_dynamic-update-slice_fusion.6
  650.7 308.4 %reduce.20 = (bf16[12,384,1536]{2,1,0:T(8,128)(2,1)}, f32[144,128]{1,0:T(8,128)}) custom-call(bf16[512,1536]{1,0:T(8,128)(2,1)} %copy-done.20, bf16[512,1536]{1,0:T(8,128)(2,1)} %add_convert_fusion.1.refs_1_, bf16[512,1536]{1,0:T(8,128)(2,1)} %copy.87.refs_2_, bf16[512,1536]{1,0:T(8,128)(2,1)} %add_convert_fusion.refs_3_, ...), custom_call_target="tpu_custom_call" | custom-call | tf_op jit(solution)/shard_map/reduce/pallas_call | solution.py:699
  960.1 9.9 %slice_convert_fusion = f32[5,384,1536]{2,1,0:T(8,128)} fusion(bf16[12,384,1536]{2,1,0:T(8,128)(2,1)} %get-tuple-element.39), kind=kLoop, calls=%fused_computation.9 | loop fusion | flops 2949120 | bytes 17694720 | tf_op jit(solution)/shard_map/convert_element_type | solution.py:1112
  970.0 2.9 bitcast_convert_fusion.1
  976.2 2.8 convert_element_type.251
  978.9 3.0 bitcast_convert_fusion
  984.4 5.2 fusion.55
  (438 shorter events, 111.7 us)
Async XLA Ops:
  0.6 414.5 %copy-start = (f32[64,1536]{1,0:T(8,128)S(1)}, f32[64,1536]{1,0:T(8,128)}, u32[]{:S(2)}) copy-start(f32[64,1536]{1,0:T(8,128)} %param.30) | copy-start | bytes 1179652
  0.7 7.5 copy-start.108
  0.7 8.3 copy-start.7
  0.7 8.3 copy-start.8
  0.7 8.3 copy-start.3
  223.5 9.7 copy-start.67
  223.5 9.7 copy-start.71
  260.8 7.6 copy-start.16
  262.7 8.9 copy-start.77
  340.6 18.2 %slice-start.2 = ((s8[4718592]{0:T(1024)(128)(4,1)}), s8[524288]{0:T(1024)(128)(4,1)S(1)}, s32[]{:S(2)}) async-start(s8[4718592]{0:T(1024)(128)(4,1)} %bitcast.286), calls=%async_computation.2 | async-start | bytes 1048576
  350.4 8.4 slice-start.3
  363.5 6.4 copy-start.32
  369.9 5.6 copy-start.29
  394.4 237.6 %collective-permute-start.5 = (bf16[512,1536]{1,0:T(8,128)(2,1)}, bf16[512,1536]{1,0:T(8,128)(2,1)}, u32[]{:S(2)}, u32[]{:S(2)}) collective-permute-start(bf16[512,1536]{1,0:T(8,128)(2,1)} %get-tuple-element.127.refs_5_), channel_id=1, source_target_pairs={{0,4},{4,0},{8,12},{12,8},{16,20},{20,16},{24,28},{28,24},{1,5},{5... | collective-permute-start | bytes 4718600 | tf_op jit(solution)/shard_map/ppermute | solution.py:838
  415.2 8.6 copy-start.113
  415.2 16.4 %slice-start.18 = ((s8[4718592]{0:T(1024)(128)(4,1)}), s8[4194304]{0:T(1024)(128)(4,1)S(1)}, s32[]{:S(2)}) async-start(s8[4718592]{0:T(1024)(128)(4,1)} %bitcast.355), calls=%async_computation.18 | async-start | bytes 8388608
  423.8 20.0 %copy-start.36 = (bf16[512,1536]{1,0:T(8,128)(2,1)}, bf16[512,1536]{1,0:T(8,128)(2,1)S(1)}, u32[]{:S(2)}) copy-start(bf16[512,1536]{1,0:T(8,128)(2,1)S(1)} %get-tuple-element.63) | copy-start | bytes 4718596
  423.8 7.8 slice-start.19
  423.8 7.8 copy-start.114
  423.8 13.4 %slice-start.8 = ((s8[4718592]{0:T(1024)(128)(4,1)}), s8[4194304]{0:T(1024)(128)(4,1)S(1)}, s32[]{:S(2)}) async-start(s8[4718592]{0:T(1024)(128)(4,1)} %bitcast.297), calls=%async_computation.8 | async-start | bytes 8388608
  423.8 16.1 %slice-start.6 = ((s8[4718592]{0:T(1024)(128)(4,1)}), s8[4194304]{0:T(1024)(128)(4,1)S(1)}, s32[]{:S(2)}) async-start(s8[4718592]{0:T(1024)(128)(4,1)} %bitcast.293), calls=%async_computation.6 | async-start | bytes 8388608
  431.6 8.2 copy-start.54
  432.1 7.8 slice-start.7
  437.2 11.1 %slice-start = ((s8[4718592]{0:T(1024)(128)(4,1)}), s8[4194304]{0:T(1024)(128)(4,1)S(1)}, s32[]{:S(2)}) async-start(s8[4718592]{0:T(1024)(128)(4,1)} %bitcast.282), calls=%async_computation | async-start | bytes 8388608
  439.9 8.3 slice-start.1
  453.9 5.8 slice-start.11
  507.1 13.1 %copy-start.48 = (bf16[512,512]{0,1:T(8,128)(2,1)S(1)}, bf16[512,512]{0,1:T(8,128)(2,1)}, u32[]{:S(2)}) copy-start(bf16[512,512]{0,1:T(8,128)(2,1)} %copy-done.47) | copy-start | bytes 1572868
  520.2 6.4 copy-start.66
  520.3 6.4 copy-start.81
  520.3 6.4 copy-start.83
  520.3 6.4 copy-start.85
  520.3 7.1 copy-start.35
  520.3 7.1 copy-start.50
  527.2 94.6 %collective-permute-start.13 = (bf16[192,512]{1,0:T(8,128)(2,1)S(1)}, bf16[192,512]{1,0:T(8,128)(2,1)S(1)}, u32[]{:S(2)}, u32[]{:S(2)}) collective-permute-start(bf16[192,512]{1,0:T(8,128)(2,1)S(1)} %convolution_convert_fusion.6), channel_id=1, source_target_pairs={{0,4},{4,0},{8,12},{12,8},{16,20},{20,16},{24,28},{28,24},{1,5},{5... | collective-permute-start | bytes 589832 | tf_op jit(solution)/shard_map/ppermute | solution.py:838
  537.7 11.4 %slice-start.4 = ((s8[4718592]{0:T(1024)(128)(4,1)}), s8[524288]{0:T(1024)(128)(4,1)S(1)}, s32[]{:S(2)}) async-start(s8[4718592]{0:T(1024)(128)(4,1)} %bitcast.289), calls=%async_computation.4 | async-start | bytes 1048576
  541.6 5.6 copy-start.52
  541.6 5.6 copy-start.53
  541.6 7.5 slice-start.5
  541.6 80.4 %collective-permute-start.7 = (bf16[512,768]{1,0:T(8,128)(2,1)}, bf16[512,768]{1,0:T(8,128)(2,1)}, u32[]{:S(2)}, u32[]{:S(2)}) collective-permute-start(bf16[512,768]{1,0:T(8,128)(2,1)} %get-tuple-element.98), channel_id=1, source_target_pairs={{0,4},{4,0},{8,12},{12,8},{16,20},{20,16},{24,28},{28,24},{1,5},{5... | collective-permute-start | bytes 2359304 | tf_op jit(solution)/shard_map/ppermute | solution.py:838
  556.9 31.5 %copy-start.39 = (bf16[512,1536]{1,0:T(8,128)(2,1)}, bf16[512,1536]{1,0:T(8,128)(2,1)S(1)}, u32[]{:S(2)}) copy-start(bf16[512,1536]{1,0:T(8,128)(2,1)S(1)} %get-tuple-element.68) | copy-start | bytes 4718596
  558.2 64.1 %collective-permute-start.6 = (bf16[512,768]{1,0:T(8,128)(2,1)}, bf16[512,768]{1,0:T(8,128)(2,1)}, u32[]{:S(2)}, u32[]{:S(2)}) collective-permute-start(bf16[512,768]{1,0:T(8,128)(2,1)} %get-tuple-element.93), channel_id=1, source_target_pairs={{0,4},{4,0},{8,12},{12,8},{16,20},{20,16},{24,28},{28,24},{1,5},{5... | collective-permute-start | bytes 2359304 | tf_op jit(solution)/shard_map/ppermute | solution.py:838
  560.5 62.0 %collective-permute-start.8 = (bf16[512,768]{1,0:T(8,128)(2,1)}, bf16[512,768]{1,0:T(8,128)(2,1)}, u32[]{:S(2)}, u32[]{:S(2)}) collective-permute-start(bf16[512,768]{1,0:T(8,128)(2,1)} %copy.95), channel_id=1, source_target_pairs={{0,4},{4,0},{8,12},{12,8},{16,20},{20,16},{24,28},{28,24},{1,5},{5... | collective-permute-start | bytes 2359304 | tf_op jit(solution)/shard_map/ppermute | solution.py:838
  578.2 7.4 slice-start.16
  591.3 9.7 copy-start.104
  591.3 11.0 %copy-start.102 = (f32[1536]{0:T(1024)S(1)}, f32[1536]{0:T(1024)}, u32[]{:S(2)}) copy-start(f32[1536]{0:T(1024)} %get-tuple-element.40) | copy-start | bytes 18436
  591.3 13.6 %copy-start.88 = (f32[1536]{0:T(1024)S(1)}, f32[1536]{0:T(1024)}, u32[]{:S(2)}) copy-start(f32[1536]{0:T(1024)} %get-tuple-element.67) | copy-start | bytes 18436
  591.3 14.9 %copy-start.103 = (f32[1536]{0:T(1024)S(1)}, f32[1536]{0:T(1024)}, u32[]{:S(2)}) copy-start(f32[1536]{0:T(1024)} %get-tuple-element.47) | copy-start | bytes 18436
  591.3 16.2 %copy-start.89 = (f32[1536]{0:T(1024)S(1)}, f32[1536]{0:T(1024)}, u32[]{:S(2)}) copy-start(f32[1536]{0:T(1024)} %get-tuple-element.64) | copy-start | bytes 18436
  591.4 20.2 %copy-start.38 = (bf16[512,1536]{1,0:T(8,128)(2,1)S(1)}, bf16[512,1536]{1,0:T(8,128)(2,1)}, u32[]{:S(2)}) copy-start(bf16[512,1536]{1,0:T(8,128)(2,1)} %copy-done.37) | copy-start | bytes 4718596
  618.4 5.8 copy-start.99
  618.4 7.1 copy-start.101
  618.4 8.4 copy-start.100
  618.4 11.0 %copy-start.27 = (bf16[512,768]{1,0:T(8,128)(2,1)S(1)}, bf16[512,768]{1,0:T(8,128)(2,1)}, u32[]{:S(2)}) copy-start(bf16[512,768]{1,0:T(8,128)(2,1)} %get-tuple-element.94) | copy-start | bytes 2359300
  619.3 11.3 %copy-start.21 = (bf16[512,1536]{1,0:T(8,128)(2,1)S(1)}, bf16[512,1536]{1,0:T(8,128)(2,1)}, u32[]{:S(2)}) copy-start(bf16[512,1536]{1,0:T(8,128)(2,1)} %copy-done.20) | copy-start | bytes 4718596
  621.8 8.0 collective-permute-start.9
  622.0 8.1 collective-permute-start.11
  622.4 8.1 collective-permute-start.10
  622.5 8.1 collective-permute-start.12
  629.8 18.9 %collective-permute-start.4 = (bf16[512,1536]{1,0:T(8,128)(2,1)}, bf16[512,1536]{1,0:T(8,128)(2,1)}, u32[]{:S(2)}, u32[]{:S(2)}) collective-permute-start(bf16[512,1536]{1,0:T(8,128)(2,1)} %get-tuple-element.125.refs_4_), channel_id=1, source_target_pairs={{0,4},{4,0},{8,12},{12,8},{16,20},{20,16},{24,28},{28,24},{1,5},{5... | collective-permute-start | bytes 4718600 | tf_op jit(solution)/shard_map/ppermute | solution.py:838
  630.0 18.7 %collective-permute-start.3 = (bf16[512,1536]{1,0:T(8,128)(2,1)}, bf16[512,1536]{1,0:T(8,128)(2,1)}, u32[]{:S(2)}, u32[]{:S(2)}) collective-permute-start(bf16[512,1536]{1,0:T(8,128)(2,1)} %add_convert_fusion.refs_3_), channel_id=1, source_target_pairs={{0,4},{4,0},{8,12},{12,8},{16,20},{20,16},{24,28},{28,24},{1,5},{5... | collective-permute-start | bytes 4718600 | tf_op jit(solution)/shard_map/ppermute | solution.py:838
  630.4 18.4 %collective-permute-start.1 = (bf16[512,1536]{1,0:T(8,128)(2,1)}, bf16[512,1536]{1,0:T(8,128)(2,1)}, u32[]{:S(2)}, u32[]{:S(2)}) collective-permute-start(bf16[512,1536]{1,0:T(8,128)(2,1)} %add_convert_fusion.1.refs_1_), channel_id=1, source_target_pairs={{0,4},{4,0},{8,12},{12,8},{16,20},{20,16},{24,28},{28,24},{1,5},{5... | collective-permute-start | bytes 4718600 | tf_op jit(solution)/shard_map/ppermute | solution.py:838
  630.6 18.2 %collective-permute-start = (bf16[512,1536]{1,0:T(8,128)(2,1)S(1)}, bf16[512,1536]{1,0:T(8,128)(2,1)}, u32[]{:S(2)}, u32[]{:S(2)}) collective-permute-start(bf16[512,1536]{1,0:T(8,128)(2,1)S(1)} %copy-done.21), channel_id=1, source_target_pairs={{0,4},{4,0},{8,12},{12,8},{16,20},{20,16},{24,28},{28,24},{1,5},{5... | collective-permute-start | bytes 4718600 | tf_op jit(solution)/shard_map/ppermute | solution.py:838
  632.0 16.8 %collective-permute-start.2 = (bf16[512,1536]{1,0:T(8,128)(2,1)}, bf16[512,1536]{1,0:T(8,128)(2,1)}, u32[]{:S(2)}, u32[]{:S(2)}) collective-permute-start(bf16[512,1536]{1,0:T(8,128)(2,1)} %copy.87.refs_2_), channel_id=1, source_target_pairs={{0,4},{4,0},{8,12},{12,8},{16,20},{20,16},{24,28},{28,24},{1,5},{5... | collective-permute-start | bytes 4718600 | tf_op jit(solution)/shard_map/ppermute | solution.py:838
  960.1 9.9 %copy-start.31 = (bf16[12,384,1536]{2,1,0:T(8,128)(2,1)S(1)}, bf16[12,384,1536]{2,1,0:T(8,128)(2,1)}, u32[]{:S(2)}) copy-start(bf16[12,384,1536]{2,1,0:T(8,128)(2,1)} %get-tuple-element.39) | copy-start | bytes 42467332
  (85 other events, 241.2 us)

commit v3 on v2

--- a/solution.py
+++ b/solution.py
@@ -372,19 +372,31 @@
 
 def reduce_kernel(groups, blocks, rel_at, *refs):
     lefts = refs[:6]
-    lefts_sib = refs[6:12]
-    conv_right, conv_right_sib = refs[12:14]
-    rights = refs[14:21]
-    rights_sib = refs[21:28]
-    rel_grad, vector = refs[28:30]
-    out, total = refs[30:32]
-    left_hold, right_hold, grad, x_one, y_one, x_two, y_two, shard_got, block_got, partial, done = refs[32:43]
-    load_sem = refs[43]
-    x1s, y1s, x2s, y2s, x1r, y1r, x2r, y2r = refs[44:52]
-    shard_send, shard_recv, block_send, block_recv = refs[52:56]
-    write_sem, send_sem, ax, ay, ad, sib_sem = refs[56:62]
-    sum_bufs = refs[62:66]
-    sum_sems = refs[66:72]
+    rights = refs[6:13]
+    rel_grad, vector = refs[13:15]
+    out, total, left_got, right_got = refs[15:19]
+    (
+        left_hold,
+        right_hold,
+        grad,
+        x_one,
+        y_one,
+        x_two,
+        y_two,
+        shard_got,
+        block_got,
+        partial,
+        done,
+        rel_got,
+    ) = refs[19:31]
+    left_send, left_recv, right_send, right_recv, rel_send, rel_recv = refs[31:37]
+    refs = refs[37:]
+    load_sem = refs[0]
+    x1s, y1s, x2s, y2s, x1r, y1r, x2r, y2r = refs[1:9]
+    shard_send, shard_recv, block_send, block_recv = refs[9:13]
+    write_sem, send_sem, ax, ay, ad, sib_sem = refs[13:19]
+    sum_bufs = refs[19:23]
+    sum_sems = refs[23:29]
 
     dp = lax.axis_index("dp")
     me = lax.axis_index("fsdp")
@@ -403,26 +415,60 @@
     others = groups - 1
     first = pl.ds(0, half)
     last = pl.ds(half, half)
-    left_of = [0] * 5 + [1, 1, 2, 3, 3, 4, 5]
+    taps = 5
+    left_of = [0] * taps + [1, 1, 2, 3, 3, 4, 5]
+    right_of = [0] * taps + [1, 2, 3, 4, 5, 6, 6]
+    own_columns = pl.ds(pl.multiple_of(core * width, 128), width)
+    sib_columns = pl.ds(pl.multiple_of((1 - core) * width, 128), width)
+
+    def left_copy(index):
+        return remote(
+            lefts[index], left_got.at[index], left_send.at[index], left_recv.at[index], (sib, me)
+        )
+
+    def right_copy(index):
+        return remote(
+            rights[index].at[:, sib_columns],
+            right_got.at[index],
+            right_send.at[index],
+            right_recv.at[index],
+            (sib, me),
+        )
+
+    def rel_copy():
+        return remote(rel_grad, rel_got, rel_send.at[0], rel_recv.at[0], (sib, me))
 
     def loads(piece, slot):
-        right = conv_right.at[piece] if piece < 5 else rights[piece - 5]
-        right_sib = conv_right_sib.at[piece] if piece < 5 else rights_sib[piece - 5]
+        left = left_of[piece]
+        right = right_of[piece]
         pairs = (
-            (lefts[left_of[piece]], left_hold.at[slot, 0]),
-            (lefts_sib[left_of[piece]], left_hold.at[slot, 1]),
-            (right, right_hold.at[slot, 0]),
-            (right_sib, right_hold.at[slot, 1]),
+            (lefts[left], left_hold.at[slot, 0]),
+            (left_got.at[left], left_hold.at[slot, 1]),
+            (rights[right].at[:, own_columns], right_hold.at[slot, 0]),
+            (right_got.at[right], right_hold.at[slot, 1]),
         )
         return [
             pltpu.make_async_copy(src, dst, load_sem.at[slot, i])
             for i, (src, dst) in enumerate(pairs)
         ]
 
-    for copy in loads(0, 0):
-        copy.start()
+    def start_loads(piece):
+        if left_of[piece] not in left_of[:piece]:
+            left_copy(left_of[piece]).wait_recv()
+        if right_of[piece] not in right_of[:piece]:
+            right_copy(right_of[piece]).wait_recv()
+        for copy in loads(piece, piece % 2):
+            copy.start()
 
     meet(near + shards + far)
+
+    for piece in range(count):
+        if left_of[piece] not in left_of[:piece]:
+            left_copy(left_of[piece]).start()
+        if right_of[piece] not in right_of[:piece]:
+            right_copy(right_of[piece]).start()
+    rel_copy().start()
+    start_loads(0)
 
     summing = sum_steps(groups, blocks, vector, total, *sum_bufs, sum_sems)
 
@@ -518,6 +564,16 @@
 
     diagonal = neighbours(along_x)[2]
 
+    def shift(piece):
+        move = piece - taps // 2
+        for window in range(2):
+            value = right_hold[piece % 2, window].astype(jnp.float32)
+            value = pltpu.roll(value, move % value.shape[0], 0)
+            row = lax.broadcasted_iota(jnp.int32, value.shape, 0)
+            inside = row >= move if move > 0 else row < value.shape[0] + move
+            value = jnp.where(inside, value, 0.0)
+            right_hold[piece % 2, window] = value.astype(right_hold.dtype)
+
     def produce(piece):
         slot = piece % slots
         hold = piece % 2
@@ -531,10 +587,17 @@
 
         lax.fori_loop(0, groups, shard_body, 0)
 
-        @pl.when(jnp.logical_and(piece == 5, core == 1))
+        @pl.when(piece == taps)
+        def _():
+            rel_copy().wait()
+
+        @pl.when(jnp.logical_and(piece == taps, core == 1))
         def _():
             for shard in range(groups):
-                grad[slot, shard, 0, :, :, pl.ds(rel_at, rel_grad.shape[3])] = rel_grad[shard]
+                value = rel_grad[shard].astype(jnp.float32) + rel_got[shard].astype(jnp.float32)
+                grad[slot, shard, 0, :, :, pl.ds(rel_at, rel_grad.shape[3])] = value.astype(
+                    grad.dtype
+                )
 
     def add(piece_slot, ref, columns, *index):
         ahead = grad[(piece_slot,) + index + (slice(None), columns)]
@@ -558,8 +621,9 @@
                     for copy in loads(piece, piece % 2):
                         copy.wait()
                     if piece + 1 < count:
-                        for copy in loads(piece + 1, (piece + 1) % 2):
-                            copy.start()
+                        start_loads(piece + 1)
+                    if piece < taps and piece != taps // 2:
+                        shift(piece)
 
             produce(n)
             for copy in one(n):
@@ -670,28 +734,19 @@
         return carry
 
     lax.fori_loop(0, count, drain, 0)
-
-
-def reduce(
-    groups,
-    blocks,
-    rel_at,
-    lefts,
-    lefts_sib,
-    conv_right,
-    conv_right_sib,
-    rights,
-    rights_sib,
-    rel_grad,
-    vector,
-):
+    for index in range(len(lefts)):
+        left_copy(index).wait_send()
+    for index in range(len(rights)):
+        right_copy(index).wait_send()
+
+
+def reduce(groups, blocks, rel_at, lefts, rights, rel_grad, vector):
     bins, columns = lefts[0].shape
     width = columns // 2
     rows = columns // groups
     part = rows // 4
     dtype = lefts[0].dtype
-    taps = conv_right.shape[0]
-    count = taps + len(rights)
+    count = 12
     slots = 5
     kept = pl.BlockSpec(memory_space=pl.ANY)
     inside = pl.BlockSpec(memory_space=pltpu.VMEM)
@@ -701,9 +756,11 @@
         out_shape=(
             jax.ShapeDtypeStruct((count, rows, columns), dtype),
             jax.ShapeDtypeStruct(vector.shape, jnp.float32),
+            jax.ShapeDtypeStruct((len(lefts), bins, columns), dtype),
+            jax.ShapeDtypeStruct((len(rights), bins, width), dtype),
         ),
-        in_specs=[kept] * 28 + [inside] * 2,
-        out_specs=[kept, inside],
+        in_specs=[kept] * (len(lefts) + len(rights)) + [inside] * 2,
+        out_specs=[kept, inside, kept, kept],
         scratch_shapes=[
             pltpu.VMEM((2, 2, bins, columns), dtype),
             pltpu.VMEM((2, 2, bins, width), dtype),
@@ -716,6 +773,13 @@
             pltpu.VMEM((count if blocks > 1 else 1, blocks, part, width), dtype),
             pltpu.VMEM((count if blocks > 1 else 1, part, width), dtype),
             pltpu.VMEM((count, part, width), dtype),
+            pltpu.VMEM(rel_grad.shape, dtype),
+            pltpu.SemaphoreType.DMA((len(lefts),)),
+            pltpu.SemaphoreType.DMA((len(lefts),)),
+            pltpu.SemaphoreType.DMA((len(rights),)),
+            pltpu.SemaphoreType.DMA((len(rights),)),
+            pltpu.SemaphoreType.DMA((1,)),
+            pltpu.SemaphoreType.DMA((1,)),
             pltpu.SemaphoreType.DMA((2, 4)),
             *([each] * 8),
             pltpu.SemaphoreType.DMA((count, groups)),
@@ -729,15 +793,16 @@
             collective_id=1, has_side_effects=True, vmem_limit_bytes=60 << 20
         ),
         name="reduce",
-    )(*lefts, *lefts_sib, conv_right, conv_right_sib, *rights, *rights_sib, rel_grad, vector)
+    )(*lefts, *rights, rel_grad, vector)
 
 
 EPSILON = 1e-05
 
 
-def position_table(length, features):
+def position_table(length, features, direction):
     basis_count = features // 6
     offsets = jnp.arange(2 * length - 1, dtype=jnp.float32) - (length - 1)
+    offsets = offsets * direction
     distance = jnp.abs(offsets)[:, None]
     max_range = math.log(length) / math.log(2.0)
     half_life = 2.0 ** jnp.linspace(3.0, max_range, basis_count, dtype=jnp.float32)
@@ -757,15 +822,6 @@
     return jnp.concatenate([symmetric, sign_row * symmetric], 1)
 
 
-def relative_shift(scores):
-    row_count = scores.shape[-2]
-    span_width = scores.shape[-1]
-    leading = scores.shape[:-2]
-    padded = jnp.pad(scores, [(0, 0)] * (scores.ndim - 1) + [(1, 0)])
-    folded = padded.reshape(leading + (span_width + 1, row_count))[..., 1:, :]
-    return folded.reshape(leading + (row_count, span_width))[..., :row_count]
-
-
 def normalize(values):
     centred = values - jnp.mean(values, -1, keepdims=True)
     inverse = lax.rsqrt(jnp.mean(centred * centred, -1, keepdims=True) + EPSILON)
@@ -792,14 +848,155 @@
     )
 
 
-def attention_scores(content_query, key_heads, position_query, position_keys):
-    content = jnp.einsum(
-        "ihk,jhk->hij", content_query, key_heads, preferred_element_type=jnp.float32
-    )
-    relative = jnp.einsum(
-        "ihk,mhk->him", position_query, position_keys, preferred_element_type=jnp.float32
-    )
-    return content + relative_shift(relative)
+def attend_kernel(content_ref, position_ref, key_ref, value_ref, table_ref, out_ref, probs_ref):
+    length = content_ref.shape[0]
+    span = table_ref.shape[0]
+    head_value = value_ref.shape[1] // 2
+    for head in range(2):
+        keys = slice(head * KEY, (head + 1) * KEY)
+        values = slice(head * head_value, (head + 1) * head_value)
+        band = dot_trailing(position_ref[:, keys], table_ref[:, keys])
+        moved = pltpu.roll(band, span - length + 1, 1, stride=1, stride_axis=0)
+        scores = dot_trailing(content_ref[:, keys], key_ref[:, keys]) + moved[:, :length]
+        weight = jnp.exp(scores - jnp.max(scores, -1, keepdims=True))
+        probs = (weight / jnp.sum(weight, -1, keepdims=True)).astype(jnp.bfloat16)
+        probs_ref[head] = probs
+        out_ref[:, values] = jnp.dot(
+            probs, value_ref[:, values], preferred_element_type=jnp.float32
+        ).astype(out_ref.dtype)
+
+
+def attend(content, position, key, value, table):
+    length = content.shape[0]
+    span = table.shape[0]
+    steps = HEADS // 2
+
+    def columns(array):
+        return pl.BlockSpec((array.shape[0], array.shape[1] // steps), lambda i: (0, i))
+
+    return pl.pallas_call(
+        attend_kernel,
+        grid=(steps,),
+        in_specs=[columns(array) for array in (content, position, key, value, table)],
+        out_specs=(columns(value), pl.BlockSpec((2, length, length), lambda i: (i, 0, 0))),
+        out_shape=(
+            jax.ShapeDtypeStruct(value.shape, jnp.bfloat16),
+            jax.ShapeDtypeStruct((HEADS, length, length), jnp.bfloat16),
+        ),
+        compiler_params=pltpu.CompilerParams(vmem_limit_bytes=40 << 20),
+        cost_estimate=pl.CostEstimate(
+            flops=2 * length * (HEADS * KEY * (length + span) + length * value.shape[1]),
+            bytes_accessed=2 * HEADS * length * length,
+            transcendentals=HEADS * length * length,
+        ),
+        name="attend",
+    )(content, position, key, value, table)
+
+
+def attend_back_kernel(
+    probs_ref,
+    out_ref,
+    value_ref,
+    key_ref,
+    content_ref,
+    position_ref,
+    table_ref,
+    query_grad_ref,
+    key_grad_ref,
+    value_grad_ref,
+    table_grad_ref,
+    offset_ref,
+):
+    length = content_ref.shape[0]
+    span = table_ref.shape[0]
+    head_value = value_ref.shape[1] // 2
+    row = lax.broadcasted_iota(jnp.int32, (length, length), 0)
+    column = lax.broadcasted_iota(jnp.int32, (length, length), 1)
+    mirror = jnp.where(row + column == length - 1, 1.0, 0.0).astype(jnp.bfloat16)
+    for head in range(2):
+        keys = slice(head * KEY, (head + 1) * KEY)
+        values = slice(head * head_value, (head + 1) * head_value)
+        probs = probs_ref[head]
+        out_grad = out_ref[:, values]
+        value_grad_ref[:, values] = dot_leading(probs, out_grad).astype(jnp.bfloat16)
+        prob_grad = dot_trailing(out_grad, value_ref[:, values])
+        probs = probs.astype(jnp.float32)
+        row_dot = jnp.sum(probs * prob_grad, -1, keepdims=True)
+        score_grad = probs * (prob_grad - row_dot)
+        rounded = score_grad.astype(jnp.bfloat16)
+        key_grad_ref[:, keys] = dot_leading(rounded, content_ref[:, keys]).astype(jnp.bfloat16)
+        content_grad = jnp.dot(rounded, key_ref[:, keys], preferred_element_type=jnp.float32)
+        mirrored = jnp.dot(rounded, mirror, preferred_element_type=jnp.float32)
+        wide = jnp.concatenate([mirrored, jnp.zeros((length, span - length), jnp.float32)], 1)
+        band = pltpu.roll(wide, 0, 1, stride=1, stride_axis=0)
+        band = band.astype(jnp.bfloat16)
+        position_grad = jnp.dot(band, table_ref[:, keys], preferred_element_type=jnp.float32)
+        table_grad_ref[:, keys] = dot_leading(band, position_ref[:, keys]).astype(jnp.bfloat16)
+        query_grad_ref[:, keys] = ((content_grad + position_grad) * KEY**-0.5).astype(
+            jnp.bfloat16
+        )
+        offset_ref[0:1, keys] = jnp.sum(content_grad, 0, keepdims=True)
+        offset_ref[1:2, keys] = jnp.sum(position_grad, 0, keepdims=True)
+
+
+def attend_back(probs, out_grad, value, key, content, position, table):
+    length = content.shape[0]
+    span = table.shape[0]
+    steps = HEADS // 2
+
+    def columns(array):
+        return pl.BlockSpec((array.shape[0], array.shape[1] // steps), lambda i: (0, i))
+
+    offsets = jax.ShapeDtypeStruct((2, key.shape[1]), jnp.float32)
+    return pl.pallas_call(
+        attend_back_kernel,
+        grid=(steps,),
+        in_specs=[pl.BlockSpec((2, length, length), lambda i: (i, 0, 0))]
+        + [columns(array) for array in (out_grad, value, key, content, position, table)],
+        out_specs=[columns(array) for array in (content, key, value, table, offsets)],
+        out_shape=[
+            jax.ShapeDtypeStruct(array.shape, jnp.bfloat16)
+            for array in (content, key, value, table)
+        ]
+        + [offsets],
+        compiler_params=pltpu.CompilerParams(vmem_limit_bytes=40 << 20),
+        cost_estimate=pl.CostEstimate(
+            flops=4 * length * (HEADS * KEY * (length + span) + length * value.shape[1]),
+            bytes_accessed=2 * HEADS * length * length,
+            transcendentals=0,
+        ),
+        name="attend_back",
+    )(probs, out_grad, value, key, content, position, table)
+
+
+def conv_back_kernel(left_ref, right_ref, out_ref):
+    @pl.when(pl.program_id(0) == 0)
+    def _():
+        out_ref[...] = jnp.zeros_like(out_ref)
+
+    out_ref[...] += dot_trailing(left_ref[...], right_ref[0])
+
+
+def conv_back(left, right):
+    length = left.shape[0]
+    taps, columns = right.shape[:2]
+    return pl.pallas_call(
+        conv_back_kernel,
+        grid=(taps,),
+        in_specs=[
+            pl.BlockSpec((length, columns), lambda i: (0, i)),
+            pl.BlockSpec((1, columns, columns), lambda i: (i, 0, 0)),
+        ],
+        out_specs=pl.BlockSpec((length, columns), lambda i: (0, 0)),
+        out_shape=jax.ShapeDtypeStruct((length, columns), jnp.float32),
+        compiler_params=pltpu.CompilerParams(vmem_limit_bytes=40 << 20),
+        cost_estimate=pl.CostEstimate(
+            flops=2 * taps * length * columns * columns,
+            bytes_accessed=2 * taps * columns * (columns + length),
+            transcendentals=0,
+        ),
+        name="conv_back",
+    )(left, right)
 
 
 def on_device(
@@ -823,8 +1020,6 @@
 ):
     groups = lax.axis_size("fsdp")
     blocks = lax.axis_size("dp") // 8
-    core = lax.axis_index("dp") % 2
-    pairs = [(i, i + 1 - 2 * (i % 2)) for i in range(lax.axis_size("dp"))]
     tap_count, piece_rows, model_width = conv_weight.shape
     half_taps = tap_count // 2
     half_width = model_width // 2
@@ -833,17 +1028,6 @@
     inputs = tokens[0].astype(jnp.float32)
     length = inputs.shape[0]
     token_total = length * lax.axis_size("dp") * lax.axis_size("fsdp")
-
-    def exchange(array):
-        return lax.ppermute(array, "dp", pairs)
-
-    def own_half(array):
-        return lax.dynamic_slice_in_dim(array, core * half_width, half_width, 1)
-
-    def sib_half(array):
-        return exchange(
-            lax.dynamic_slice_in_dim(array, (1 - core) * half_width, half_width, 1)
-        )
 
     small_parts = [gains, biases, up_bias, rel_bias]
     small = jnp.concatenate([part.reshape(-1) for part in small_parts])
@@ -913,35 +1097,21 @@
     mixed_raw = jnp.dot(normed_one, mixed_full, preferred_element_type=jnp.float32)
     query_raw = mixed_raw[:, :key_width]
     key_scale = KEY ** (-0.5)
-    content_query = (
-        (query_raw * key_scale + rel_offset[0]).astype(jnp.bfloat16).reshape(length, HEADS, -1)
-    )
-    position_query = (
-        (query_raw * key_scale + rel_offset[1]).astype(jnp.bfloat16).reshape(length, HEADS, -1)
-    )
-    key_heads = mixed_raw[:, key_width:].astype(jnp.bfloat16).reshape(length, HEADS, -1)
-    value_heads = (
-        jnp.dot(normed_one, value_full, preferred_element_type=jnp.float32)
-        .astype(jnp.bfloat16)
-        .reshape(length, HEADS, -1)
-    )
-    table = position_table(length, rel_full.shape[0]).astype(jnp.bfloat16)
-    position_keys = (
-        jnp.dot(table, rel_full, preferred_element_type=jnp.float32)
-        .astype(jnp.bfloat16)
-        .reshape(table.shape[0], HEADS, -1)
-    )
-    scores = attention_scores(content_query, key_heads, position_query, position_keys)
-    row_peak = jnp.max(scores, -1, keepdims=True)
-    normalizer = row_peak + jnp.log(jnp.sum(jnp.exp(scores - row_peak), -1, keepdims=True))
-    attention_probs = jnp.exp(scores - normalizer)
-    attended = jnp.einsum(
-        "hij,jhv->ihv",
-        attention_probs.astype(jnp.bfloat16),
-        value_heads,
-        preferred_element_type=jnp.float32,
-    )
-    attended = attended.reshape(length, model_width).astype(jnp.bfloat16)
+    content_query = (query_raw * key_scale + rel_offset[0]).astype(jnp.bfloat16)
+    position_query = (query_raw * key_scale + rel_offset[1]).astype(jnp.bfloat16)
+    keys = mixed_raw[:, key_width:].astype(jnp.bfloat16)
+    values = jnp.dot(normed_one, value_full, preferred_element_type=jnp.float32).astype(
+        jnp.bfloat16
+    )
+    table, mirrored_table = [
+        jnp.pad(position_table(length, rel_rows, direction), ((0, 1), (0, 0))).astype(jnp.bfloat16)
+        for direction in (1.0, -1.0)
+    ]
+    position_keys, mirrored_keys = [
+        jnp.dot(side, rel_full, preferred_element_type=jnp.float32).astype(jnp.bfloat16)
+        for side in (table, mirrored_table)
+    ]
+    attended, probs = attend(content_query, position_query, keys, values, position_keys)
     after_attention = (
         after_conv + jnp.dot(attended, out_full, preferred_element_type=jnp.float32) + bias_rows[3]
     )
@@ -981,45 +1151,9 @@
     )
     branch_grad = attention_grad.astype(jnp.bfloat16)
     grad_out_bias = jnp.sum(branch_grad.astype(jnp.float32), 0)
-    attended_grad = (
-        dot_trailing(branch_grad, out_full).astype(jnp.bfloat16).reshape(length, HEADS, -1)
-    )
-    scores = attention_scores(content_query, key_heads, position_query, position_keys)
-    attention_probs = jnp.exp(scores - normalizer)
-    value_grad = jnp.einsum(
-        "hij,ihv->jhv",
-        attention_probs.astype(jnp.bfloat16),
-        attended_grad,
-        preferred_element_type=jnp.float32,
-    )
-    value_grad = value_grad.reshape(length, model_width).astype(jnp.bfloat16)
-    prob_grad = jnp.einsum(
-        "ihv,jhv->hij", attended_grad, value_heads, preferred_element_type=jnp.float32
-    )
-    row_dot = jnp.sum(attention_probs * prob_grad, -1, keepdims=True)
-    score_grad = (attention_probs * (prob_grad - row_dot)).astype(jnp.bfloat16)
-    content_grad = jnp.einsum(
-        "hij,jhk->ihk", score_grad, key_heads, preferred_element_type=jnp.float32
-    )
-    key_grad = jnp.einsum(
-        "hij,ihk->jhk", score_grad, content_query, preferred_element_type=jnp.float32
-    )
-    key_grad = key_grad.reshape(length, -1).astype(jnp.bfloat16)
-    band_zeros = jnp.zeros((HEADS, length, position_keys.shape[0]), jnp.float32)
-    shift_pull = jax.vjp(relative_shift, band_zeros)[1]
-    band_grad = shift_pull(score_grad.astype(jnp.float32))[0].astype(jnp.bfloat16)
-    position_grad = jnp.einsum(
-        "him,mhk->ihk", band_grad, position_keys, preferred_element_type=jnp.float32
-    )
-    table_grad = jnp.einsum(
-        "him,ihk->mhk", band_grad, position_query, preferred_element_type=jnp.float32
-    )
-    table_grad = table_grad.reshape(table.shape[0], -1).astype(jnp.bfloat16)
-    grad_rel_bias = jnp.stack(
-        [jnp.sum(content_grad, 0).reshape(-1), jnp.sum(position_grad, 0).reshape(-1)]
-    )
-    query_grad = (
-        ((content_grad + position_grad) * key_scale).reshape(length, -1).astype(jnp.bfloat16)
+    attended_grad = dot_trailing(branch_grad, out_full).astype(jnp.bfloat16)
+    query_grad, key_grad, value_grad, table_grad, grad_rel_bias = attend_back(
+        probs, attended_grad, values, keys, content_query, position_query, mirrored_keys
     )
     mixed_grad = jnp.concatenate([query_grad, key_grad], 1)
     normed_one_grad = (
@@ -1034,10 +1168,10 @@
     conv_grad = conv_side_grad.astype(jnp.bfloat16)
     grad_conv_bias = jnp.sum(conv_grad.astype(jnp.float32), 0)
     padded = jnp.pad(conv_grad, ((half_taps, half_taps), (0, 0)))
-    activated_grad = 0.0
-    for tap in range(tap_count):
-        moved = padded[tap_count - 1 - tap : tap_count - 1 - tap + length]
-        activated_grad = activated_grad + dot_trailing(moved, conv_full[tap])
+    stacked_grad = jnp.concatenate(
+        [padded[tap : tap + length] for tap in reversed(range(tap_count))], 1
+    )
+    activated_grad = conv_back(stacked_grad, conv_full)
     act_pull = jax.vjp(jax.nn.gelu, normed)[1]
     normed_grad = act_pull(activated_grad)[0]
     sum_parts = [
@@ -1056,33 +1190,22 @@
     ]
     sums = jnp.concatenate(sum_parts)
     sums = jnp.pad(sums, (0, -sums.shape[0] % 1024)).reshape(-1, 128)
-    grad_rel = dot_leading(table, table_grad).astype(jnp.bfloat16)
-    grad_rel = grad_rel.astype(jnp.float32) + exchange(grad_rel).astype(jnp.float32)
+    grad_rel = dot_leading(mirrored_table, table_grad).astype(jnp.bfloat16)
     grad_rel = jnp.moveaxis(grad_rel.reshape(rel_rows, groups, rel_columns), 0, 1)
-    grad_rel = grad_rel.reshape(groups, 2, rel_rows // 2, rel_columns).astype(jnp.bfloat16)
+    grad_rel = grad_rel.reshape(groups, 2, rel_rows // 2, rel_columns)
     mixed_wide = jnp.pad(mixed_grad, ((0, 0), (0, model_width - 2 * key_width)))
     lefts = [activated, normed_one, attended, normed_two, hidden[0], hidden[1]]
-    rights = [mixed_wide, value_grad, branch_grad, pre_grad[0], pre_grad[1], cotangent]
-    lefts_sib = [exchange(left) for left in lefts]
-    rights_own = [own_half(right) for right in rights]
-    rights_sib = [sib_half(right) for right in rights]
-
-    def shifted(array):
-        padded = jnp.pad(array, ((half_taps, half_taps), (0, 0)))
-        return jnp.stack([padded[tap : tap + length] for tap in reversed(range(tap_count))])
-
-    pieces, sums = reduce(
-        groups,
-        blocks,
-        2 * key_width - half_width,
-        lefts,
-        lefts_sib,
-        shifted(own_half(conv_grad)),
-        shifted(sib_half(conv_grad)),
-        rights_own + rights_own[5:],
-        rights_sib + rights_sib[5:],
-        grad_rel,
-        sums,
+    rights = [
+        conv_grad,
+        mixed_wide,
+        value_grad,
+        branch_grad,
+        pre_grad[0],
+        pre_grad[1],
+        cotangent,
+    ]
+    pieces, sums, _, _ = reduce(
+        groups, blocks, 2 * key_width - half_width, lefts, rights, grad_rel, sums
     )
     flat = sums.reshape(-1)
     bn_sums = flat[: 4 * model_width].reshape(4, model_width)

time: 1000 us -> 791 us (0.79)
  local copies, waits for them, and re-layouts: 260 us -> 68.1 us
  matrix products: 153 us -> 92.1 us
  Pallas kernels: 507 us -> 566 us
  other arithmetic: 62.3 us -> 51.4 us
    reshape x4 -> x1, local copies, waits for them, and re-layouts: 72.3 us -> 0.71 us  [on_device(): grad_rel.reshape(rel_rows, groups, rel_columns)]
    pallas_call x0 -> x3, Pallas kernels: none -> 49.6 us  [the longest x1 18.1 us: attend_back(): pl.pallas_call(attend_back_kernel, grid=(steps,), in_specs=[pl.BlockSpec(...]
    dot_general x10 -> x2, matrix products: 38.4 us -> 0.93 us  [on_device(): jnp.dot(side, rel_full, preferred_element_type=jnp.float32)]
    unnamed x308 -> x221, local copies, waits for them, and re-layouts: 80 us -> 42.7 us
    slice x6 -> x2, local copies, waits for them, and re-layouts: 38.2 us -> 1.3 us  [the longest x1 1.29 us: on_device(): keys = mixed_raw[:, key_width:].astype(jnp.bfloat16)]
    dot_general x12 -> x7, matrix products: 50.5 us -> 27 us  [dot_trailing(): lax.dot_general(left_side, right_side, (((1,), (1,)), ((), ())), preferre...]
    pad x3 -> x1, local copies, waits for them, and re-layouts: 22.7 us -> 2.47 us  [on_device(): mixed_wide = jnp.pad(mixed_grad, ((0, 0), (0, model_width - 2 * key_width)))]
    dynamic_slice x7 -> x0, local copies, waits for them, and re-layouts: 10.2 us -> none  [sib_half(): lax.dynamic_slice_in_dim(array, (1 - core) * half_width, half_width, 1)]
  transfers between devices with their start and end apart: 14 -> 0, of which waited for: 0 -> 0; matrix products, arithmetic and copies ran while one was open for 25% -> 0% of each run, Pallas kernels for 0% -> 0%
where the time goes in v3:
time: 791 us; the launch traced here: 781 us
  Pallas kernels  566 us (72%)
  matrix products  92.1 us (12%)
  local copies, waits for them, and re-layouts  68.1 us (9%)
  other arithmetic  51.4 us (6%)
    pallas_call x1, Pallas kernels, reduce(): pl.pallas_call(functools.partial(reduce_kernel, groups, blocks, rel_at),...  318 us
    pallas_call x1, Pallas kernels, gather(): pl.pallas_call(functools.partial(gather_kernel, groups, blocks), out_shap...  198 us
    unnamed x221, local copies, waits for them, and re-layouts  42.7 us
    dot_general x7, matrix products, dot_trailing(): lax.dot_general(left_side, right_side, (((1,), (1,)), ((), ())), preferre...  27 us
    dot_general x1, matrix products, on_device(): jnp.dot(stacked, conv_full.reshape(-1, model_width), preferred_element_ty...  18.6 us
    pallas_call x1, Pallas kernels, attend_back(): pl.pallas_call(attend_back_kernel, grid=(steps,), in_specs=[pl.BlockSpec(...  18.1 us
    pallas_call x1, Pallas kernels, conv_back(): pl.pallas_call(conv_back_kernel, grid=(taps,), in_specs=[pl.BlockSpec((le...  16.3 us

profile of v3, /device:TPU:0, one launch (start us, length us, event | category | flops | bytes accessed | tf_op | source)
XLA Modules:
  0.0 780.9 jit_solution(12961939893665703947)
XLA Ops:
  1.6 1.4 reshape.295
  3.7 1.7 convert_reduce_fusion.1
  5.4 1.8 fusion.6
  7.2 1.7 copy-done.3
  8.9 1.3 copy-done.6
  10.1 1.3 copy-done.7
  11.4 198.2 %gather.1 = (bf16[5,4,384,1536]{3,2,1,0:T(8,128)(2,1)}, bf16[4,384,1024]{2,1,0:T(8,128)(2,1)S(1)}, bf16[4,384,1536]{2,1,0:T(8,128)(2,1)S(1)}, bf16[4,384,1536]{2...) custom-call(bf16[5,384,1536]{2,1,0:T(8,128)(2,1)} %refs_0_.1, ...), custom_call_target="tpu_custom_call" | custom-call | tf_op jit(solution)/shard_map/gather/pallas_call | solution.py:342
  210.3 2.2 copy-done.13
  212.5 2.2 copy-done.14
  214.7 2.2 copy-done.15
  216.9 2.2 copy-done.16
  219.1 1.6 copy-done.17
  222.1 2.9 fusion.17.refs_0_
  225.8 1.2 copy-done.26
  227.0 1.5 constant_dynamic-update-slice_fusion
  229.2 3.2 copy-done.48
  232.4 18.6 %fusion.110 = (f32[512]{0:T(512)S(1)}, f32[512,1536]{1,0:T(8,128)S(1)}) fusion(f32[1536]{0:T(1024)S(1)} %add.280, bf16[512,7680]{1,0:T(8,128)(2,1)} %copy-done.48, bf16[7680,1536]{1,0:T(8,128)(2,1)} %bitcast.257, bf16[1,512,1536]{2,1,0:T(8,128)(2,1)S(1)} %copy-done.26), kind=kOutput, calls=%fused_computation.247 | convolution fusion | flops 12082741248 | bytes 36184064 | tf_op jit(solution)/shard_map/dot_general | solution.py:1091
  251.1 1.6 copy-done.31
  253.2 2.5 add_convert_fusion.1.refs_1_
  255.7 6.6 convolution_convert_fusion.1.value_ref
  262.3 3.1 fusion.112
  265.5 1.4 add_convert_fusion.2
  266.9 1.3 slice.329.key_ref
  272.3 15.1 %attend.1 = (bf16[512,1536]{1,0:T(8,128)(2,1)S(1)}, bf16[8,512,512]{2,1,0:T(8,128)(2,1)S(1)}) custom-call(bf16[512,512]{1,0:T(8,128)(2,1)S(1)} %get-tuple-element.96.content_ref, bf16[512,512]{1,0:T(8,128)(2,1)S(1)} %get-tuple-element.95.position_ref, bf16[512,512]{1,0:T(8,128)(2,1)S(1)} %slice.329.key_ref, bf16[512,1536]{1,0:T(8,128)(2,1)S(1)} %copy-done.22, ...), custom_call_target="tpu_custom_call" | custom-call | flops 1610612736 | bytes 4194304 | tf_op jit(solution)/shard_map/attend/pallas_call | solution.py:877
  287.4 2.0 copy-done.20
  289.4 1.3 add.295
  290.7 6.0 fusion.111
  296.8 1.6 copy-done.28
  300.1 2.5 add_convert_fusion.refs_3_
  302.6 1.3 slice.278
  303.9 1.3 reshape.307
  305.2 1.4 slice_reduce_fusion.1
  306.7 1.3 add.308
  308.0 7.4 multiply_convert_fusion
  315.4 1.3 add.302
  316.7 7.4 multiply_convert_fusion.1
  324.1 7.2 convolution_add_fusion.4
  331.3 1.3 add.314
  334.1 7.4 convert_reduce_fusion
  341.6 7.8 convert_reduce_fusion.2
  349.4 5.0 convert_reduce_fusion.3
  354.5 1.1 copy-done.44
  355.6 2.6 fusion.113
  358.4 3.8 multiply_reduce_fusion
  362.2 2.7 convert_reduce_fusion.4
  365.0 2.6 convolution_convert_fusion.out_ref
  368.3 1.5 copy-done.21
  369.9 18.1 %attend_back.1 = (bf16[512,512]{1,0:T(8,128)(2,1)S(1)}, bf16[512,512]{1,0:T(8,128)(2,1)S(1)}, bf16[512,1536]{1,0:T(8,128)(2,1)S(1)}, bf16[1024,512]{1,0:T(8,128)(2,1)S(1)}, f32[2,512]{1,0:T(2,128)S(1)}) custom-call(bf16[8,512,512]{2,1,0:T(8,128)(2,1)S(1)} %copy-done.21, bf16[512,1536]{1,0:T(8,128)(2,1)S(1)} %convolution_convert_fusion.out_ref, ...), custom_call_target="tpu_custom_call" | custom-call | flops 3221225472 | bytes 4194304 | tf_op jit(solution)/shard_map/attend_back/pallas_call | solution.py:951
  388.2 1.8 fusion.114
  390.1 1.1 slice-done.1
  392.1 3.2 multiply_reduce_fusion.1
  395.4 2.4 convert_reduce_fusion.5
  399.4 16.3 %conv_back.1 = f32[512,1536]{1,0:T(8,128)S(1)} custom-call(bf16[512,7680]{1,0:T(8,128)(2,1)S(1)} %slice_dynamic-update-slice_fusion.left_ref, bf16[5,1536,1536]{2,1,0:T(8,128)(2,1)} %bitcast.258), custom_call_target="tpu_custom_call" | custom-call | flops 12079595520 | bytes 31457280 | tf_op jit(solution)/shard_map/conv_back/pallas_call | solution.py:983
  415.9 4.1 fusion.103
  420.8 2.5 pad.33.refs_7_
  424.4 318.2 %reduce.20 = (bf16[12,384,1536]{2,1,0:T(8,128)(2,1)}, f32[144,128]{1,0:T(8,128)}, bf16[6,512,1536]{2,1,0:T(8,128)(2,1)}, bf16[7,512,768]{2,1,0:T(8,128)(2,1)}) custom-call(bf16[512,1536]{1,0:T(8,128)(2,1)} %copy-done.25, bf16[512,1536]{1,0:T(8,128)(2,1)} %copy-done.36, bf16[512,1536]{1,0:T(8,128)(2,1)} %copy-done.4, bf16[512,1536]{1,0:T(8,128)(2,1)} %copy-done.37, ...), custom_call_target="tpu_custom_call" | custom-call | tf_op jit(solution)/shard_map/reduce/pallas_call | solution.py:754
  750.9 2.8 convert_element_type.172
  753.6 8.8 %slice_convert_fusion = f32[5,384,1536]{2,1,0:T(8,128)} fusion(bf16[12,384,1536]{2,1,0:T(8,128)(2,1)} %get-tuple-element.55), kind=kLoop, calls=%fused_computation | loop fusion | flops 2949120 | bytes 17694720 | tf_op jit(solution)/shard_map/convert_element_type | solution.py:1235
  762.5 4.9 bitcast_convert_fusion.1
  767.4 1.3 fusion.107
  769.3 1.8 slice.255
  771.1 3.2 bitcast_convert_fusion
  774.3 1.3 copy-done.34
  775.7 2.3 fusion.45
  (281 shorter events, 28.7 us)
Async XLA Ops:
  0.6 332.6 %copy-start = (f32[64,1536]{1,0:T(8,128)S(1)}, f32[64,1536]{1,0:T(8,128)}, u32[]{:S(2)}) copy-start(f32[64,1536]{1,0:T(8,128)} %param.34) | copy-start | bytes 1179652
  0.7 6.5 copy-start.8
  0.7 6.5 copy-start.9
  0.7 6.5 copy-start.2
  3.0 4.2 copy-start.12
  220.7 44.7 %copy-start.49 = (f32[1,4,40,128]{3,1,2,0:T(4,128)}, f32[1,4,40,128]{3,1,2,0:T(4,128)S(1)}, u32[]{:S(2)}) copy-start(f32[1,4,40,128]{3,1,2,0:T(4,128)S(1)} %copy.49) | copy-start | bytes 245764
  221.4 4.3 copy-start.56
  222.1 3.7 copy-start.50
  222.1 3.7 copy-start.52
  222.1 3.7 copy-start.54
  225.0 3.8 copy-start.25
  229.2 3.2 copy-start.48
  251.1 4.6 copy-start.72
  253.2 9.2 %copy-start.76 = (f32[512]{0:T(512)}, f32[512]{0:T(512)S(1)}, u32[]{:S(2)}) copy-start(f32[512]{0:T(512)S(1)} %add_rsqrt_fusion.1) | copy-start | bytes 6148
  255.7 6.6 copy-start.36
  255.7 6.6 copy-start.18
  265.4 5.7 copy-start.11
  289.4 7.3 copy-start.4
  296.8 3.3 copy-start.74
  296.8 3.3 copy-start.70
  302.6 14.1 %copy-start.37 = (bf16[512,1536]{1,0:T(8,128)(2,1)}, bf16[512,1536]{1,0:T(8,128)(2,1)S(1)}, u32[]{:S(2)}) copy-start(bf16[512,1536]{1,0:T(8,128)(2,1)S(1)} %add_convert_fusion.refs_3_) | copy-start | bytes 4718596
  316.7 7.4 copy-start.29
  324.1 7.2 copy-start.42
  324.1 10.0 %copy-start.41 = (bf16[512,1536]{1,0:T(8,128)(2,1)S(1)}, bf16[512,1536]{1,0:T(8,128)(2,1)}, u32[]{:S(2)}) copy-start(bf16[512,1536]{1,0:T(8,128)(2,1)} %get-tuple-element.134.refs_5_) | copy-start | bytes 4718596
  334.1 7.5 copy-start.83
  334.1 15.3 %slice-start.8 = ((s8[4718592]{0:T(1024)(128)(4,1)}), s8[4194304]{0:T(1024)(128)(4,1)S(1)}, s32[]{:S(2)}) async-start(s8[4718592]{0:T(1024)(128)(4,1)} %bitcast.260), calls=%async_computation.8 | async-start | bytes 8388608
  341.6 20.7 %copy-start.38 = (bf16[512,1536]{1,0:T(8,128)(2,1)}, bf16[512,1536]{1,0:T(8,128)(2,1)S(1)}, u32[]{:S(2)}) copy-start(bf16[512,1536]{1,0:T(8,128)(2,1)S(1)} %get-tuple-element.81.refs_12_) | copy-start | bytes 4718596
  341.6 7.8 %slice-start.9 = ((s8[4718592]{0:T(1024)(128)(4,1)}), s8[524288]{0:T(1024)(128)(4,1)S(1)}, s32[]{:S(2)}) async-start(s8[4718592]{0:T(1024)(128)(4,1)} %bitcast.260), calls=%async_computation.9 | async-start | bytes 1048576
  341.6 7.8 %copy-start.84 = (f32[512,1536]{1,0:T(8,128)S(1)}, f32[512,1536]{1,0:T(8,128)}, u32[]{:S(2)}) copy-start(f32[512,1536]{1,0:T(8,128)} %get-tuple-element.133) | copy-start | bytes 9437188
  341.6 14.0 %slice-start.6 = ((s8[4718592]{0:T(1024)(128)(4,1)}), s8[4194304]{0:T(1024)(128)(4,1)S(1)}, s32[]{:S(2)}) async-start(s8[4718592]{0:T(1024)(128)(4,1)} %bitcast.232), calls=%async_computation.6 | async-start | bytes 8388608
  341.6 16.7 %slice-start.4 = ((s8[4718592]{0:T(1024)(128)(4,1)}), s8[4194304]{0:T(1024)(128)(4,1)S(1)}, s32[]{:S(2)}) async-start(s8[4718592]{0:T(1024)(128)(4,1)} %bitcast.228), calls=%async_computation.4 | async-start | bytes 8388608
  349.4 8.9 %copy-start.43 = (bf16[512,1536]{1,0:T(8,128)(2,1)}, bf16[512,1536]{1,0:T(8,128)(2,1)S(1)}, u32[]{:S(2)}) copy-start(bf16[512,1536]{1,0:T(8,128)(2,1)S(1)} %get-tuple-element.77.refs_11_) | copy-start | bytes 4718596
  349.4 6.2 slice-start.7
  349.4 8.9 %slice-start.5 = ((s8[4718592]{0:T(1024)(128)(4,1)}), s8[524288]{0:T(1024)(128)(4,1)S(1)}, s32[]{:S(2)}) async-start(s8[4718592]{0:T(1024)(128)(4,1)} %bitcast.228), calls=%async_computation.5 | async-start | bytes 1048576
  355.6 9.3 %slice-start.2 = ((s8[4718592]{0:T(1024)(128)(4,1)}), s8[4194304]{0:T(1024)(128)(4,1)S(1)}, s32[]{:S(2)}) async-start(s8[4718592]{0:T(1024)(128)(4,1)} %bitcast.224), calls=%async_computation.2 | async-start | bytes 8388608
  358.4 6.6 slice-start.3
  365.0 2.8 copy-start.59
  365.0 2.8 copy-start.60
  365.0 2.8 copy-start.61
  365.0 2.8 copy-start.63
  365.0 2.8 copy-start.65
  365.0 2.8 copy-start.67
  365.0 3.3 copy-start.23
  369.9 18.3 %copy-start.19 = (bf16[4,384,1024]{2,1,0:T(8,128)(2,1)S(1)}, bf16[4,384,1024]{2,1,0:T(8,128)(2,1)}, u32[]{:S(2)}) copy-start(bf16[4,384,1024]{2,1,0:T(8,128)(2,1)} %copy-done.17) | copy-start | bytes 9437188
  369.9 20.2 %slice-start = ((s8[4718592]{0:T(1024)(128)(4,1)}), s8[524288]{0:T(1024)(128)(4,1)S(1)}, s32[]{:S(2)}) async-start(s8[4718592]{0:T(1024)(128)(4,1)} %bitcast.220), calls=%async_computation | async-start | bytes 1048576
  388.0 3.1 slice-start.1
  388.2 3.9 copy-start.32
  388.2 3.9 copy-start.73
  388.2 3.9 copy-start.77
  392.1 3.2 copy-start.35
  399.4 16.4 %copy-start.27 = (bf16[1,512,1536]{2,1,0:T(8,128)(2,1)S(1)}, bf16[1,512,1536]{2,1,0:T(8,128)(2,1)}, u32[]{:S(2)}) copy-start(bf16[1,512,1536]{2,1,0:T(8,128)(2,1)} %param.21) | copy-start | bytes 4718596
  399.4 16.4 %copy-start.51 = (f32[1536]{0:T(1024)S(1)}, f32[1536]{0:T(1024)}, u32[]{:S(2)}) copy-start(f32[1536]{0:T(1024)} %copy-done.50) | copy-start | bytes 18436
  399.4 16.4 %copy-start.53 = (f32[1536]{0:T(1024)S(1)}, f32[1536]{0:T(1024)}, u32[]{:S(2)}) copy-start(f32[1536]{0:T(1024)} %copy-done.52) | copy-start | bytes 18436
  399.4 16.4 %copy-start.55 = (f32[1536]{0:T(1024)S(1)}, f32[1536]{0:T(1024)}, u32[]{:S(2)}) copy-start(f32[1536]{0:T(1024)} %copy-done.54) | copy-start | bytes 18436
  399.4 16.4 %copy-start.57 = (f32[1536]{0:T(1024)S(1)}, f32[1536]{0:T(1024)}, u32[]{:S(2)}) copy-start(f32[1536]{0:T(1024)} %copy-done.56) | copy-start | bytes 18436
  415.8 4.2 copy-start.82
  415.8 4.2 copy-start.81
  415.8 4.3 copy-start.78
  415.8 4.3 copy-start.80
  415.8 4.3 copy-start.79
  771.1 3.2 copy-start.58
  771.1 3.2 copy-start.33
  771.1 4.6 copy-start.34
  774.3 6.2 copy-start.1
  (31 other events, 57.7 us)

commit v4 on v3

--- a/solution.py
+++ b/solution.py
@@ -141,14 +141,20 @@
 def gather_kernel(groups, blocks, *refs):
     weights = refs[:8]
     conv, query, key, value, out, up, down, rel = weights
-    small, stats = refs[8:10]
-    outs = refs[10:21]
-    rel_full, small_full, stat_total = outs[8:]
-    hold, hold_mixed, local_sem, write_sem = refs[21:25]
-    z_sem, x_sem, y_sem, d_sem, sib_sem, send_sem, right_send, left_send = refs[25:33]
-    rel_send, rel_recv, small_send, small_recv = refs[33:37]
-    near_got, sums, shard_got, block_got = refs[37:41]
-    sum_sems = refs[41:47]
+    small, stats, inputs, tables = refs[8:12]
+    outs = refs[12:21]
+    conv_out, mixed_out, value_out, out_out, up_out, down_out = outs[:6]
+    rel_full, small_full, stat_total = outs[6:]
+    results = refs[21:33]
+    hold, hold_mixed, local_sem, write_sem = refs[33:37]
+    z_sem, x_sem, y_sem, d_sem, sib_sem, send_sem, right_send, left_send = refs[37:45]
+    rel_send, rel_recv, small_send, small_recv = refs[45:49]
+    near_got, sums, shard_got, block_got = refs[49:53]
+    sum_sems = refs[53:59]
+    weight_hold, weight_sem, result_sem = refs[59:62]
+    params, shifted_ref, total_ref = refs[62:65]
+    act_ref, norm_ref, content_ref, position_ref, key_ref, value_ref = refs[65:71]
+    table_ref, probs_ref, attended_ref = refs[71:74]
     dp = lax.axis_index("dp")
     me = lax.axis_index("fsdp")
     near, shards, far = peers_of(groups, blocks)
@@ -156,7 +162,10 @@
     rows = conv.shape[1]
     part = rows // 8
     others = groups - 1
-    pieces = [outs[0].at[tap] for tap in range(5)] + list(outs[1:8])
+    columns = conv.shape[2]
+    pieces = [conv_out.at[tap] for tap in range(5)] + [mixed_out, value_out, out_out]
+    pieces += [up_out.at[:, :, pl.ds(half * columns, columns)] for half in range(2)]
+    pieces += [down_out.at[:, pl.ds(half * rows, rows)] for half in range(2)]
     count = len(pieces)
     holds = [hold.at[i] for i in range(5)] + [hold_mixed] + [hold.at[i] for i in range(5, 11)]
 
@@ -177,12 +186,7 @@
     load(value, holds[6], 6)
     load(out, holds[7], 7)
     for half in range(2):
-        for shard in range(groups):
-            load(
-                up.at[:, pl.ds((shard * 2 + half) * rows, rows)],
-                holds[8 + half].at[:, pl.ds(shard * rows, rows)],
-                8 + half,
-            )
+        load(up.at[:, pl.ds(half * columns, columns)], holds[8 + half], 8 + half)
     for half in range(2):
         load(down.at[pl.ds(half * rows, rows)], holds[10 + half], 10 + half)
 
@@ -251,8 +255,8 @@
 
     diagonal = neighbours(along_x)[2]
 
-    def stage_a(piece):
-        for shard in order:
+    def stage_a(piece, shards_now):
+        for shard in shards_now:
             copy_of(piece, shard, dp, z_sem.at[piece, shard], dp).wait_recv()
 
             @pl.when(jnp.logical_and(shard < me, me + 1 < groups))
@@ -267,8 +271,8 @@
             copy_of(piece, shard, dp, y_sem.at[piece, shard], along_y).start()
             copy_of(piece, shard, dp, sib_sem.at[piece], sib).start()
 
-    def stage_b(piece):
-        for shard in order:
+    def stage_b(piece, shards_now):
+        for shard in shards_now:
             route = (piece + shard) % 2
             copy_of(piece, shard, along_x, x_sem.at[piece, shard], dp).wait_recv()
             copy_of(piece, shard, along_y, y_sem.at[piece, shard], dp).wait_recv()
@@ -278,8 +282,8 @@
             copy_of(piece, shard, along_x, sib_sem.at[piece], sib).start()
             copy_of(piece, shard, along_y, sib_sem.at[piece], sib).start()
 
-    def stage_c(piece):
-        for shard in order:
+    def stage_c(piece, shards_now):
+        for shard in shards_now:
             copy_of(piece, shard, diagonal, d_sem.at[piece, shard], dp).wait_recv()
             copy_of(piece, shard, diagonal, sib_sem.at[piece], sib).start()
 
@@ -293,17 +297,271 @@
         if piece < AHEAD:
             z_send(piece)
 
-    for n in range(count + 2):
+    def complete(piece):
+        writes[piece].wait()
+        got = pieces[piece].at[pl.ds(0, others), pl.ds(0, 4 * part)]
+        remote(got, got, send_sem.at[piece], sib_sem.at[piece], (sib, me)).wait_recv()
+
+    def weight_loads(piece):
+        width = pieces[piece].shape[2]
+        return [
+            pltpu.make_async_copy(
+                pieces[piece].at[shard],
+                weight_hold.at[piece % 2, pl.ds(shard * rows, rows), pl.ds(0, width)],
+                weight_sem.at[piece % 2, shard],
+            )
+            for shard in range(groups)
+        ]
+
+    def start_weight(piece):
+        for copy in weight_loads(piece):
+            copy.start()
+
+    def wait_weight(piece):
+        for copy in weight_loads(piece):
+            copy.wait()
+
+    def wait_smalls():
+        for j in range(others):
+            shard = (me + 1 + j) % groups
+            remote(
+                rel, rel_full.at[shard], rel_send.at[j], rel_recv.at[shard], shards[j]
+            ).wait()
+            remote(
+                small, small_full.at[shard], small_send.at[j], small_recv.at[shard], shards[j]
+            ).wait()
+
+    length = inputs.shape[0]
+    block_rows = 128
+    tile = 512
+    per_row = rows // 128
+    token_total = length * 8 * blocks * groups
+
+    def by_rows(fn):
+        def row_body(i, carry):
+            fn(pl.ds(pl.multiple_of(i * block_rows, block_rows), block_rows))
+            return carry
+
+        lax.fori_loop(0, length // block_rows, row_body, 0)
+
+    def unpack():
+        for row in range(9):
+            for shard in range(groups):
+                for j in range(per_row):
+                    at = shard * rows + j * 128
+                    source = row * per_row + j
+                    params[row : row + 1, at : at + 128] = small_full[
+                        shard, source : source + 1, :
+                    ]
+        lanes = columns // 128
+        for j in range(lanes):
+            centre = stat_total[j : j + 1, :] / token_total
+            square = stat_total[lanes + j : lanes + j + 1, :] / token_total
+            params[9:10, j * 128 : (j + 1) * 128] = centre
+            params[10:11, j * 128 : (j + 1) * 128] = lax.rsqrt(
+                square - centre * centre + EPSILON
+            )
+        taken = (9 * rows + 2 * rows) // 128
+        for side in range(2):
+            for shard in range(groups):
+                params[11 + side : 12 + side, shard * 128 : (shard + 1) * 128] = small_full[
+                    shard, taken + side : taken + side + 1, :
+                ]
+
+    def activate():
+        def rows_fn(at):
+            standard = (inputs[at, :].astype(jnp.float32) - params[9:10, :]) * params[10:11, :]
+            act_ref[at, :] = jax.nn.gelu(standard * params[0:1, :] + params[3:4, :]).astype(
+                act_ref.dtype
+            )
+
+        by_rows(rows_fn)
+
+    result_of = [
+        act_ref,
+        total_ref,
+        norm_ref,
+        content_ref,
+        position_ref,
+        key_ref,
+        value_ref,
+        table_ref.at[1],
+        probs_ref,
+        attended_ref,
+        total_ref,
+        norm_ref,
+    ]
+
+    def write_result(index):
+        return pltpu.make_async_copy(result_of[index], results[index], result_sem.at[index])
+
+    def shift_tap(tap):
+        move = tap - 2
+
+        def column_body(i, carry):
+            at = pl.ds(pl.multiple_of(i * rows, 128), rows)
+            value = act_ref[:, at].astype(jnp.float32)
+            value = pltpu.roll(value, -move % length, 0)
+            row = lax.broadcasted_iota(jnp.int32, value.shape, 0)
+            inside = row < length - move if move > 0 else row >= -move
+            shifted_ref[:, at] = jnp.where(inside, value, 0.0).astype(shifted_ref.dtype)
+            return carry
+
+        lax.fori_loop(0, columns // rows, column_body, 0)
+
+    def conv_tap(tap, i):
+        at = pl.ds(i * tile, tile)
+        left = act_ref if tap == 2 else shifted_ref
+        value = jnp.dot(
+            left[...], weight_hold[tap % 2, :, at], preferred_element_type=jnp.float32
+        )
+        if tap == 0:
+            value = value + (inputs[:, at].astype(jnp.float32) + params[4:5, at])
+        else:
+            value = value + total_ref[:, at]
+        total_ref[:, at] = value
+
+    def norm_step(gain, bias):
+        def rows_fn(at):
+            standard, _ = normalize(total_ref[at, :])
+            norm_ref[at, :] = (
+                standard * params[gain : gain + 1, :] + params[bias : bias + 1, :]
+            ).astype(norm_ref.dtype)
+
+        by_rows(rows_fn)
+
+    def query_step():
+        raw = jnp.dot(
+            norm_ref[...], weight_hold[1, :, 0:width], preferred_element_type=jnp.float32
+        )
+        raw = raw * KEY**-0.5
+        content_ref[...] = (raw + params[11:12, 0:width]).astype(content_ref.dtype)
+        position_ref[...] = (raw + params[12:13, 0:width]).astype(position_ref.dtype)
+
+    def key_step():
+        key_ref[...] = jnp.dot(
+            norm_ref[...], weight_hold[1, :, width : 2 * width], preferred_element_type=jnp.float32
+        ).astype(key_ref.dtype)
+
+    def table_step():
+        for side in range(2):
+            for shard in range(groups):
+                table_ref[side, :, shard * 128 : (shard + 1) * 128] = jnp.dot(
+                    tables[side], rel_full[shard], preferred_element_type=jnp.float32
+                ).astype(table_ref.dtype)
+
+    def value_step(i):
+        at = pl.ds(i * tile, tile)
+        value_ref[:, at] = jnp.dot(
+            norm_ref[...], weight_hold[0, :, at], preferred_element_type=jnp.float32
+        ).astype(value_ref.dtype)
+
+    def head_step(head):
+        head_value = columns // HEADS
+        span = tables.shape[1]
+        pair = slice(head // 2 * 2 * KEY, (head // 2 + 1) * 2 * KEY)
+        value_pair = slice(head // 2 * 2 * head_value, (head // 2 + 1) * 2 * head_value)
+        keys = slice(head % 2 * KEY, (head % 2 + 1) * KEY)
+        band = dot_trailing(position_ref[:, pair][:, keys], table_ref[0, :, pair][:, keys])
+        moved = pltpu.roll(band, span - length + 1, 1, stride=1, stride_axis=0)
+        scores = dot_trailing(content_ref[:, pair][:, keys], key_ref[:, pair][:, keys])
+        scores = scores + moved[:, :length]
+        weight = jnp.exp(scores - jnp.max(scores, -1, keepdims=True))
+        probs = (weight / jnp.sum(weight, -1, keepdims=True)).astype(probs_ref.dtype)
+        probs_ref[head] = probs
+        chosen = value_ref[:, value_pair][
+            :, head % 2 * head_value : (head % 2 + 1) * head_value
+        ]
+        return jnp.dot(probs, chosen, preferred_element_type=jnp.float32)
+
+    def pair_step(index):
+        both = [head_step(2 * index + side).astype(attended_ref.dtype) for side in range(2)]
+        wide = 2 * columns // HEADS
+        attended_ref[:, index * wide : (index + 1) * wide] = jnp.concatenate(both, 1)
+
+    def out_step(i):
+        at = pl.ds(i * tile, tile)
+        value = jnp.dot(
+            attended_ref[...], weight_hold[1, :, at], preferred_element_type=jnp.float32
+        )
+        total_ref[:, at] = total_ref[:, at] + value + params[6:7, at]
+
+    tiles = range(columns // tile)
+
+    def compute_list(n):
+        if n == 2:
+            return [wait_smalls, unpack, activate, lambda: write_result(0).start()]
+        piece = n - 4
+        if 0 <= piece < 5:
+            work = [functools.partial(wait_weight, piece)]
+            if piece != 2:
+                work.append(functools.partial(shift_tap, piece))
+            work += [functools.partial(conv_tap, piece, i) for i in tiles]
+            return work
+        if piece == 5:
+            return [
+                lambda: write_result(1).start(),
+                functools.partial(norm_step, 1, 5),
+                lambda: write_result(2).start(),
+                table_step,
+                lambda: write_result(7).start(),
+                functools.partial(wait_weight, piece),
+                query_step,
+                key_step,
+                lambda: [write_result(i).start() for i in (3, 4, 5)],
+            ]
+        if piece == 6:
+            work = [functools.partial(wait_weight, piece)]
+            work += [functools.partial(value_step, i) for i in tiles]
+            work += [lambda: write_result(6).start(), functools.partial(pair_step, 0)]
+            return work + [functools.partial(pair_step, 1)]
+        if piece == 7:
+            work = [functools.partial(pair_step, 2), functools.partial(pair_step, 3)]
+            work += [lambda: [write_result(i).start() for i in (8, 9)]]
+            work += [functools.partial(wait_weight, piece), lambda: write_result(1).wait()]
+            work += [functools.partial(out_step, i) for i in tiles]
+            work += [lambda: write_result(10).start(), lambda: write_result(2).wait()]
+            return work + [
+                functools.partial(norm_step, 2, 7),
+                lambda: write_result(11).start(),
+            ]
+        return []
+
+    def send_list(n):
+        work = []
         if n + AHEAD < count:
-            z_send(n + AHEAD)
-        if n < count:
-            stage_a(n)
-        if 1 <= n <= count:
-            stage_b(n - 1)
-        if n >= 2:
-            stage_c(n - 2)
-        if 1 <= n < len(summing):
-            summing[n]()
+            work.append(functools.partial(z_send, n + AHEAD))
+        for shard in order:
+            if n < count:
+                work.append(functools.partial(stage_a, n, [shard]))
+            if 1 <= n <= count:
+                work.append(functools.partial(stage_b, n - 1, [shard]))
+            if 2 <= n < count + 2:
+                work.append(functools.partial(stage_c, n - 2, [shard]))
+        return work
+
+    for step in summing[1:4]:
+        step()
+
+    for n in range(count + 3):
+        sends = send_list(n)
+        work = compute_list(n)
+        if 0 <= n - 3 < count:
+            complete(n - 3)
+            if n - 3 < 8:
+                start_weight(n - 3)
+        slots = max(len(work), 1)
+        for i in range(slots):
+            for send in sends[len(sends) * i // slots : len(sends) * (i + 1) // slots]:
+                send()
+            if i < len(work):
+                work[i]()
+        if n < 2:
+            summing[4 + n]()
+
+    for index in range(len(results)):
+        if index not in (1, 2):
+            write_result(index).wait()
 
     for piece in range(count):
         for shard in range(groups):
@@ -316,45 +574,59 @@
             def _():
                 left_copy(piece, shard).wait_send()
 
-        writes[piece].wait()
-        got = pieces[piece].at[pl.ds(0, others), pl.ds(0, 4 * part)]
-        remote(got, got, send_sem.at[piece], sib_sem.at[piece], (sib, me)).wait_recv()
         sent = pieces[piece].at[pl.ds(0, others), pl.ds(0, 7 * part)]
         remote(sent, sent, send_sem.at[piece], sib_sem.at[piece], (sib, me)).wait_send()
-    for j in range(others):
-        shard = (me + 1 + j) % groups
-        remote(rel, rel_full.at[shard], rel_send.at[j], rel_recv.at[shard], shards[j]).wait()
-        remote(
-            small, small_full.at[shard], small_send.at[j], small_recv.at[shard], shards[j]
-        ).wait()
-
-
-def gather(groups, blocks, weights, small, stats):
+
+
+def gather(groups, blocks, weights, small, stats, inputs, tables):
     conv, query = weights[:2]
     rel = weights[7]
     taps, rows, columns = conv.shape
+    width = query.shape[1]
+    length = inputs.shape[0]
+    span = tables.shape[1]
     dtype = conv.dtype
     kept = pl.BlockSpec(memory_space=pl.ANY)
     inside = pl.BlockSpec(memory_space=pltpu.VMEM)
     full = jax.ShapeDtypeStruct((groups, rows, columns), dtype)
     count = taps + 7
     grid_sems = [pltpu.SemaphoreType.DMA((count, groups))] * 4
+    wide = (length, columns)
+    narrow = (length, width)
+    made = [
+        jax.ShapeDtypeStruct(wide, dtype),
+        jax.ShapeDtypeStruct(wide, jnp.float32),
+        jax.ShapeDtypeStruct(wide, dtype),
+        jax.ShapeDtypeStruct(narrow, dtype),
+        jax.ShapeDtypeStruct(narrow, dtype),
+        jax.ShapeDtypeStruct(narrow, dtype),
+        jax.ShapeDtypeStruct(wide, dtype),
+        jax.ShapeDtypeStruct((span, width), dtype),
+        jax.ShapeDtypeStruct((HEADS, length, length), dtype),
+        jax.ShapeDtypeStruct(wide, dtype),
+        jax.ShapeDtypeStruct(wide, jnp.float32),
+        jax.ShapeDtypeStruct(wide, dtype),
+    ]
     return pl.pallas_call(
         functools.partial(gather_kernel, groups, blocks),
         out_shape=(
             jax.ShapeDtypeStruct((taps, groups, rows, columns), dtype),
-            jax.ShapeDtypeStruct((groups, rows, 2 * query.shape[1]), dtype),
-            *([full] * 6),
+            jax.ShapeDtypeStruct((groups, rows, 2 * width), dtype),
+            full,
+            full,
+            jax.ShapeDtypeStruct((groups, rows, 2 * columns), dtype),
+            jax.ShapeDtypeStruct((groups, 2 * rows, columns), dtype),
             jax.ShapeDtypeStruct((groups,) + rel.shape, dtype),
             jax.ShapeDtypeStruct((groups,) + small.shape, jnp.float32),
             jax.ShapeDtypeStruct(stats.shape, jnp.float32),
+            *made,
         ),
-        in_specs=[kept] * 7 + [inside] * 3,
-        out_specs=[kept] * 8 + [inside] * 3,
+        in_specs=[kept] * 7 + [inside] * 5,
+        out_specs=[kept] * 6 + [inside] * 3 + [kept] * len(made),
         scratch_shapes=[
             pltpu.VMEM((count - 1, rows, columns), dtype),
-            pltpu.VMEM((rows, 2 * query.shape[1]), dtype),
-            pltpu.SemaphoreType.DMA((taps + 6 + 2 * groups,)),
+            pltpu.VMEM((rows, 2 * width), dtype),
+            pltpu.SemaphoreType.DMA((taps + 8,)),
             pltpu.SemaphoreType.DMA((count,)),
             *grid_sems,
             pltpu.SemaphoreType.DMA((count,)),
@@ -362,19 +634,34 @@
             *grid_sems[:2],
             *([pltpu.SemaphoreType.DMA((groups,))] * 4),
             *sum_scratch(groups, blocks, stats.shape),
+            pltpu.VMEM((2, columns, columns), dtype),
+            pltpu.SemaphoreType.DMA((2, groups)),
+            pltpu.SemaphoreType.DMA((len(made),)),
+            pltpu.VMEM((16, columns), jnp.float32),
+            pltpu.VMEM(wide, dtype),
+            pltpu.VMEM(wide, jnp.float32),
+            pltpu.VMEM(wide, dtype),
+            pltpu.VMEM(wide, dtype),
+            pltpu.VMEM(narrow, dtype),
+            pltpu.VMEM(narrow, dtype),
+            pltpu.VMEM(narrow, dtype),
+            pltpu.VMEM(wide, dtype),
+            pltpu.VMEM((2, span, width), dtype),
+            pltpu.VMEM((HEADS, length, length), dtype),
+            pltpu.VMEM(wide, dtype),
         ],
         compiler_params=pltpu.CompilerParams(
-            collective_id=0, has_side_effects=True, vmem_limit_bytes=24 << 20
+            collective_id=0, has_side_effects=True, vmem_limit_bytes=60 << 20
         ),
         name="gather",
-    )(*weights, small, stats)
+    )(*weights, small, stats, inputs, tables)
 
 
 def reduce_kernel(groups, blocks, rel_at, *refs):
-    lefts = refs[:6]
-    rights = refs[6:13]
-    rel_grad, vector = refs[13:15]
-    out, total, left_got, right_got = refs[15:19]
+    lefts = refs[:5]
+    rights = list(refs[5:11])
+    rel_grad, vector = refs[11:13]
+    out, total, left_got, wide_got, right_got = refs[13:18]
     (
         left_hold,
         right_hold,
@@ -388,9 +675,9 @@
         partial,
         done,
         rel_got,
-    ) = refs[19:31]
-    left_send, left_recv, right_send, right_recv, rel_send, rel_recv = refs[31:37]
-    refs = refs[37:]
+    ) = refs[18:30]
+    left_send, left_recv, right_send, right_recv, rel_send, rel_recv = refs[30:36]
+    refs = refs[36:]
     load_sem = refs[0]
     x1s, y1s, x2s, y2s, x1r, y1r, x2r, y2r = refs[1:9]
     shard_send, shard_recv, block_send, block_recv = refs[9:13]
@@ -416,14 +703,17 @@
     first = pl.ds(0, half)
     last = pl.ds(half, half)
     taps = 5
-    left_of = [0] * taps + [1, 1, 2, 3, 3, 4, 5]
+    up_right = rights[4]
+    rights[4:5] = [up_right.at[:, pl.ds(side * 2 * width, 2 * width)] for side in range(2)]
+    lefts_got = [left_got.at[index] for index in range(4)] + [wide_got]
+    left_of = [0] * taps + [1, 1, 2, 3, 3, 4, 4]
     right_of = [0] * taps + [1, 2, 3, 4, 5, 6, 6]
     own_columns = pl.ds(pl.multiple_of(core * width, 128), width)
     sib_columns = pl.ds(pl.multiple_of((1 - core) * width, 128), width)
 
     def left_copy(index):
         return remote(
-            lefts[index], left_got.at[index], left_send.at[index], left_recv.at[index], (sib, me)
+            lefts[index], lefts_got[index], left_send.at[index], left_recv.at[index], (sib, me)
         )
 
     def right_copy(index):
@@ -441,12 +731,19 @@
     def loads(piece, slot):
         left = left_of[piece]
         right = right_of[piece]
-        pairs = (
-            (lefts[left], left_hold.at[slot, 0]),
-            (left_got.at[left], left_hold.at[slot, 1]),
+        pairs = [
             (rights[right].at[:, own_columns], right_hold.at[slot, 0]),
             (right_got.at[right], right_hold.at[slot, 1]),
-        )
+        ]
+        if left < 4:
+            pairs.append((lefts[left], left_hold.at[slot, 0]))
+            pairs.append((lefts_got[left], left_hold.at[slot, 1]))
+        else:
+            for shard in range(groups):
+                source = pl.ds((2 * shard + piece % 2) * rows, rows)
+                target = pl.ds(shard * rows, rows)
+                pairs.append((lefts[left].at[:, source], left_hold.at[slot, 0, :, target]))
+                pairs.append((lefts_got[left].at[:, source], left_hold.at[slot, 1, :, target]))
         return [
             pltpu.make_async_copy(src, dst, load_sem.at[slot, i])
             for i, (src, dst) in enumerate(pairs)
@@ -756,11 +1053,12 @@
         out_shape=(
             jax.ShapeDtypeStruct((count, rows, columns), dtype),
             jax.ShapeDtypeStruct(vector.shape, jnp.float32),
-            jax.ShapeDtypeStruct((len(lefts), bins, columns), dtype),
-            jax.ShapeDtypeStruct((len(rights), bins, width), dtype),
+            jax.ShapeDtypeStruct((4, bins, columns), dtype),
+            jax.ShapeDtypeStruct(lefts[4].shape, dtype),
+            jax.ShapeDtypeStruct((len(rights) + 1, bins, width), dtype),
         ),
         in_specs=[kept] * (len(lefts) + len(rights)) + [inside] * 2,
-        out_specs=[kept, inside, kept, kept],
+        out_specs=[kept, inside, kept, kept, kept],
         scratch_shapes=[
             pltpu.VMEM((2, 2, bins, columns), dtype),
             pltpu.VMEM((2, 2, bins, width), dtype),
@@ -776,11 +1074,11 @@
             pltpu.VMEM(rel_grad.shape, dtype),
             pltpu.SemaphoreType.DMA((len(lefts),)),
             pltpu.SemaphoreType.DMA((len(lefts),)),
-            pltpu.SemaphoreType.DMA((len(rights),)),
-            pltpu.SemaphoreType.DMA((len(rights),)),
+            pltpu.SemaphoreType.DMA((len(rights) + 1,)),
+            pltpu.SemaphoreType.DMA((len(rights) + 1,)),
             pltpu.SemaphoreType.DMA((1,)),
             pltpu.SemaphoreType.DMA((1,)),
-            pltpu.SemaphoreType.DMA((2, 4)),
+            pltpu.SemaphoreType.DMA((2, 2 + 2 * groups)),
             *([each] * 8),
             pltpu.SemaphoreType.DMA((count, groups)),
             pltpu.SemaphoreType.DMA((count, groups)),
@@ -846,51 +1144,6 @@
     return lax.dot_general(
         left_side, right_side, (((1,), (1,)), ((), ())), preferred_element_type=jnp.float32
     )
-
-
-def attend_kernel(content_ref, position_ref, key_ref, value_ref, table_ref, out_ref, probs_ref):
-    length = content_ref.shape[0]
-    span = table_ref.shape[0]
-    head_value = value_ref.shape[1] // 2
-    for head in range(2):
-        keys = slice(head * KEY, (head + 1) * KEY)
-        values = slice(head * head_value, (head + 1) * head_value)
-        band = dot_trailing(position_ref[:, keys], table_ref[:, keys])
-        moved = pltpu.roll(band, span - length + 1, 1, stride=1, stride_axis=0)
-        scores = dot_trailing(content_ref[:, keys], key_ref[:, keys]) + moved[:, :length]
-        weight = jnp.exp(scores - jnp.max(scores, -1, keepdims=True))
-        probs = (weight / jnp.sum(weight, -1, keepdims=True)).astype(jnp.bfloat16)
-        probs_ref[head] = probs
-        out_ref[:, values] = jnp.dot(
-            probs, value_ref[:, values], preferred_element_type=jnp.float32
-        ).astype(out_ref.dtype)
-
-
-def attend(content, position, key, value, table):
-    length = content.shape[0]
-    span = table.shape[0]
-    steps = HEADS // 2
-
-    def columns(array):
-        return pl.BlockSpec((array.shape[0], array.shape[1] // steps), lambda i: (0, i))
-
-    return pl.pallas_call(
-        attend_kernel,
-        grid=(steps,),
-        in_specs=[columns(array) for array in (content, position, key, value, table)],
-        out_specs=(columns(value), pl.BlockSpec((2, length, length), lambda i: (i, 0, 0))),
-        out_shape=(
-            jax.ShapeDtypeStruct(value.shape, jnp.bfloat16),
-            jax.ShapeDtypeStruct((HEADS, length, length), jnp.bfloat16),
-        ),
-        compiler_params=pltpu.CompilerParams(vmem_limit_bytes=40 << 20),
-        cost_estimate=pl.CostEstimate(
-            flops=2 * length * (HEADS * KEY * (length + span) + length * value.shape[1]),
-            bytes_accessed=2 * HEADS * length * length,
-            transcendentals=HEADS * length * length,
-        ),
-        name="attend",
-    )(content, position, key, value, table)
 
 
 def attend_back_kernel(
@@ -1033,18 +1286,34 @@
     small = jnp.concatenate([part.reshape(-1) for part in small_parts])
     small = jnp.pad(small, (0, -small.shape[0] % 1024)).reshape(-1, 128)
     stats = jnp.concatenate([jnp.sum(inputs, 0), jnp.sum(inputs * inputs, 0)]).reshape(-1, 128)
+    tables = jnp.stack(
+        [
+            jnp.pad(position_table(length, rel_rows, direction), ((0, 1), (0, 0)))
+            for direction in (1.0, -1.0)
+        ]
+    ).astype(jnp.bfloat16)
     (
         conv_full,
         mixed_full,
         value_full,
         out_full,
-        up_first,
-        up_last,
-        down_first,
-        down_last,
-        rel_full,
+        up_full,
+        down_full,
+        _,
         small_full,
         stats,
+        activated,
+        after_conv,
+        normed_one,
+        content_query,
+        position_query,
+        keys,
+        values,
+        mirrored_keys,
+        probs,
+        attended,
+        after_attention,
+        normed_two,
     ) = gather(
         groups,
         blocks,
@@ -1060,14 +1329,15 @@
         ],
         small,
         stats,
+        tokens[0],
+        tables,
     )
     conv_full = conv_full.reshape(tap_count, model_width, model_width)
     mixed_full = mixed_full.reshape(model_width, -1)
     value_full = value_full.reshape(model_width, -1)
     out_full = out_full.reshape(model_width, -1)
-    up_full = [up_first.reshape(model_width, -1), up_last.reshape(model_width, -1)]
-    down_full = [down_first.reshape(model_width, -1), down_last.reshape(model_width, -1)]
-    rel_full = jnp.concatenate([rel_full[shard] for shard in range(groups)], 1)
+    up_full = up_full.reshape(model_width, -1)
+    down_full = down_full.reshape(-1, model_width)
     flat = small_full.reshape(groups, -1)
     taken = 0
     unpacked = []
@@ -1077,55 +1347,20 @@
         taken += part.size
     gain_rows = jnp.moveaxis(unpacked[0], 0, 1).reshape(gains.shape[0], -1)
     bias_rows = jnp.moveaxis(unpacked[1], 0, 1).reshape(biases.shape[0], -1)
-    up_offset = jnp.moveaxis(unpacked[2].reshape(groups, 2, piece_rows), 0, 1).reshape(2, -1)
-    rel_offset = jnp.moveaxis(unpacked[3], 0, 1).reshape(2, -1)
+    up_offset = unpacked[2].reshape(-1)
     batch_sums = stats.reshape(2, -1)
     centre = batch_sums[0] / token_total
     variance = batch_sums[1] / token_total - centre * centre
     inverse = lax.rsqrt(variance + EPSILON)
     standard = (inputs - centre) * inverse
     normed = standard * gain_rows[0] + bias_rows[0]
-    activated = jax.nn.gelu(normed).astype(jnp.bfloat16)
-    padded = jnp.pad(activated, ((half_taps, half_taps), (0, 0)))
-    stacked = jnp.concatenate([padded[tap : tap + length] for tap in range(tap_count)], 1)
-    conv_out = jnp.dot(
-        stacked, conv_full.reshape(-1, model_width), preferred_element_type=jnp.float32
-    )
-    after_conv = inputs + conv_out + bias_rows[1]
     standard_one, inverse_one = normalize(after_conv)
-    normed_one = (standard_one * gain_rows[1] + bias_rows[2]).astype(jnp.bfloat16)
-    mixed_raw = jnp.dot(normed_one, mixed_full, preferred_element_type=jnp.float32)
-    query_raw = mixed_raw[:, :key_width]
-    key_scale = KEY ** (-0.5)
-    content_query = (query_raw * key_scale + rel_offset[0]).astype(jnp.bfloat16)
-    position_query = (query_raw * key_scale + rel_offset[1]).astype(jnp.bfloat16)
-    keys = mixed_raw[:, key_width:].astype(jnp.bfloat16)
-    values = jnp.dot(normed_one, value_full, preferred_element_type=jnp.float32).astype(
-        jnp.bfloat16
-    )
-    table, mirrored_table = [
-        jnp.pad(position_table(length, rel_rows, direction), ((0, 1), (0, 0))).astype(jnp.bfloat16)
-        for direction in (1.0, -1.0)
-    ]
-    position_keys, mirrored_keys = [
-        jnp.dot(side, rel_full, preferred_element_type=jnp.float32).astype(jnp.bfloat16)
-        for side in (table, mirrored_table)
-    ]
-    attended, probs = attend(content_query, position_query, keys, values, position_keys)
-    after_attention = (
-        after_conv + jnp.dot(attended, out_full, preferred_element_type=jnp.float32) + bias_rows[3]
-    )
     standard_two, inverse_two = normalize(after_attention)
-    normed_two = (standard_two * gain_rows[2] + bias_rows[4]).astype(jnp.bfloat16)
-    hidden_pre = [
-        jnp.dot(normed_two, up_full[half], preferred_element_type=jnp.float32) + up_offset[half]
-        for half in range(2)
-    ]
-    hidden = [jax.nn.gelu(half).astype(jnp.bfloat16) for half in hidden_pre]
+    hidden_pre = jnp.dot(normed_two, up_full, preferred_element_type=jnp.float32) + up_offset
+    hidden = jax.nn.gelu(hidden_pre).astype(jnp.bfloat16)
     outputs = (
         after_attention
-        + jnp.dot(hidden[0], down_full[0], preferred_element_type=jnp.float32)
-        + jnp.dot(hidden[1], down_full[1], preferred_element_type=jnp.float32)
+        + jnp.dot(hidden, down_full, preferred_element_type=jnp.float32)
         + bias_rows[5]
     )
     target_row = lax.dynamic_index_in_dim(target_table, window_ids[0], 0, keepdims=False)
@@ -1135,15 +1370,11 @@
     cotangent = jnp.clip(outputs - target_row, -limits, limits).astype(jnp.bfloat16)
     cot_value = cotangent.astype(jnp.float32)
     grad_down_bias = jnp.sum(cot_value, 0)
-    pre_grad = []
-    for half in range(2):
-        hidden_grad = dot_trailing(cotangent, down_full[half])
-        gelu_pull = jax.vjp(jax.nn.gelu, hidden_pre[half])[1]
-        pre_grad.append(gelu_pull(hidden_grad)[0].astype(jnp.bfloat16))
-    grad_up_bias = jnp.stack([jnp.sum(half.astype(jnp.float32), 0) for half in pre_grad])
-    normed_two_grad = dot_trailing(pre_grad[0], up_full[0]) + dot_trailing(
-        pre_grad[1], up_full[1]
-    )
+    hidden_grad = dot_trailing(cotangent, down_full)
+    gelu_pull = jax.vjp(jax.nn.gelu, hidden_pre)[1]
+    pre_grad = gelu_pull(hidden_grad)[0].astype(jnp.bfloat16)
+    grad_up_bias = jnp.sum(pre_grad.astype(jnp.float32), 0)
+    normed_two_grad = dot_trailing(pre_grad, up_full)
     grad_gain_two = jnp.sum(normed_two_grad * standard_two, 0)
     grad_bias_two = jnp.sum(normed_two_grad, 0)
     attention_grad = cot_value + norm_back(
@@ -1184,27 +1415,25 @@
         grad_out_bias,
         grad_bias_two,
         grad_down_bias,
-        grad_up_bias[0],
-        grad_up_bias[1],
+        grad_up_bias,
         grad_rel_bias.reshape(-1),
     ]
     sums = jnp.concatenate(sum_parts)
     sums = jnp.pad(sums, (0, -sums.shape[0] % 1024)).reshape(-1, 128)
-    grad_rel = dot_leading(mirrored_table, table_grad).astype(jnp.bfloat16)
+    grad_rel = dot_leading(tables[1], table_grad).astype(jnp.bfloat16)
     grad_rel = jnp.moveaxis(grad_rel.reshape(rel_rows, groups, rel_columns), 0, 1)
     grad_rel = grad_rel.reshape(groups, 2, rel_rows // 2, rel_columns)
     mixed_wide = jnp.pad(mixed_grad, ((0, 0), (0, model_width - 2 * key_width)))
-    lefts = [activated, normed_one, attended, normed_two, hidden[0], hidden[1]]
+    lefts = [activated, normed_one, attended, normed_two, hidden]
     rights = [
         conv_grad,
         mixed_wide,
         value_grad,
         branch_grad,
-        pre_grad[0],
-        pre_grad[1],
+        pre_grad,
         cotangent,
     ]
-    pieces, sums, _, _ = reduce(
+    pieces, sums, _, _, _ = reduce(
         groups, blocks, 2 * key_width - half_width, lefts, rights, grad_rel, sums
     )
     flat = sums.reshape(-1)
@@ -1214,19 +1443,14 @@
         - gain_rows[0] * (bn_sums[3] + standard * bn_sums[0]) / token_total
     )
     shard = lax.axis_index("fsdp")
-    by_shard = flat[: 11 * model_width].reshape(11, groups, -1)
+    by_shard = flat[: 9 * model_width].reshape(9, groups, -1)
     by_shard = lax.dynamic_index_in_dim(by_shard, shard, 1, keepdims=False)
+    up_sums = flat[9 * model_width : 11 * model_width].reshape(groups, -1)
+    up_sums = lax.dynamic_index_in_dim(up_sums, shard, 0, keepdims=False)
     rel_sums = flat[11 * model_width : 11 * model_width + 2 * key_width]
     rel_sums = rel_sums.reshape(2, groups, -1)
     rel_sums = lax.dynamic_index_in_dim(rel_sums, shard, 1, keepdims=False)
-    up_grad = jnp.concatenate(
-        [
-            pieces[8 + half, :, index * piece_rows : (index + 1) * piece_rows]
-            for index in range(groups)
-            for half in range(2)
-        ],
-        1,
-    )
+    up_grad = jnp.concatenate([pieces[8], pieces[9]], 1)
     mixed_sum = pieces[5].astype(jnp.float32)
     rel_at = 2 * key_width
     return (
@@ -1242,7 +1466,7 @@
         pieces[10:12].reshape(2 * piece_rows, -1).astype(jnp.float32),
         by_shard[:3],
         by_shard[3:9],
-        by_shard[9:11].reshape(-1),
+        up_sums,
         rel_sums,
     )
 

time: 791 us -> 675 us (0.85)
  local copies, waits for them, and re-layouts: 68.1 us -> 13.8 us
  matrix products: 92.1 us -> 51.5 us
  Pallas kernels: 566 us -> 551 us
    dot_general x10 -> x2, matrix products: 64.8 us -> 17.7 us  [the longest x1 10.9 us: on_device(): jnp.dot(normed_two, up_full, preferred_element_type=jnp.float32) + up_offset]
    unnamed x221 -> x95, local copies, waits for them, and re-layouts: 42.7 us -> 4.45 us
    pallas_call x1 -> x0, Pallas kernels: 15.1 us -> none  [attend(): pl.pallas_call(attend_kernel, grid=(steps,), in_specs=[columns(array) for...]
    convert_element_type x5 -> x0, other arithmetic: 14.2 us -> none  [the longest x1 4.9 us: on_device(): pieces[7].astype(jnp.float32)]
    dot_general x7 -> x5, matrix products: 27 us -> 33 us  [dot_trailing(): lax.dot_general(left_side, right_side, (((1,), (1,)), ((), ())), preferre...]
where the time goes in v4:
time: 675 us; the launch traced here: 668 us
  Pallas kernels  551 us (82%)
  matrix products  51.5 us (8%)
  other arithmetic  48.9 us (7%)
  local copies, waits for them, and re-layouts  13.8 us (2%)
    pallas_call x1, Pallas kernels, reduce(): pl.pallas_call(functools.partial(reduce_kernel, groups, blocks, rel_at),...  315 us
    pallas_call x1, Pallas kernels, gather(): pl.pallas_call(functools.partial(gather_kernel, groups, blocks), out_shap...  201 us
    dot_general x5, matrix products, dot_trailing(): lax.dot_general(left_side, right_side, (((1,), (1,)), ((), ())), preferre...  33 us
    pallas_call x1, Pallas kernels, attend_back(): pl.pallas_call(attend_back_kernel, grid=(steps,), in_specs=[pl.BlockSpec(...  18.2 us
    pallas_call x1, Pallas kernels, conv_back(): pl.pallas_call(conv_back_kernel, grid=(taps,), in_specs=[pl.BlockSpec((le...  16.5 us

profile of v4, /device:TPU:0, one launch (start us, length us, event | category | flops | bytes accessed | tf_op | source)
XLA Modules:
  0.0 667.6 jit_solution(1524064434256980407)
XLA Ops:
  1.4 0.3 copy-done
  1.7 0.6 dynamic-slice_reduce_fusion
  2.3 0.8 select_reduce_fusion
  3.1 0.6 neg.8
  3.6 0.7 reshape.267
  4.3 0.7 reshape.266
  5.0 1.3 fusion.58.refs_8_
  6.4 1.8 convert_reduce_fusion.1
  8.2 0.6 pad_maximum_fusion.1.refs_9_
  8.8 0.1 multiply_add_fusion.3
  8.9 0.6 fusion.51
  9.6 0.9 fusion.56
  10.5 0.3 fusion.52
  10.9 0.1 fusion.73
  10.9 0.3 fusion.54
  11.3 0.5 fusion.49
  11.8 0.6 fusion.96
  12.4 0.5 fusion.48
  12.9 0.6 fusion.44
  13.5 1.2 pad_maximum_fusion.refs_11_
  14.7 200.7 %gather.1 = (bf16[5,4,384,1536]{3,2,1,0:T(8,128)(2,1)}, bf16[4,384,1024]{2,1,0:T(8,128)(2,1)}, bf16[4,384,1536]{2,1,0:T(8,128)(2,1)}, bf16[4,384,1536]{2,1,0:T(8...) custom-call(bf16[5,384,1536]{2,1,0:T(8,128)(2,1)} %refs_0_.1, ...), custom_call_target="tpu_custom_call" | custom-call | tf_op jit(solution)/shard_map/gather/pallas_call | solution.py:610
  215.4 0.9 copy.48
  216.5 10.9 %multiply_convert_fusion = (bf16[512,3072]{1,0:T(8,128)(2,1)S(1)}, f32[512,3072]{1,0:T(8,128)}) fusion(f32[3072]{0:T(1024)S(1)} %add.180, bf16[512,1536]{1,0:T(8,128)(2,1)} %get-tuple-element.44.refs_3_, bf16[1536,3072]{1,0:T(8,128)(2,1)} %bitcast.128), kind=kOutput, calls=%fused_computation.10 | convolution fusion | flops 4847566848 | bytes 20459520 | tf_op jit(solution)/shard_map/dot_general | solution.py:1359
  227.5 6.7 %convert_reduce_fusion.2 = (f32[1536]{0:T(1024)S(1)}, bf16[512,1536]{1,0:T(8,128)(2,1)}, bf16[1,512,1536]{2,1,0:T(8,128)(2,1)}) fusion(f32[1536]{0:T(1024)S(1)} %copy-done.27, bf16[512]{0:T(512)(128)(2,1)S(1)} %copy-done.29, f32[512]{0:T(512)S(1)} %select_reduce_fusion, f32[1536]{0:T(1024)S(1)} %add.186, f32[512,1536]{1,0:T(8,128)S(1)} %copy-done.10, ...), kind=kOutput, calls=%fused_computation.17 | convolution fusion | flops 4840487424 | bytes 18895872 | tf_op jit(solution)/shard_map/dot_general | solution.py:1363
  234.2 0.2 reduce_sum.192
  234.5 0.5 multiply_reduce_fusion.5
  234.9 0.6 add_rsqrt_fusion.1
  235.5 12.7 %convert_reduce_fusion = (f32[3072]{0:T(1024)S(1)}, bf16[512,3072]{1,0:T(8,128)(2,1)S(1)}) fusion(f32[512,3072]{1,0:T(8,128)} %get-tuple-element.131, f32[3072]{0:T(1024)} %copy-done.26, bf16[512,1536]{1,0:T(8,128)(2,1)} %get-tuple-element.89.refs_10_, bf16[3072,1536]{1,0:T(8,128)(2,1)} %bitcast.130), kind=kOutput, calls=%fused_computation.9 | convolution fusion | flops 4868011008 | bytes 20471808 | tf_op jit(solution)/shard_map/dot_general | solution.py:1144
  248.2 9.7 %multiply_reduce_fusion = (f32[1536]{0:T(1024)S(1)}, f32[512]{0:T(512)S(1)}, f32[512]{0:T(512)S(1)}, f32[1536]{0:T(1024)S(1)}, f32[512,1536]{1,0:T(8,128)S(1)}) fusion(f32[512,1536]{1,0:T(8,128)S(1)} %copy-done.10, f32[512]{0:T(512)S(1)} %copy-done.28, f32[512]{0:T(512)S(1)} %broadcast_multiply_fusion.5, f32[1536]{0:T(1024)S(1)} %mul.445, ...), kind=kOutput, calls=%fused_computation.47 | convolution fusion | flops 4838912000 | bytes 18900992 | tf_op jit(solution)/shard_map/dot_general | solution.py:1144
  258.0 2.9 convert_reduce_fusion.3
  260.9 2.3 reduce_sum.196
  263.2 0.6 copy-done.11
  263.8 0.4 multiply_reduce_fusion.3
  264.3 5.6 convolution_convert_fusion.out_ref
  270.0 18.2 %attend_back.1 = (bf16[512,512]{1,0:T(8,128)(2,1)S(1)}, bf16[512,512]{1,0:T(8,128)(2,1)S(1)}, bf16[512,1536]{1,0:T(8,128)(2,1)S(1)}, bf16[1024,512]{1,0:T(8,128)(2,1)S(1)}, f32[2,512]{1,0:T(2,128)S(1)}) custom-call(bf16[8,512,512]{2,1,0:T(8,128)(2,1)S(1)} %copy-done.3, bf16[512,1536]{1,0:T(8,128)(2,1)S(1)} %convolution_convert_fusion.out_ref, ...), custom_call_target="tpu_custom_call" | custom-call | flops 3221225472 | bytes 4194304 | tf_op jit(solution)/shard_map/attend_back/pallas_call | solution.py:1204
  288.2 0.1 constant_dynamic-update-slice_fusion
  288.3 1.9 fusion.79
  290.2 3.2 multiply_reduce_fusion.1
  293.5 2.5 convert_reduce_fusion.4
  296.0 1.4 pad.29.refs_6_
  297.4 0.8 fusion.32
  298.2 0.7 copy.47
  299.0 0.4 slice_dynamic-update-slice_fusion.3
  299.3 0.4 slice_dynamic-update-slice_fusion.2
  299.7 0.1 constant_dynamic-update-slice_fusion.2
  299.8 0.4 slice_dynamic-update-slice_fusion.1
  300.2 0.4 slice_dynamic-update-slice_fusion.left_ref
  300.5 16.5 %conv_back.1 = f32[512,1536]{1,0:T(8,128)S(1)} custom-call(bf16[512,7680]{1,0:T(8,128)(2,1)S(1)} %slice_dynamic-update-slice_fusion.left_ref, bf16[5,1536,1536]{2,1,0:T(8,128)(2,1)} %bitcast.127), custom_call_target="tpu_custom_call" | custom-call | flops 12079595520 | bytes 31457280 | tf_op jit(solution)/shard_map/conv_back/pallas_call | solution.py:1236
  317.1 5.3 fusion.74
  322.5 0.6 pad_bitcast_fusion.refs_12_
  323.1 315.4 %reduce.9 = (bf16[12,384,1536]{2,1,0:T(8,128)(2,1)}, f32[144,128]{1,0:T(8,128)}, bf16[4,512,1536]{2,1,0:T(8,128)(2,1)}, bf16[512,3072]{1,0:T(8,128)(2,1)}, bf16[7,512,768]{2,1,0:T(8,128)(2,1)}) custom-call(bf16[512,1536]{1,0:T(8,128)(2,1)} %get-tuple-element.63.refs_0_, bf16[512,1536]{1,0:T(8,128)(2,1)} %get-tuple-element.64.refs_1_, ...), custom_call_target="tpu_custom_call" | custom-call | tf_op jit(solution)/shard_map/reduce/pallas_call | solution.py:1051
  638.5 0.7 slice_bitcast_fusion.3
  639.2 5.3 fusion.31
  644.5 9.0 %slice_convert_fusion = f32[5,384,1536]{2,1,0:T(8,128)} fusion(bf16[12,384,1536]{2,1,0:T(8,128)(2,1)} %get-tuple-element.69), kind=kLoop, calls=%fused_computation.11 | loop fusion | flops 2949120 | bytes 17694720 | tf_op jit(solution)/shard_map/convert_element_type | solution.py:1459
  653.5 3.3 slice_bitcast_fusion.1
  656.8 1.3 fusion.77
  658.1 0.7 slice.162
  658.7 2.8 maximum_convert_fusion
  661.5 0.2 slice.144
  661.7 3.0 bitcast_convert_fusion
  664.7 0.6 copy.50
  665.3 0.6 copy.49
  665.9 0.6 dynamic-slice_reduce_fusion.1
  666.6 0.6 constant_dynamic-slice_fusion.1
  (127 shorter events, 0.7 us)
Async XLA Ops:
  0.6 1.0 copy-start
  10.8 2.1 copy-start.20
  11.3 1.1 copy-start.22
  11.8 1.1 copy-start.18
  216.5 11.0 %copy-start.26 = (f32[3072]{0:T(1024)}, f32[3072]{0:T(1024)S(1)}, u32[]{:S(2)}) copy-start(f32[3072]{0:T(1024)S(1)} %add.180) | copy-start | bytes 36868
  216.5 11.0 %copy-start.10 = (f32[512,1536]{1,0:T(8,128)S(1)}, f32[512,1536]{1,0:T(8,128)}, u32[]{:S(2)}) copy-start(f32[512,1536]{1,0:T(8,128)} %get-tuple-element.43) | copy-start | bytes 9437188
  216.5 11.0 %copy-start.27 = (f32[1536]{0:T(1024)S(1)}, f32[1536]{0:T(1024)}, u32[]{:S(2)}) copy-start(f32[1536]{0:T(1024)} %dynamic-slice_reduce_fusion) | copy-start | bytes 18436
  216.5 11.0 %copy-start.29 = (bf16[512]{0:T(512)(128)(2,1)S(1)}, bf16[512]{0:T(512)(128)(2,1)}, u32[]{:S(2)}) copy-start(bf16[512]{0:T(512)(128)(2,1)} %neg.8) | copy-start | bytes 3076
  216.5 11.0 %copy-start.30 = (bf16[4,768,1536]{2,1,0:T(8,128)(2,1)S(1)}, bf16[4,768,1536]{2,1,0:T(8,128)(2,1)}, u32[]{:S(2)}) copy-start(bf16[4,768,1536]{2,1,0:T(8,128)(2,1)} %get-tuple-element.47) | copy-start | bytes 28311556
  227.5 6.8 %copy-start.16 = (bf16[512,3072]{1,0:T(8,128)(2,1)}, bf16[512,3072]{1,0:T(8,128)(2,1)S(1)}, u32[]{:S(2)}) copy-start(bf16[512,3072]{1,0:T(8,128)(2,1)S(1)} %get-tuple-element.130.refs_4_) | copy-start | bytes 9437188
  235.5 12.7 %copy-start.28 = (f32[512]{0:T(512)S(1)}, f32[512]{0:T(512)}, u32[]{:S(2)}) copy-start(f32[512]{0:T(512)} %add_rsqrt_fusion.1) | copy-start | bytes 6148
  248.2 9.7 %copy-start.17 = (bf16[512,3072]{1,0:T(8,128)(2,1)}, bf16[512,3072]{1,0:T(8,128)(2,1)S(1)}, u32[]{:S(2)}) copy-start(bf16[512,3072]{1,0:T(8,128)(2,1)S(1)} %get-tuple-element.87.refs_9_) | copy-start | bytes 9437188
  248.2 9.8 %copy-start.15 = (bf16[512,1536]{1,0:T(8,128)(2,1)S(1)}, bf16[512,1536]{1,0:T(8,128)(2,1)}, u32[]{:S(2)}) copy-start(bf16[512,1536]{1,0:T(8,128)(2,1)} %get-tuple-element.89.refs_10_) | copy-start | bytes 4718596
  260.9 2.8 copy-start.11
  264.2 5.7 copy-start.3
  264.2 5.7 copy-start.4
  264.2 5.7 copy-start.5
  264.2 5.7 copy-start.6
  264.3 5.7 copy-start.7
  264.3 5.7 copy-start.8
  269.9 18.3 %copy-start.31 = (bf16[4,384,1024]{2,1,0:T(8,128)(2,1)S(1)}, bf16[4,384,1024]{2,1,0:T(8,128)(2,1)}, u32[]{:S(2)}) copy-start(bf16[4,384,1024]{2,1,0:T(8,128)(2,1)} %get-tuple-element.58) | copy-start | bytes 9437188
  269.9 20.2 %slice-start.4 = ((s8[4718592]{0:T(1024)(128)(4,1)}), s8[4194304]{0:T(1024)(128)(4,1)S(1)}, s32[]{:S(2)}) async-start(s8[4718592]{0:T(1024)(128)(4,1)} %bitcast.132), calls=%async_computation.4 | async-start | bytes 8388608
  288.1 2.0 copy-start.2
  288.1 2.0 slice-start.5
  290.2 3.3 copy-start.12
  290.2 3.3 copy-start.14
  293.5 3.9 copy-start.19
  293.5 3.9 copy-start.21
  293.5 3.9 copy-start.23
  296.0 4.2 copy-start.9
  297.4 1.6 copy-start.25
  323.1 316.1 %copy-start.13 = (bf16[1,512,1536]{2,1,0:T(8,128)(2,1)S(1)}, bf16[1,512,1536]{2,1,0:T(8,128)(2,1)}, u32[]{:S(2)}) copy-start(bf16[1,512,1536]{2,1,0:T(8,128)(2,1)} %param.21) | copy-start | bytes 4718596
  639.2 14.3 %slice-start = ((s8[14155776]{0:T(1024)(128)(4,1)}), s8[4194304]{0:T(1024)(128)(4,1)S(1)}, s32[]{:S(2)}) async-start(s8[14155776]{0:T(1024)(128)(4,1)} %bitcast.109), calls=%async_computation | async-start | bytes 8388608
  639.2 14.3 %slice-start.1 = ((s8[14155776]{0:T(1024)(128)(4,1)}), s8[4194304]{0:T(1024)(128)(4,1)S(1)}, s32[]{:S(2)}) async-start(s8[14155776]{0:T(1024)(128)(4,1)} %bitcast.109), calls=%async_computation.1 | async-start | bytes 8388608
  644.5 9.0 %slice-start.2 = ((s8[14155776]{0:T(1024)(128)(4,1)}), s8[4194304]{0:T(1024)(128)(4,1)S(1)}, s32[]{:S(2)}) async-start(s8[14155776]{0:T(1024)(128)(4,1)} %bitcast.109), calls=%async_computation.2 | async-start | bytes 8388608
  644.5 9.0 %slice-start.3 = ((s8[14155776]{0:T(1024)(128)(4,1)}), s8[1572864]{0:T(1024)(128)(4,1)S(1)}, s32[]{:S(2)}) async-start(s8[14155776]{0:T(1024)(128)(4,1)} %bitcast.109), calls=%async_computation.3 | async-start | bytes 3145728
  661.5 5.6 copy-start.1
  661.7 3.0 copy-start.24

commit v5 on v4

--- a/solution.py
+++ b/solution.py
@@ -12,6 +12,8 @@
 KEY = 64
 MESH = pl.DeviceIdType.MESH
 AHEAD = 2
+GELU = 0.7978845608028654
+VMEM_LIMIT = 62 << 20
 
 
 def neighbours(dp):
@@ -657,11 +659,23 @@
     )(*weights, small, stats, inputs, tables)
 
 
+def gelu_slope(value):
+    inner = GELU * (value + 0.044715 * value * value * value)
+    curve = jnp.tanh(inner)
+    slope = GELU * (1.0 + 3 * 0.044715 * value * value)
+    return 0.5 * (1.0 + curve) + 0.5 * value * (1.0 - curve * curve) * slope
+
+
 def reduce_kernel(groups, blocks, rel_at, *refs):
     lefts = refs[:5]
-    rights = list(refs[5:11])
-    rel_grad, vector = refs[11:13]
-    out, total, left_got, wide_got, right_got = refs[13:18]
+    cotangent, hidden_pre, after_attention, after_conv, tokens = refs[5:10]
+    down_full, up_full, out_full, value_full, mixed_full, conv_full = refs[10:16]
+    probs, values, keys, contents, positions, mirrored_keys = refs[16:22]
+    params, table = refs[22:24]
+    out, total, part_grad = refs[24:27]
+    made = refs[27:32]
+    hidden_got, left_got, right_got = refs[32:35]
+    rights = [cotangent, *made]
     (
         left_hold,
         right_hold,
@@ -672,18 +686,36 @@
         y_two,
         shard_got,
         block_got,
-        partial,
         done,
+        rel_grad,
         rel_got,
-    ) = refs[18:30]
-    left_send, left_recv, right_send, right_recv, rel_send, rel_recv = refs[30:36]
-    refs = refs[36:]
-    load_sem = refs[0]
-    x1s, y1s, x2s, y2s, x1r, y1r, x2r, y2r = refs[1:9]
-    shard_send, shard_recv, block_send, block_recv = refs[9:13]
-    write_sem, send_sem, ax, ay, ad, sib_sem = refs[13:19]
-    sum_bufs = refs[19:23]
-    sum_sems = refs[23:29]
+        vector,
+    ) = refs[35:48]
+    left_send, left_recv, right_send, right_recv, rel_send, rel_recv = refs[48:54]
+    load_sem = refs[54]
+    x1s, y1s, x2s, y2s, x1r, y1r, x2r, y2r = refs[55:63]
+    shard_send, shard_recv, block_send, block_recv = refs[63:67]
+    write_sem, send_sem, ax, ay, ad, sib_sem = refs[67:73]
+    sum_bufs = refs[73:77]
+    sum_sems = refs[77:83]
+    credit, shard_credit = refs[83:85]
+    (
+        attn_grad,
+        total_ref,
+        kept_ref,
+        weight_hold,
+        wide_hold,
+        right_ref,
+        value_grad_ref,
+        mixed_ref,
+        key_ref,
+        content_ref,
+        position_ref,
+        table_ref,
+        table_grad_ref,
+        probs_ref,
+    ) = refs[85:99]
+    tile_sem, host_sem, probs_sem, kept_sem = refs[99:103]
 
     dp = lax.axis_index("dp")
     me = lax.axis_index("fsdp")
@@ -703,11 +735,13 @@
     first = pl.ds(0, half)
     last = pl.ds(half, half)
     taps = 5
-    up_right = rights[4]
-    rights[4:5] = [up_right.at[:, pl.ds(side * 2 * width, 2 * width)] for side in range(2)]
-    lefts_got = [left_got.at[index] for index in range(4)] + [wide_got]
-    left_of = [0] * taps + [1, 1, 2, 3, 3, 4, 4]
-    right_of = [0] * taps + [1, 2, 3, 4, 5, 6, 6]
+    up_right = rights[1]
+    rights[1:2] = [up_right.at[:, pl.ds(side * 2 * width, 2 * width)] for side in range(2)]
+    lefts_got = [hidden_got] + [left_got.at[index] for index in range(4)]
+    left_of = [0, 0, 1, 1, 2, 3, 3] + [4] * taps
+    right_of = [0, 0, 1, 2, 3, 4, 5] + [6] * taps
+    mixed_piece = 6
+    first_tap = 7
     own_columns = pl.ds(pl.multiple_of(core * width, 128), width)
     sib_columns = pl.ds(pl.multiple_of((1 - core) * width, 128), width)
 
@@ -735,7 +769,7 @@
             (rights[right].at[:, own_columns], right_hold.at[slot, 0]),
             (right_got.at[right], right_hold.at[slot, 1]),
         ]
-        if left < 4:
+        if left > 0:
             pairs.append((lefts[left], left_hold.at[slot, 0]))
             pairs.append((lefts_got[left], left_hold.at[slot, 1]))
         else:
@@ -759,29 +793,41 @@
 
     meet(near + shards + far)
 
-    for piece in range(count):
-        if left_of[piece] not in left_of[:piece]:
-            left_copy(left_of[piece]).start()
-        if right_of[piece] not in right_of[:piece]:
-            right_copy(right_of[piece]).start()
-    rel_copy().start()
+    for index in range(len(lefts)):
+        left_copy(index).start()
+        if index == 0:
+            right_copy(0).start()
     start_loads(0)
 
     summing = sum_steps(groups, blocks, vector, total, *sum_bufs, sum_sems)
+
+    ring = x_one.shape[0]
+
+    def pay(piece, index, device):
+        @pl.when(piece < count - ring)
+        def _():
+            pl.semaphore_signal(
+                credit.at[index], inc=1, device_id=(device, me), device_id_type=MESH
+            )
+
+    def claim(piece, index):
+        @pl.when(piece >= ring)
+        def _():
+            pl.semaphore_wait(credit.at[index], 1)
 
     def one(piece):
         slot = piece % slots
         return (
             remote(
                 grad.at[slot, :, :, 1 - at_x, :, first],
-                x_one.at[piece],
+                x_one.at[piece % ring],
                 x1s.at[piece],
                 x1r.at[piece],
                 (along_x, me),
             ),
             remote(
                 grad.at[slot, :, 1 - at_y, :, :, last],
-                y_one.at[piece],
+                y_one.at[piece % ring],
                 y1s.at[piece],
                 y1r.at[piece],
                 (along_y, me),
@@ -793,14 +839,14 @@
         return (
             remote(
                 grad.at[slot, :, 1 - at_y, at_x, :, first],
-                y_two.at[piece],
+                y_two.at[piece % ring],
                 y2s.at[piece],
                 y2r.at[piece],
                 (along_y, me),
             ),
             remote(
                 grad.at[slot, :, at_y, 1 - at_x, :, last],
-                x_two.at[piece],
+                x_two.at[piece % ring],
                 x2s.at[piece],
                 x2r.at[piece],
                 (along_x, me),
@@ -811,7 +857,7 @@
         other = (me + 1 + j) % groups
         return remote(
             grad.at[piece % slots, other, at_y, at_x],
-            shard_got.at[piece, me],
+            shard_got.at[piece % ring, me],
             shard_send.at[piece, j],
             shard_recv.at[piece, me],
             (dp, other),
@@ -821,7 +867,7 @@
         other = (me + 1 + j) % groups
         return remote(
             grad.at[piece % slots, other, at_y, at_x],
-            shard_got.at[piece, other],
+            shard_got.at[piece % ring, other],
             shard_send.at[piece, j],
             shard_recv.at[piece, other],
             (dp, other),
@@ -829,7 +875,7 @@
 
     def block_copy(piece, j):
         return remote(
-            partial.at[piece],
+            done.at[piece],
             block_got.at[piece, block],
             block_send.at[piece, j],
             block_recv.at[piece, block],
@@ -839,7 +885,7 @@
     def block_arrival(piece, j):
         other = (block + 1 + j) % blocks
         return remote(
-            partial.at[piece],
+            done.at[piece],
             block_got.at[piece, other],
             block_send.at[piece, j],
             block_recv.at[piece, other],
@@ -862,7 +908,7 @@
     diagonal = neighbours(along_x)[2]
 
     def shift(piece):
-        move = piece - taps // 2
+        move = piece - first_tap - taps // 2
         for window in range(2):
             value = right_hold[piece % 2, window].astype(jnp.float32)
             value = pltpu.roll(value, move % value.shape[0], 0)
@@ -884,11 +930,11 @@
 
         lax.fori_loop(0, groups, shard_body, 0)
 
-        @pl.when(piece == taps)
+        @pl.when(piece == mixed_piece)
         def _():
             rel_copy().wait()
 
-        @pl.when(jnp.logical_and(piece == taps, core == 1))
+        @pl.when(jnp.logical_and(piece == mixed_piece, core == 1))
         def _():
             for shard in range(groups):
                 value = rel_grad[shard].astype(jnp.float32) + rel_got[shard].astype(jnp.float32)
@@ -899,6 +945,362 @@
     def add(piece_slot, ref, columns, *index):
         ahead = grad[(piece_slot,) + index + (slice(None), columns)]
         return ahead.astype(jnp.float32) + ref.astype(jnp.float32)
+
+    length = tokens.shape[0]
+    columns = 2 * width
+    tile = 512
+    block_rows = 128
+    head_value = columns // HEADS
+    tiles = columns // tile
+    hidden_tiles = hidden_pre.shape[1] // tile
+
+    def tile_of(phase, i):
+        at = pl.ds(pl.multiple_of(i * tile, tile), tile)
+        if phase == 0:
+            return down_full.at[at]
+        if phase == 1:
+            at = pl.ds(pl.multiple_of(i // 2 * tile, tile), tile)
+            return up_full.at[at, pl.ds(pl.multiple_of(i % 2 * columns, columns), columns)]
+        if phase == 5:
+            at = pl.ds(pl.multiple_of(i % tiles * tile, tile), tile)
+            return conv_full.at[i // tiles, at]
+        return (out_full, mixed_full, value_full)[phase - 2].at[at]
+
+    lengths = [hidden_tiles, 2 * tiles, tiles, tiles, tiles, taps * tiles]
+    widths = [columns, columns, columns, mixed_full.shape[1], columns, columns]
+
+    def tile_load(phase, i):
+        slot = (sum(lengths[:phase]) + i) % 2
+        return pltpu.make_async_copy(
+            tile_of(phase, i),
+            weight_hold.at[slot, :, pl.ds(0, widths[phase])],
+            tile_sem.at[slot],
+        )
+
+    def next_tile(phase, i):
+        tile_load(phase, i).wait()
+
+        @pl.when(i + 1 < lengths[phase])
+        def _():
+            tile_load(phase, i + 1).start()
+
+        if phase + 1 < len(lengths):
+
+            @pl.when(i + 1 == lengths[phase])
+            def _():
+                tile_load(phase + 1, 0).start()
+
+        slot = (sum(lengths[:phase]) + i) % 2
+        return weight_hold[slot, :, 0 : widths[phase]]
+
+    def over(count, fn):
+        def step_body(i, carry):
+            fn(i)
+            return carry
+
+        lax.fori_loop(0, count, step_body, 0)
+
+    def columns_at(i, wide, offset=0):
+        return pl.ds(pl.multiple_of(offset + i * wide, 128), wide)
+
+    def host_load(index):
+        pairs = [
+            (cotangent, right_ref),
+            (after_attention, kept_ref),
+            (after_conv, kept_ref),
+            (values, wide_hold.at[:, pl.ds(columns, columns)]),
+            (keys, key_ref),
+            (contents, content_ref),
+            (positions, position_ref),
+            (mirrored_keys, table_ref),
+            (tokens, wide_hold.at[:, pl.ds(columns, columns)]),
+            (wide_hold, made[0]),
+            (right_ref, made[1]),
+            (value_grad_ref, made[2]),
+            (mixed_ref, made[3]),
+            (right_ref, made[4]),
+        ]
+        return pltpu.make_async_copy(*pairs[index], host_sem.at[index])
+
+    def load(*indices):
+        def thunk():
+            for index in indices:
+                host_load(index).start()
+
+        return thunk
+
+    def ready(*indices):
+        def thunk():
+            for index in indices:
+                host_load(index).wait()
+
+        return thunk
+
+    def send_right(*indices):
+        def thunk():
+            for index in indices:
+                right_copy(index).start()
+
+        return thunk
+
+    def pre_load(i):
+        return pltpu.make_async_copy(
+            hidden_pre.at[:, columns_at(i, tile)],
+            kept_ref.at[:, columns_at(i % 3, tile)],
+            kept_sem.at[i],
+        )
+
+    def write_part():
+        return pltpu.make_async_copy(attn_grad, part_grad, kept_sem.at[hidden_tiles])
+
+    def by_rows(fn):
+        def row_body(i, carry):
+            fn(pl.ds(pl.multiple_of(i * block_rows, block_rows), block_rows))
+            return carry
+
+        lax.fori_loop(0, length // block_rows, row_body, 0)
+
+    def put(row, value):
+        vector[row : row + 1, :] += jnp.sum(value, 0, keepdims=True)
+
+    def clear_total():
+        def rows_fn(at):
+            total_ref[at, :] = jnp.zeros((block_rows, columns), jnp.float32)
+
+        by_rows(rows_fn)
+
+    def begin():
+        vector[...] = jnp.zeros_like(vector)
+        mixed_ref[...] = jnp.zeros_like(mixed_ref)
+        tile_load(0, 0).start()
+        for i in range(3):
+            pre_load(i).start()
+        clear_total()
+
+    def hidden_step(i):
+        value = dot_trailing(right_ref[...], next_tile(0, i))
+        pre_load(i).wait()
+        value = value * gelu_slope(kept_ref[:, columns_at(i % 3, tile)])
+
+        @pl.when(i + 3 < hidden_tiles)
+        def _():
+            pre_load(i + 3).start()
+
+        rounded = value.astype(wide_hold.dtype)
+        wide_hold[:, columns_at(i, tile)] = rounded
+        sums_here = jnp.sum(rounded.astype(jnp.float32), 0, keepdims=True)
+        for side in range(2):
+
+            @pl.when(i // tiles == side)
+            def _():
+                vector[9 + side : 10 + side, columns_at(i % tiles, tile)] = sums_here
+
+    def norm_two_step(i):
+        left = wide_hold[:, columns_at(i % 2, columns)]
+        total_ref[:, columns_at(i // 2, tile)] += dot_trailing(left, next_tile(1, i))
+
+    def norm_two_back():
+        def rows_fn(at):
+            standard, inverse = normalize(kept_ref[at, :])
+            value = total_ref[at, :]
+            put(2, value * standard)
+            put(7, value)
+            cot = right_ref[at, :].astype(jnp.float32)
+            put(8, cot)
+            value = cot + norm_back(value * params[2:3, :], standard, inverse)
+            attn_grad[at, :] = value
+            rounded = value.astype(right_ref.dtype)
+            right_ref[at, :] = rounded
+            put(6, rounded.astype(jnp.float32))
+
+        by_rows(rows_fn)
+
+    def attended_step(i):
+        value = dot_trailing(right_ref[...], next_tile(2, i))
+        wide_hold[:, columns_at(i, tile)] = value.astype(wide_hold.dtype)
+
+    def probs_load(head):
+        return pltpu.make_async_copy(
+            probs.at[head], probs_ref.at[head % 2], probs_sem.at[head % 2]
+        )
+
+    def pair_step(index):
+        span = table_ref.shape[0]
+        row = lax.broadcasted_iota(jnp.int32, (length, length), 0)
+        column = lax.broadcasted_iota(jnp.int32, (length, length), 1)
+        mirror = jnp.where(row + column == length - 1, 1.0, 0.0).astype(jnp.bfloat16)
+        pair = columns_at(index, 2 * KEY)
+        key_pair = columns_at(index, 2 * KEY, key_ref.shape[1])
+        value_pair = columns_at(index, 2 * head_value)
+        far_pair = columns_at(index, 2 * head_value, columns)
+        made_here = [[], [], [], [], [], []]
+        for side in range(2):
+            head = 2 * index + side
+            probs_load(head).wait()
+            keys_at = slice(side * KEY, (side + 1) * KEY)
+            values_at = slice(side * head_value, (side + 1) * head_value)
+            prob = probs_ref[side]
+            out_grad = wide_hold[:, value_pair][:, values_at]
+            made_here[0].append(dot_leading(prob, out_grad).astype(jnp.bfloat16))
+            prob_grad = dot_trailing(out_grad, wide_hold[:, far_pair][:, values_at])
+            prob = prob.astype(jnp.float32)
+            row_dot = jnp.sum(prob * prob_grad, -1, keepdims=True)
+            rounded = (prob * (prob_grad - row_dot)).astype(jnp.bfloat16)
+            content = content_ref[:, pair][:, keys_at]
+            made_here[1].append(dot_leading(rounded, content).astype(jnp.bfloat16))
+            content_grad = jnp.dot(
+                rounded, key_ref[:, pair][:, keys_at], preferred_element_type=jnp.float32
+            )
+            mirrored = jnp.dot(rounded, mirror, preferred_element_type=jnp.float32)
+            wide = jnp.concatenate([mirrored, jnp.zeros((length, span - length), jnp.float32)], 1)
+            band = pltpu.roll(wide, 0, 1, stride=1, stride_axis=0).astype(jnp.bfloat16)
+            position_grad = jnp.dot(
+                band, table_ref[:, pair][:, keys_at], preferred_element_type=jnp.float32
+            )
+            position = position_ref[:, pair][:, keys_at]
+            made_here[2].append(dot_leading(band, position).astype(jnp.bfloat16))
+            made_here[3].append(((content_grad + position_grad) * KEY**-0.5).astype(jnp.bfloat16))
+            made_here[4].append(jnp.sum(content_grad, 0, keepdims=True))
+            made_here[5].append(jnp.sum(position_grad, 0, keepdims=True))
+        value_grad_ref[:, value_pair] = jnp.concatenate(made_here[0], 1)
+        mixed_ref[:, key_pair] = jnp.concatenate(made_here[1], 1)
+        table_grad_ref[:, pair] = jnp.concatenate(made_here[2], 1)
+        mixed_ref[:, pair] = jnp.concatenate(made_here[3], 1)
+        vector[11:12, pair] = jnp.concatenate(made_here[4], 1)
+        vector[11:12, key_pair] = jnp.concatenate(made_here[5], 1)
+
+        @pl.when(index + 1 < HEADS // 2)
+        def _():
+            for side in range(2):
+                probs_load(2 * index + 2 + side).start()
+
+    def rel_step():
+        for shard in range(groups):
+            value = dot_leading(table[...], table_grad_ref[:, shard * 128 : (shard + 1) * 128])
+            rel_grad[shard] = value.astype(rel_grad.dtype).reshape(rel_grad.shape[1:])
+        rel_copy().start()
+
+    def mixed_step(i):
+        left = mixed_ref[:, 0 : mixed_full.shape[1]]
+        total_ref[:, columns_at(i, tile)] = dot_trailing(left, next_tile(3, i))
+
+    def value_step(i):
+        total_ref[:, columns_at(i, tile)] += dot_trailing(value_grad_ref[...], next_tile(4, i))
+
+    def norm_one_back():
+        def rows_fn(at):
+            standard, inverse = normalize(kept_ref[at, :])
+            value = total_ref[at, :]
+            put(1, value * standard)
+            put(5, value)
+            value = attn_grad[at, :] + norm_back(value * params[1:2, :], standard, inverse)
+            attn_grad[at, :] = value
+            rounded = value.astype(right_ref.dtype)
+            right_ref[at, :] = rounded
+            put(4, rounded.astype(jnp.float32))
+
+        by_rows(rows_fn)
+
+    def conv_shift(tap):
+        move = tap - taps // 2
+
+        def column_body(i, carry):
+            at = columns_at(i, rows)
+            value = right_ref[:, at].astype(jnp.float32)
+            value = pltpu.roll(value, (move + length) % length, 0)
+            row = lax.broadcasted_iota(jnp.int32, value.shape, 0) - move
+            inside = jnp.logical_and(row >= 0, row < length)
+            wide_hold[:, at] = jnp.where(inside, value, 0.0).astype(wide_hold.dtype)
+            return carry
+
+        lax.fori_loop(0, columns // rows, column_body, 0)
+
+    def conv_step(i):
+        left = wide_hold[:, 0:columns]
+        total_ref[:, columns_at(i % tiles, tile)] += dot_trailing(left, next_tile(5, i))
+
+    def batch_back():
+        def rows_fn(at):
+            value = wide_hold[at, columns : 2 * columns].astype(jnp.float32)
+            standard = (value - params[4:5, :]) * params[5:6, :]
+            normed = standard * params[0:1, :] + params[3:4, :]
+            value = total_ref[at, :] * gelu_slope(normed)
+            put(0, value * standard)
+            put(3, value)
+            attn_grad[at, :] += params[5:6, :] * params[0:1, :] * value
+
+        by_rows(rows_fn)
+
+    def start_probs():
+        for head in range(2):
+            probs_load(head).start()
+
+    def step_zero():
+        begin()
+        ready(0)()
+        over(hidden_tiles, hidden_step)
+        load(9, 1)()
+        ready(9)()
+        send_right(1, 2)()
+
+    def step_one():
+        over(2 * tiles, norm_two_step)
+        load(3)()
+        ready(1)()
+        norm_two_back()
+        load(10, 2)()
+        start_probs()
+
+    def step_two():
+        over(tiles, attended_step)
+        ready(10)()
+        send_right(3)()
+        ready(3, 4, 5, 6, 7)()
+
+    def step_three():
+        load(11, 12, 8)()
+        rel_step()
+        ready(11, 12)()
+        send_right(4, 5)()
+
+    def step_four():
+        over(tiles, mixed_step)
+        over(tiles, value_step)
+        ready(2)()
+        norm_one_back()
+        load(13)()
+        ready(13)()
+        send_right(6)()
+        clear_total()
+
+    def step_last():
+        ready(8)()
+        batch_back()
+        write_part().start()
+
+    pairs_each = HEADS // 4
+
+    for copy in (0, 4, 5, 6, 7):
+        host_load(copy).start()
+
+    def host(n):
+        pl.when(n == 0)(step_zero)
+        pl.when(n == 1)(step_one)
+        pl.when(n == 2)(step_two)
+
+        @pl.when(jnp.logical_and(n >= 2, n < 4))
+        def _():
+            over(pairs_each, lambda i: pair_step((n - 2) * pairs_each + i))
+
+        pl.when(n == 3)(step_three)
+        pl.when(n == 4)(step_four)
+
+        @pl.when(jnp.logical_and(n >= 5, n < 5 + taps))
+        def _():
+            conv_shift(n - 5)
+            over(tiles, lambda i: conv_step((n - 5) * tiles + i))
+
+        pl.when(n == 4 + taps)(step_last)
 
     def body(n, carry):
         @pl.when(n < count)
@@ -919,12 +1321,16 @@
                         copy.wait()
                     if piece + 1 < count:
                         start_loads(piece + 1)
-                    if piece < taps and piece != taps // 2:
+                    if piece >= first_tap and piece != first_tap + taps // 2:
                         shift(piece)
 
             produce(n)
+            claim(n, 0)
+            claim(n, 1)
             for copy in one(n):
                 copy.start()
+
+        host(n)
 
         @pl.when(jnp.logical_and(n >= 1, n < count + 1))
         def _():
@@ -935,13 +1341,17 @@
 
             def shard_body(shard, carry):
                 for other in range(2):
-                    value = add(slot, x_one[piece, shard, other], first, shard, other, at_x)
+                    value = add(slot, x_one[piece % ring, shard, other], first, shard, other, at_x)
                     grad[slot, shard, other, at_x, :, first] = value.astype(grad.dtype)
-                    value = add(slot, y_one[piece, shard, other], last, shard, at_y, other)
+                    value = add(slot, y_one[piece % ring, shard, other], last, shard, at_y, other)
                     grad[slot, shard, at_y, other, :, last] = value.astype(grad.dtype)
                 return carry
 
             lax.fori_loop(0, groups, shard_body, 0)
+            pay(piece, 0, along_x)
+            pay(piece, 1, along_y)
+            claim(piece, 2)
+            claim(piece, 3)
             for copy in two(piece):
                 copy.start()
 
@@ -953,14 +1363,21 @@
                 copy.wait_recv()
 
             def shard_body(shard, carry):
-                value = add(slot, y_two[piece, shard], first, shard, at_y, at_x)
+                value = add(slot, y_two[piece % ring, shard], first, shard, at_y, at_x)
                 grad[slot, shard, at_y, at_x, :, first] = value.astype(grad.dtype)
-                value = add(slot, x_two[piece, shard], last, shard, at_y, at_x)
+                value = add(slot, x_two[piece % ring, shard], last, shard, at_y, at_x)
                 grad[slot, shard, at_y, at_x, :, last] = value.astype(grad.dtype)
                 return carry
 
             lax.fori_loop(0, groups, shard_body, 0)
+            pay(piece, 2, along_y)
+            pay(piece, 3, along_x)
             for j in range(others):
+
+                @pl.when(piece >= ring)
+                def _():
+                    pl.semaphore_wait(shard_credit.at[(me + 1 + j) % groups], 1)
+
                 shard_copy(piece, j).start()
 
         @pl.when(jnp.logical_and(n >= 3, n < count + 3))
@@ -969,10 +1386,18 @@
             value = grad[piece % slots, me, at_y, at_x].astype(jnp.float32)
             for j in range(others):
                 shard_arrival(piece, j).wait_recv()
-                value = value + shard_got[piece, (me + 1 + j) % groups].astype(jnp.float32)
+                value = value + shard_got[piece % ring, (me + 1 + j) % groups].astype(jnp.float32)
+
+            @pl.when(piece < count - ring)
+            def _():
+                for j in range(others):
+                    pl.semaphore_signal(
+                        shard_credit.at[me], inc=1, device_id=shards[j], device_id_type=MESH
+                    )
+
             if blocks > 1:
-                partial[piece] = value.astype(partial.dtype)
-                block_got[piece, block] = value.astype(partial.dtype)
+                done[piece] = value.astype(done.dtype)
+                block_got[piece, block] = value.astype(done.dtype)
                 for j in range(blocks - 1):
                     block_copy(piece, j).start()
                 for j in range(blocks - 1):
@@ -1007,13 +1432,14 @@
 
         for step in range(len(summing)):
 
-            @pl.when(n == step)
+            @pl.when(n == count + step - 1)
             def _():
                 summing[step]()
 
         return carry
 
     lax.fori_loop(0, count + 5, body, 0)
+    write_part().wait()
 
     def drain(piece, carry):
         @pl.when(piece >= count - slots)
@@ -1037,61 +1463,91 @@
         right_copy(index).wait_send()
 
 
-def reduce(groups, blocks, rel_at, lefts, rights, rel_grad, vector):
-    bins, columns = lefts[0].shape
+def reduce(groups, blocks, rel_at, lefts, saved, weights, heads, params, table):
+    hidden, _, _, _, activated = lefts
+    length, columns = activated.shape
     width = columns // 2
     rows = columns // groups
     part = rows // 4
-    dtype = lefts[0].dtype
+    dtype = activated.dtype
     count = 12
-    slots = 5
+    slots = 4
+    ring = 3 if blocks == 1 else 2
+    narrow = heads[2].shape
+    span = table.shape[0]
     kept = pl.BlockSpec(memory_space=pl.ANY)
     inside = pl.BlockSpec(memory_space=pltpu.VMEM)
     each = pltpu.SemaphoreType.DMA((count,))
+    wide = (length, columns)
+    rel_shape = (groups, 2, table.shape[1] // 2, 128)
+    sums = (16, columns)
+    inputs = [*lefts, *saved, *weights, *heads]
+    half_got = (ring, groups, part, width // 2)
+    two_got = (ring, groups, 2, part, width // 2)
     return pl.pallas_call(
         functools.partial(reduce_kernel, groups, blocks, rel_at),
         out_shape=(
             jax.ShapeDtypeStruct((count, rows, columns), dtype),
-            jax.ShapeDtypeStruct(vector.shape, jnp.float32),
-            jax.ShapeDtypeStruct((4, bins, columns), dtype),
-            jax.ShapeDtypeStruct(lefts[4].shape, dtype),
-            jax.ShapeDtypeStruct((len(rights) + 1, bins, width), dtype),
+            jax.ShapeDtypeStruct(sums, jnp.float32),
+            jax.ShapeDtypeStruct(wide, jnp.float32),
+            jax.ShapeDtypeStruct(hidden.shape, dtype),
+            jax.ShapeDtypeStruct(wide, dtype),
+            jax.ShapeDtypeStruct(wide, dtype),
+            jax.ShapeDtypeStruct(wide, dtype),
+            jax.ShapeDtypeStruct(wide, dtype),
+            jax.ShapeDtypeStruct(hidden.shape, dtype),
+            jax.ShapeDtypeStruct((4,) + wide, dtype),
+            jax.ShapeDtypeStruct((7, length, width), dtype),
         ),
-        in_specs=[kept] * (len(lefts) + len(rights)) + [inside] * 2,
-        out_specs=[kept, inside, kept, kept, kept],
+        in_specs=[kept] * len(inputs) + [inside] * 2,
+        out_specs=[kept, inside] + [kept] * 9,
         scratch_shapes=[
-            pltpu.VMEM((2, 2, bins, columns), dtype),
-            pltpu.VMEM((2, 2, bins, width), dtype),
+            pltpu.VMEM((2, 2) + wide, dtype),
+            pltpu.VMEM((2, 2, length, width), dtype),
             pltpu.VMEM((slots, groups, 2, 2, part, width), dtype),
-            pltpu.VMEM((count, groups, 2, part, width // 2), dtype),
-            pltpu.VMEM((count, groups, 2, part, width // 2), dtype),
-            pltpu.VMEM((count, groups, part, width // 2), dtype),
-            pltpu.VMEM((count, groups, part, width // 2), dtype),
-            pltpu.VMEM((count, groups, part, width), dtype),
+            pltpu.VMEM(two_got, dtype),
+            pltpu.VMEM(two_got, dtype),
+            pltpu.VMEM(half_got, dtype),
+            pltpu.VMEM(half_got, dtype),
+            pltpu.VMEM((ring, groups, part, width), dtype),
             pltpu.VMEM((count if blocks > 1 else 1, blocks, part, width), dtype),
-            pltpu.VMEM((count if blocks > 1 else 1, part, width), dtype),
             pltpu.VMEM((count, part, width), dtype),
-            pltpu.VMEM(rel_grad.shape, dtype),
-            pltpu.SemaphoreType.DMA((len(lefts),)),
-            pltpu.SemaphoreType.DMA((len(lefts),)),
-            pltpu.SemaphoreType.DMA((len(rights) + 1,)),
-            pltpu.SemaphoreType.DMA((len(rights) + 1,)),
-            pltpu.SemaphoreType.DMA((1,)),
-            pltpu.SemaphoreType.DMA((1,)),
+            pltpu.VMEM(rel_shape, dtype),
+            pltpu.VMEM(rel_shape, dtype),
+            pltpu.VMEM(sums, jnp.float32),
+            *([pltpu.SemaphoreType.DMA((5,))] * 2),
+            *([pltpu.SemaphoreType.DMA((7,))] * 2),
+            *([pltpu.SemaphoreType.DMA((1,))] * 2),
             pltpu.SemaphoreType.DMA((2, 2 + 2 * groups)),
             *([each] * 8),
-            pltpu.SemaphoreType.DMA((count, groups)),
-            pltpu.SemaphoreType.DMA((count, groups)),
-            pltpu.SemaphoreType.DMA((count, blocks)),
-            pltpu.SemaphoreType.DMA((count, blocks)),
+            *([pltpu.SemaphoreType.DMA((count, groups))] * 2),
+            *([pltpu.SemaphoreType.DMA((count, blocks))] * 2),
             *([each] * 6),
-            *sum_scratch(groups, blocks, vector.shape),
+            *sum_scratch(groups, blocks, sums),
+            pltpu.SemaphoreType.REGULAR((4,)),
+            pltpu.SemaphoreType.REGULAR((groups,)),
+            pltpu.VMEM(wide, jnp.float32),
+            pltpu.VMEM(wide, jnp.float32),
+            pltpu.VMEM(wide, jnp.float32),
+            pltpu.VMEM((2, 512, columns), dtype),
+            pltpu.VMEM(hidden.shape, dtype),
+            pltpu.VMEM(wide, dtype),
+            pltpu.VMEM(wide, dtype),
+            pltpu.VMEM(wide, dtype),
+            *([pltpu.VMEM(narrow, dtype)] * 3),
+            pltpu.VMEM((span, narrow[1]), dtype),
+            pltpu.VMEM((span, narrow[1]), dtype),
+            pltpu.VMEM((2, length, length), dtype),
+            pltpu.SemaphoreType.DMA((2,)),
+            pltpu.SemaphoreType.DMA((14,)),
+            pltpu.SemaphoreType.DMA((2,)),
+            pltpu.SemaphoreType.DMA((hidden.shape[1] // 512 + 1,)),
         ],
         compiler_params=pltpu.CompilerParams(
-            collective_id=1, has_side_effects=True, vmem_limit_bytes=60 << 20
+            collective_id=1, has_side_effects=True, vmem_limit_bytes=VMEM_LIMIT
         ),
         name="reduce",
-    )(*lefts, *rights, rel_grad, vector)
+    )(*inputs, params, table)
 
 
 EPSILON = 1e-05
@@ -1144,112 +1600,6 @@
     return lax.dot_general(
         left_side, right_side, (((1,), (1,)), ((), ())), preferred_element_type=jnp.float32
     )
-
-
-def attend_back_kernel(
-    probs_ref,
-    out_ref,
-    value_ref,
-    key_ref,
-    content_ref,
-    position_ref,
-    table_ref,
-    query_grad_ref,
-    key_grad_ref,
-    value_grad_ref,
-    table_grad_ref,
-    offset_ref,
-):
-    length = content_ref.shape[0]
-    span = table_ref.shape[0]
-    head_value = value_ref.shape[1] // 2
-    row = lax.broadcasted_iota(jnp.int32, (length, length), 0)
-    column = lax.broadcasted_iota(jnp.int32, (length, length), 1)
-    mirror = jnp.where(row + column == length - 1, 1.0, 0.0).astype(jnp.bfloat16)
-    for head in range(2):
-        keys = slice(head * KEY, (head + 1) * KEY)
-        values = slice(head * head_value, (head + 1) * head_value)
-        probs = probs_ref[head]
-        out_grad = out_ref[:, values]
-        value_grad_ref[:, values] = dot_leading(probs, out_grad).astype(jnp.bfloat16)
-        prob_grad = dot_trailing(out_grad, value_ref[:, values])
-        probs = probs.astype(jnp.float32)
-        row_dot = jnp.sum(probs * prob_grad, -1, keepdims=True)
-        score_grad = probs * (prob_grad - row_dot)
-        rounded = score_grad.astype(jnp.bfloat16)
-        key_grad_ref[:, keys] = dot_leading(rounded, content_ref[:, keys]).astype(jnp.bfloat16)
-        content_grad = jnp.dot(rounded, key_ref[:, keys], preferred_element_type=jnp.float32)
-        mirrored = jnp.dot(rounded, mirror, preferred_element_type=jnp.float32)
-        wide = jnp.concatenate([mirrored, jnp.zeros((length, span - length), jnp.float32)], 1)
-        band = pltpu.roll(wide, 0, 1, stride=1, stride_axis=0)
-        band = band.astype(jnp.bfloat16)
-        position_grad = jnp.dot(band, table_ref[:, keys], preferred_element_type=jnp.float32)
-        table_grad_ref[:, keys] = dot_leading(band, position_ref[:, keys]).astype(jnp.bfloat16)
-        query_grad_ref[:, keys] = ((content_grad + position_grad) * KEY**-0.5).astype(
-            jnp.bfloat16
-        )
-        offset_ref[0:1, keys] = jnp.sum(content_grad, 0, keepdims=True)
-        offset_ref[1:2, keys] = jnp.sum(position_grad, 0, keepdims=True)
-
-
-def attend_back(probs, out_grad, value, key, content, position, table):
-    length = content.shape[0]
-    span = table.shape[0]
-    steps = HEADS // 2
-
-    def columns(array):
-        return pl.BlockSpec((array.shape[0], array.shape[1] // steps), lambda i: (0, i))
-
-    offsets = jax.ShapeDtypeStruct((2, key.shape[1]), jnp.float32)
-    return pl.pallas_call(
-        attend_back_kernel,
-        grid=(steps,),
-        in_specs=[pl.BlockSpec((2, length, length), lambda i: (i, 0, 0))]
-        + [columns(array) for array in (out_grad, value, key, content, position, table)],
-        out_specs=[columns(array) for array in (content, key, value, table, offsets)],
-        out_shape=[
-            jax.ShapeDtypeStruct(array.shape, jnp.bfloat16)
-            for array in (content, key, value, table)
-        ]
-        + [offsets],
-        compiler_params=pltpu.CompilerParams(vmem_limit_bytes=40 << 20),
-        cost_estimate=pl.CostEstimate(
-            flops=4 * length * (HEADS * KEY * (length + span) + length * value.shape[1]),
-            bytes_accessed=2 * HEADS * length * length,
-            transcendentals=0,
-        ),
-        name="attend_back",
-    )(probs, out_grad, value, key, content, position, table)
-
-
-def conv_back_kernel(left_ref, right_ref, out_ref):
-    @pl.when(pl.program_id(0) == 0)
-    def _():
-        out_ref[...] = jnp.zeros_like(out_ref)
-
-    out_ref[...] += dot_trailing(left_ref[...], right_ref[0])
-
-
-def conv_back(left, right):
-    length = left.shape[0]
-    taps, columns = right.shape[:2]
-    return pl.pallas_call(
-        conv_back_kernel,
-        grid=(taps,),
-        in_specs=[
-            pl.BlockSpec((length, columns), lambda i: (0, i)),
-            pl.BlockSpec((1, columns, columns), lambda i: (i, 0, 0)),
-        ],
-        out_specs=pl.BlockSpec((length, columns), lambda i: (0, 0)),
-        out_shape=jax.ShapeDtypeStruct((length, columns), jnp.float32),
-        compiler_params=pltpu.CompilerParams(vmem_limit_bytes=40 << 20),
-        cost_estimate=pl.CostEstimate(
-            flops=2 * taps * length * columns * columns,
-            bytes_accessed=2 * taps * columns * (columns + length),
-            transcendentals=0,
-        ),
-        name="conv_back",
-    )(left, right)
 
 
 def on_device(
@@ -1353,9 +1703,6 @@
     variance = batch_sums[1] / token_total - centre * centre
     inverse = lax.rsqrt(variance + EPSILON)
     standard = (inputs - centre) * inverse
-    normed = standard * gain_rows[0] + bias_rows[0]
-    standard_one, inverse_one = normalize(after_conv)
-    standard_two, inverse_two = normalize(after_attention)
     hidden_pre = jnp.dot(normed_two, up_full, preferred_element_type=jnp.float32) + up_offset
     hidden = jax.nn.gelu(hidden_pre).astype(jnp.bfloat16)
     outputs = (
@@ -1368,102 +1715,43 @@
     selector = (clip_index[0][:, None] == levels[None, :]).astype(jnp.float32)
     limits = jnp.sum(selector * clip_levels[None, :], 1)[:, None]
     cotangent = jnp.clip(outputs - target_row, -limits, limits).astype(jnp.bfloat16)
-    cot_value = cotangent.astype(jnp.float32)
-    grad_down_bias = jnp.sum(cot_value, 0)
-    hidden_grad = dot_trailing(cotangent, down_full)
-    gelu_pull = jax.vjp(jax.nn.gelu, hidden_pre)[1]
-    pre_grad = gelu_pull(hidden_grad)[0].astype(jnp.bfloat16)
-    grad_up_bias = jnp.sum(pre_grad.astype(jnp.float32), 0)
-    normed_two_grad = dot_trailing(pre_grad, up_full)
-    grad_gain_two = jnp.sum(normed_two_grad * standard_two, 0)
-    grad_bias_two = jnp.sum(normed_two_grad, 0)
-    attention_grad = cot_value + norm_back(
-        normed_two_grad * gain_rows[2], standard_two, inverse_two
+    params = jnp.concatenate([gain_rows, bias_rows[:1], centre[None], inverse[None]], 0)
+    params = jnp.pad(params, ((0, 2), (0, 0)))
+    pieces, sums, part_grad, *_ = reduce(
+        groups,
+        blocks,
+        2 * key_width - half_width,
+        [hidden, normed_two, attended, normed_one, activated],
+        [cotangent, hidden_pre, after_attention, after_conv, tokens[0]],
+        [down_full, up_full, out_full, value_full, mixed_full, conv_full],
+        [probs, values, keys, content_query, position_query, mirrored_keys],
+        params,
+        tables[1],
     )
-    branch_grad = attention_grad.astype(jnp.bfloat16)
-    grad_out_bias = jnp.sum(branch_grad.astype(jnp.float32), 0)
-    attended_grad = dot_trailing(branch_grad, out_full).astype(jnp.bfloat16)
-    query_grad, key_grad, value_grad, table_grad, grad_rel_bias = attend_back(
-        probs, attended_grad, values, keys, content_query, position_query, mirrored_keys
-    )
-    mixed_grad = jnp.concatenate([query_grad, key_grad], 1)
-    normed_one_grad = (
-        dot_trailing(mixed_grad, mixed_full)
-        + dot_trailing(value_grad, value_full)
-    )
-    grad_gain_one = jnp.sum(normed_one_grad * standard_one, 0)
-    grad_bias_one = jnp.sum(normed_one_grad, 0)
-    conv_side_grad = attention_grad + norm_back(
-        normed_one_grad * gain_rows[1], standard_one, inverse_one
-    )
-    conv_grad = conv_side_grad.astype(jnp.bfloat16)
-    grad_conv_bias = jnp.sum(conv_grad.astype(jnp.float32), 0)
-    padded = jnp.pad(conv_grad, ((half_taps, half_taps), (0, 0)))
-    stacked_grad = jnp.concatenate(
-        [padded[tap : tap + length] for tap in reversed(range(tap_count))], 1
-    )
-    activated_grad = conv_back(stacked_grad, conv_full)
-    act_pull = jax.vjp(jax.nn.gelu, normed)[1]
-    normed_grad = act_pull(activated_grad)[0]
-    sum_parts = [
-        jnp.sum(normed_grad * standard, 0),
-        grad_gain_one,
-        grad_gain_two,
-        jnp.sum(normed_grad, 0),
-        grad_conv_bias,
-        grad_bias_one,
-        grad_out_bias,
-        grad_bias_two,
-        grad_down_bias,
-        grad_up_bias,
-        grad_rel_bias.reshape(-1),
-    ]
-    sums = jnp.concatenate(sum_parts)
-    sums = jnp.pad(sums, (0, -sums.shape[0] % 1024)).reshape(-1, 128)
-    grad_rel = dot_leading(tables[1], table_grad).astype(jnp.bfloat16)
-    grad_rel = jnp.moveaxis(grad_rel.reshape(rel_rows, groups, rel_columns), 0, 1)
-    grad_rel = grad_rel.reshape(groups, 2, rel_rows // 2, rel_columns)
-    mixed_wide = jnp.pad(mixed_grad, ((0, 0), (0, model_width - 2 * key_width)))
-    lefts = [activated, normed_one, attended, normed_two, hidden]
-    rights = [
-        conv_grad,
-        mixed_wide,
-        value_grad,
-        branch_grad,
-        pre_grad,
-        cotangent,
-    ]
-    pieces, sums, _, _, _ = reduce(
-        groups, blocks, 2 * key_width - half_width, lefts, rights, grad_rel, sums
-    )
-    flat = sums.reshape(-1)
-    bn_sums = flat[: 4 * model_width].reshape(4, model_width)
-    input_grad = conv_side_grad + inverse * (
-        normed_grad * gain_rows[0]
-        - gain_rows[0] * (bn_sums[3] + standard * bn_sums[0]) / token_total
-    )
+    input_grad = part_grad - inverse * gain_rows[0] * (
+        sums[3] + standard * sums[0]
+    ) / token_total
     shard = lax.axis_index("fsdp")
-    by_shard = flat[: 9 * model_width].reshape(9, groups, -1)
+    by_shard = sums[:9].reshape(9, groups, -1)
     by_shard = lax.dynamic_index_in_dim(by_shard, shard, 1, keepdims=False)
-    up_sums = flat[9 * model_width : 11 * model_width].reshape(groups, -1)
+    up_sums = sums[9:11].reshape(groups, -1)
     up_sums = lax.dynamic_index_in_dim(up_sums, shard, 0, keepdims=False)
-    rel_sums = flat[11 * model_width : 11 * model_width + 2 * key_width]
-    rel_sums = rel_sums.reshape(2, groups, -1)
+    rel_sums = sums[11, : 2 * key_width].reshape(2, groups, -1)
     rel_sums = lax.dynamic_index_in_dim(rel_sums, shard, 1, keepdims=False)
-    up_grad = jnp.concatenate([pieces[8], pieces[9]], 1)
-    mixed_sum = pieces[5].astype(jnp.float32)
+    up_grad = jnp.concatenate([pieces[2], pieces[3]], 1)
+    mixed_sum = pieces[6].astype(jnp.float32)
     rel_at = 2 * key_width
     return (
         outputs.astype(jnp.bfloat16)[None],
         input_grad.astype(jnp.bfloat16)[None],
-        pieces[:5].astype(jnp.float32),
+        pieces[7:12].astype(jnp.float32),
         mixed_sum[:, :key_width],
         mixed_sum[:, key_width:rel_at],
-        pieces[6].astype(jnp.float32),
-        pieces[7].astype(jnp.float32),
+        pieces[5].astype(jnp.float32),
+        pieces[4].astype(jnp.float32),
         mixed_sum[:rel_rows, rel_at : rel_at + rel_columns],
         up_grad.astype(jnp.float32),
-        pieces[10:12].reshape(2 * piece_rows, -1).astype(jnp.float32),
+        pieces[:2].reshape(2 * piece_rows, -1).astype(jnp.float32),
         by_shard[:3],
         by_shard[3:9],
         up_sums,

time: 675 us -> 605 us (0.90)
  matrix products: 51.5 us -> 17.7 us
  Pallas kernels: 551 us -> 526 us
  other arithmetic: 48.9 us -> 38.2 us
    pallas_call x2 -> x0, Pallas kernels: 34.6 us -> none  [the longest x1 18.2 us: attend_back(): pl.pallas_call(attend_back_kernel, grid=(steps,), in_specs=[pl.BlockSpec(...]
    dot_general x6 -> x0, matrix products: 33.9 us -> none  [the longest x5 33 us: dot_trailing(): lax.dot_general(left_side, right_side, (((1,), (1,)), ((), ())), preferre...]
    reduce_sum x7 -> x0, other arithmetic: 14.1 us -> none  [the longest x1 5.26 us: on_device(): jnp.sum(normed_grad, 0)]
    pallas_call x1, Pallas kernels: 315 us -> 325 us  [reduce(): pl.pallas_call(functools.partial(reduce_kernel, groups, blocks, rel_at),...]
where the time goes in v5:
time: 605 us; the launch traced here: 595 us
  Pallas kernels  526 us (87%)
  other arithmetic  38.2 us (6%)
  matrix products  17.7 us (3%)
  local copies, waits for them, and re-layouts  11.1 us (2%)
    pallas_call x1, Pallas kernels, reduce(): pl.pallas_call(functools.partial(reduce_kernel, groups, blocks, rel_at),...  325 us
    pallas_call x1, Pallas kernels, gather(): pl.pallas_call(functools.partial(gather_kernel, groups, blocks), out_shap...  201 us

profile of v5, /device:TPU:0, one launch (start us, length us, event | category | flops | bytes accessed | tf_op | source)
XLA Modules:
  0.0 595.1 jit_solution(12535716515744263719)
XLA Ops:
  0.6 0.0 copy-start
  1.4 0.1 fusion.63
  1.5 0.1 multiply_add_fusion.2
  1.6 0.8 select_reduce_fusion
  2.4 0.0 copy-done
  2.5 0.7 reshape.231
  3.2 0.6 fusion.36
  3.8 0.7 reshape.232
  4.5 1.3 fusion.43.refs_8_
  5.8 1.8 convert_reduce_fusion
  7.7 0.6 pad_maximum_fusion.1.refs_9_
  8.3 0.9 fusion.41
  9.2 0.3 fusion.37
  9.5 0.3 fusion.39
  9.9 0.5 fusion.34
  10.4 0.5 fusion.33
  10.8 0.6 fusion.29
  11.4 0.6 fusion.71
  12.0 1.4 fusion.32.refs_23_
  13.4 1.2 pad_maximum_fusion.refs_11_
  14.5 200.9 %gather.1 = (bf16[5,4,384,1536]{3,2,1,0:T(8,128)(2,1)}, bf16[4,384,1024]{2,1,0:T(8,128)(2,1)}, bf16[4,384,1536]{2,1,0:T(8,128)(2,1)}, bf16[4,384,1536]{2,1,0:T(8...) custom-call(bf16[5,384,1536]{2,1,0:T(8,128)(2,1)} %refs_0_.1, ...), custom_call_target="tpu_custom_call" | custom-call | tf_op jit(solution)/shard_map/gather/pallas_call | solution.py:612
  215.5 0.9 copy.47
  216.4 0.0 slice-start
  216.5 0.8 fusion.64
  217.3 0.8 fusion.46
  218.1 0.7 select_maximum_fusion.refs_22_
  218.8 0.0 slice-start.1
  218.8 0.0 slice-start.2
  218.8 0.0 copy-start.3
  218.8 11.0 %broadcast_add_fusion = (f32[512,3072]{1,0:T(8,128)}, bf16[512,3072]{1,0:T(8,128)(2,1)S(1)}) fusion(f32[3072]{0:T(1024)S(1)} %add.142, bf16[512,1536]{1,0:T(8,128)(2,1)} %get-tuple-element.40.refs_1_, bf16[1536,3072]{1,0:T(8,128)(2,1)} %bitcast.105), kind=kOutput, calls=%fused_computation.24 | convolution fusion | flops 4847566848 | bytes 20459520 | tf_op jit(solution)/shard_map/dot_general | solution.py:1706
  229.8 0.0 copy-start.4
  229.8 0.0 slice-done
  229.8 0.0 slice-done.1
  229.8 0.0 slice-done.2
  229.8 0.0 copy-done.3
  229.9 6.7 %minimum_convert_fusion = (bf16[512,1536]{1,0:T(8,128)(2,1)}, bf16[512,1536]{1,0:T(8,128)(2,1)}) fusion(f32[1536]{0:T(1024)S(1)} %dynamic-slice_reduce_fusion, bf16[512]{0:T(512)(128)(2,1)S(1)} %neg.8, f32[512]{0:T(512)S(1)} %select_reduce_fusion, f32[1536]{0:T(1024)S(1)} %add.149, f32[512,1536]{1,0:T(8,128)S(1)} %copy-done.3, ...), kind=kOutput, calls=%fused_computation.23 | convolution fusion | flops 4838916096 | bytes 18889728 | tf_op jit(solution)/shard_map/dot_general | solution.py:1710
  236.5 0.0 copy-done.4
  236.5 0.0 copy-start.2
  236.5 325.2 %reduce.9 = (bf16[12,384,1536]{2,1,0:T(8,128)(2,1)}, f32[16,1536]{1,0:T(8,128)}, f32[512,1536]{1,0:T(8,128)}, bf16[512,3072]{1,0:T(8,128)(2,1)}, bf16[512,1536]{...) custom-call(bf16[512,3072]{1,0:T(8,128)(2,1)} %copy-done.4, ...), custom_call_target="tpu_custom_call" | custom-call | tf_op jit(solution)/shard_map/reduce/pallas_call | solution.py:1487
  561.7 0.8 slice.116
  562.4 0.6 constant_dynamic-slice_fusion.1
  563.0 0.8 slice.115
  563.8 0.6 dynamic-slice_reduce_fusion.1
  564.5 0.9 slice_reduce_fusion.1
  565.4 0.0 copy-done.2
  565.4 0.0 copy-start.5
  565.4 3.9 fusion.17
  569.3 0.0 copy-done.5
  569.4 0.6 copy.49
  570.0 0.6 copy.48
  570.6 1.8 slice.109
  572.4 3.0 bitcast_convert_fusion
  575.4 5.7 slice_bitcast_fusion.1
  581.2 8.8 %slice_convert_fusion = f32[5,384,1536]{2,1,0:T(8,128)} fusion(bf16[12,384,1536]{2,1,0:T(8,128)(2,1)} %get-tuple-element.61), kind=kLoop, calls=%fused_computation.9 | loop fusion | flops 2949120 | bytes 17694720 | tf_op jit(solution)/shard_map/convert_element_type | solution.py:1747
  590.0 0.7 slice.125
  590.6 1.3 fusion.66
  591.9 0.0 copy-start.1
  591.9 2.8 maximum_convert_fusion
  594.6 0.0 copy-done.1
  (27 shorter events, 0.3 us)
Async XLA Ops:
  0.6 1.8 copy-start
  216.4 13.4 %slice-start = ((s8[9437184]{0:T(1024)(128)(4,1)}), s8[1048576]{0:T(1024)(128)(4,1)S(1)}, s32[]{:S(2)}) async-start(s8[9437184]{0:T(1024)(128)(4,1)} %bitcast.108), calls=%async_computation | async-start | bytes 2097152
  218.8 11.1 %slice-start.1 = ((s8[9437184]{0:T(1024)(128)(4,1)}), s8[4194304]{0:T(1024)(128)(4,1)S(1)}, s32[]{:S(2)}) async-start(s8[9437184]{0:T(1024)(128)(4,1)} %bitcast.108), calls=%async_computation.1 | async-start | bytes 8388608
  218.8 11.1 %slice-start.2 = ((s8[9437184]{0:T(1024)(128)(4,1)}), s8[4194304]{0:T(1024)(128)(4,1)S(1)}, s32[]{:S(2)}) async-start(s8[9437184]{0:T(1024)(128)(4,1)} %bitcast.108), calls=%async_computation.2 | async-start | bytes 8388608
  218.8 11.1 %copy-start.3 = (f32[512,1536]{1,0:T(8,128)S(1)}, f32[512,1536]{1,0:T(8,128)}, u32[]{:S(2)}) copy-start(f32[512,1536]{1,0:T(8,128)} %get-tuple-element.39.refs_7_) | copy-start | bytes 9437188
  229.8 6.7 %copy-start.4 = (bf16[512,3072]{1,0:T(8,128)(2,1)}, bf16[512,3072]{1,0:T(8,128)(2,1)S(1)}, u32[]{:S(2)}) copy-start(bf16[512,3072]{1,0:T(8,128)(2,1)S(1)} %get-tuple-element.78.refs_0_) | copy-start | bytes 9437188
  236.5 328.9 %copy-start.2 = (bf16[1,512,1536]{2,1,0:T(8,128)(2,1)S(1)}, bf16[1,512,1536]{2,1,0:T(8,128)(2,1)}, u32[]{:S(2)}) copy-start(bf16[1,512,1536]{2,1,0:T(8,128)(2,1)} %param.21) | copy-start | bytes 4718596
  565.4 4.0 copy-start.5
  591.9 2.8 copy-start.1

commit v6 on v5

--- a/solution.py
+++ b/solution.py
@@ -143,20 +143,28 @@
 def gather_kernel(groups, blocks, *refs):
     weights = refs[:8]
     conv, query, key, value, out, up, down, rel = weights
-    small, stats, inputs, tables = refs[8:12]
+    small, inputs, target, limits = refs[8:12]
     outs = refs[12:21]
     conv_out, mixed_out, value_out, out_out, up_out, down_out = outs[:6]
     rel_full, small_full, stat_total = outs[6:]
-    results = refs[21:33]
-    hold, hold_mixed, local_sem, write_sem = refs[33:37]
-    z_sem, x_sem, y_sem, d_sem, sib_sem, send_sem, right_send, left_send = refs[37:45]
-    rel_send, rel_recv, small_send, small_recv = refs[45:49]
-    near_got, sums, shard_got, block_got = refs[49:53]
-    sum_sems = refs[53:59]
-    weight_hold, weight_sem, result_sem = refs[59:62]
-    params, shifted_ref, total_ref = refs[62:65]
-    act_ref, norm_ref, content_ref, position_ref, key_ref, value_ref = refs[65:71]
-    table_ref, probs_ref, attended_ref = refs[71:74]
+    results = list(refs[21:37])
+    pre_out = results.pop(12)
+    hidden_out = results.pop(12)
+    results[12:12] = [
+        hidden_out.at[:, pl.ds(side * conv.shape[2], conv.shape[2])] for side in range(2)
+    ]
+    tables = refs[37]
+    refs = refs[38:]
+    hold, hold_mixed, local_sem, write_sem = refs[:4]
+    z_sem, x_sem, y_sem, d_sem, sib_sem, send_sem, right_send, left_send = refs[4:12]
+    rel_send, rel_recv, small_send, small_recv = refs[12:16]
+    near_got, sums, shard_got, block_got = refs[16:20]
+    sum_sems = refs[20:26]
+    weight_hold, weight_sem, result_sem = refs[26:29]
+    params, shifted_ref, total_ref = refs[29:32]
+    act_ref, norm_ref, content_ref, position_ref, key_ref, value_ref = refs[32:38]
+    table_ref, probs_ref, attended_ref = refs[38:41]
+    stats, loss_ref, part_sem, part_right, part_left = refs[41:46]
     dp = lax.axis_index("dp")
     me = lax.axis_index("fsdp")
     near, shards, far = peers_of(groups, blocks)
@@ -197,8 +205,6 @@
     summing = sum_steps(
         groups, blocks, stats, stat_total, near_got, sums, shard_got, block_got, sum_sems
     )
-    summing[0]()
-
     for j in range(others):
         remote(
             rel, rel_full.at[me], rel_send.at[j], rel_recv.at[me], shards[j]
@@ -243,6 +249,44 @@
             z_sem.at[piece, shard],
             (dp, (me + groups - 1) % groups),
         )
+
+    last = count - 1
+
+    def part_copy(step, shard, device, sems, src=None):
+        dst = slice_of(last, shard, 2 * step + dp % 2)
+        return remote(
+            dst if src is None else src,
+            dst,
+            sems.at[step, shard],
+            part_sem.at[step, shard],
+            (dp, device),
+        )
+
+    def part_send(step):
+        at = pl.ds(pl.multiple_of((2 * step + dp % 2) * part, 16), part)
+        src = holds[last].at[at]
+
+        @pl.when(me + 1 < groups)
+        def _():
+            part_copy(step, me, (me + 1) % groups, part_right, src).start()
+
+        @pl.when(me > 0)
+        def _():
+            part_copy(step, me, (me + groups - 1) % groups, part_left, src).start()
+
+    def part_stage(step, shard):
+        part_copy(step, shard, me, part_right).wait_recv()
+
+        @pl.when(jnp.logical_and(shard < me, me + 1 < groups))
+        def _():
+            part_copy(step, shard, (me + 1) % groups, part_right).start()
+
+        @pl.when(jnp.logical_and(shard > me, me > 0))
+        def _():
+            part_copy(step, shard, (me + groups - 1) % groups, part_left).start()
+
+        ref = slice_of(last, shard, 2 * step + dp % 2)
+        remote(ref, ref, send_sem.at[last], sib_sem.at[last], (sib, me)).start()
 
     def z_send(piece):
         src = holds[piece].at[pl.ds(pl.multiple_of(dp % 8 * part, 16), part)]
@@ -335,7 +379,7 @@
 
     length = inputs.shape[0]
     block_rows = 128
-    tile = 512
+    tile = 256
     per_row = rows // 128
     token_total = length * 8 * blocks * groups
 
@@ -345,6 +389,20 @@
             return carry
 
         lax.fori_loop(0, length // block_rows, row_body, 0)
+
+    def local_sums():
+        stats[...] = jnp.zeros_like(stats)
+        lanes = columns // 128
+
+        def rows_fn(at):
+            value = inputs[at, :].astype(jnp.float32)
+            total = jnp.sum(value, 0, keepdims=True)
+            square = jnp.sum(value * value, 0, keepdims=True)
+            for j in range(lanes):
+                stats[j : j + 1, :] += total[:, j * 128 : (j + 1) * 128]
+                stats[lanes + j : lanes + j + 1, :] += square[:, j * 128 : (j + 1) * 128]
+
+        by_rows(rows_fn)
 
     def unpack():
         for row in range(9):
@@ -363,6 +421,13 @@
             params[10:11, j * 128 : (j + 1) * 128] = lax.rsqrt(
                 square - centre * centre + EPSILON
             )
+        for shard in range(groups):
+            for j in range(2 * per_row):
+                source = 9 * per_row + j
+                at = (shard * 2 * per_row + j) * 128
+                params[13 + at // columns : 14 + at // columns, at % columns : at % columns + 128] = (
+                    small_full[shard, source : source + 1, :]
+                )
         taken = (9 * rows + 2 * rows) // 128
         for side in range(2):
             for shard in range(groups):
@@ -392,10 +457,18 @@
         attended_ref,
         total_ref,
         norm_ref,
+        shifted_ref,
+        act_ref,
+        attended_ref,
+        norm_ref,
     ]
 
     def write_result(index):
         return pltpu.make_async_copy(result_of[index], results[index], result_sem.at[index])
+
+    def write_pre(half):
+        at = pl.ds(half * columns, columns)
+        return pltpu.make_async_copy(loss_ref, pre_out.at[:, at], result_sem.at[16 + half])
 
     def shift_tap(tap):
         move = tap - 2
@@ -412,7 +485,7 @@
         lax.fori_loop(0, columns // rows, column_body, 0)
 
     def conv_tap(tap, i):
-        at = pl.ds(i * tile, tile)
+        at = pl.ds(pl.multiple_of(i * tile, 128), tile)
         left = act_ref if tap == 2 else shifted_ref
         value = jnp.dot(
             left[...], weight_hold[tap % 2, :, at], preferred_element_type=jnp.float32
@@ -453,52 +526,127 @@
                 ).astype(table_ref.dtype)
 
     def value_step(i):
-        at = pl.ds(i * tile, tile)
+        at = pl.ds(pl.multiple_of(i * tile, 128), tile)
         value_ref[:, at] = jnp.dot(
             norm_ref[...], weight_hold[0, :, at], preferred_element_type=jnp.float32
         ).astype(value_ref.dtype)
 
-    def head_step(head):
+    def head_step(index, side):
         head_value = columns // HEADS
         span = tables.shape[1]
-        pair = slice(head // 2 * 2 * KEY, (head // 2 + 1) * 2 * KEY)
-        value_pair = slice(head // 2 * 2 * head_value, (head // 2 + 1) * 2 * head_value)
-        keys = slice(head % 2 * KEY, (head % 2 + 1) * KEY)
+        pair = pl.ds(pl.multiple_of(index * 2 * KEY, 128), 2 * KEY)
+        value_pair = pl.ds(pl.multiple_of(index * 2 * head_value, 128), 2 * head_value)
+        keys = slice(side * KEY, (side + 1) * KEY)
         band = dot_trailing(position_ref[:, pair][:, keys], table_ref[0, :, pair][:, keys])
         moved = pltpu.roll(band, span - length + 1, 1, stride=1, stride_axis=0)
         scores = dot_trailing(content_ref[:, pair][:, keys], key_ref[:, pair][:, keys])
         scores = scores + moved[:, :length]
         weight = jnp.exp(scores - jnp.max(scores, -1, keepdims=True))
         probs = (weight / jnp.sum(weight, -1, keepdims=True)).astype(probs_ref.dtype)
-        probs_ref[head] = probs
-        chosen = value_ref[:, value_pair][
-            :, head % 2 * head_value : (head % 2 + 1) * head_value
-        ]
+        probs_ref[2 * index + side] = probs
+        chosen = value_ref[:, value_pair][:, side * head_value : (side + 1) * head_value]
         return jnp.dot(probs, chosen, preferred_element_type=jnp.float32)
 
     def pair_step(index):
-        both = [head_step(2 * index + side).astype(attended_ref.dtype) for side in range(2)]
+        both = [head_step(index, side).astype(attended_ref.dtype) for side in range(2)]
         wide = 2 * columns // HEADS
-        attended_ref[:, index * wide : (index + 1) * wide] = jnp.concatenate(both, 1)
+        attended_ref[:, pl.ds(pl.multiple_of(index * wide, 128), wide)] = jnp.concatenate(both, 1)
 
     def out_step(i):
-        at = pl.ds(i * tile, tile)
+        at = pl.ds(pl.multiple_of(i * tile, 128), tile)
         value = jnp.dot(
             attended_ref[...], weight_hold[1, :, at], preferred_element_type=jnp.float32
         )
         total_ref[:, at] = total_ref[:, at] + value + params[6:7, at]
 
-    tiles = range(columns // tile)
+    def make_tables():
+        features = rel.shape[0]
+        basis = features // 6
+        span = tables.shape[1]
+        row = lax.broadcasted_iota(jnp.int32, (span, features), 0)
+        column = lax.broadcasted_iota(jnp.int32, (span, features), 1)
+        offset = row - (length - 1)
+        whole = jnp.abs(offset)
+        distance = whole.astype(jnp.float32)
+        order_at = column % basis
+        index = order_at.astype(jnp.float32)
+        ratio = index / (basis - 1)
+        half_life = jnp.exp2(3.0 + (math.log2(length) - 3.0) * ratio)
+        decaying = jnp.exp(-math.log(2.0) / half_life * distance)
+        limit = lax.shift_left(jnp.ones_like(order_at), jnp.minimum(order_at + 1, 16)) - 1
+        central = jnp.where(limit > whole, 1.0, 0.0)
+        stddev = length / (2.0 * basis)
+        centres = length / basis + (length - length / basis) * ratio
+        shape_par = (centres / stddev) * (centres / stddev)
+        rate_par = centres / (stddev * stddev)
+        safe = jnp.maximum(distance, 1.0)
+        score = (shape_par - 1.0) * jnp.log(safe) - rate_par * safe
+        peak = jnp.max(jnp.where(whole < length, score, -jnp.inf), 0, keepdims=True)
+        gamma = jnp.where(whole > 0, jnp.exp(score - peak), 0.0)
+        kind = column // basis % 3
+        value = jnp.where(kind == 0, decaying, jnp.where(kind == 1, central, gamma))
+        value = jnp.where(whole < length, value, 0.0)
+        flipped = column >= 3 * basis
+        for side in range(2):
+            signed = offset if side == 0 else -offset
+            sign = jnp.where(signed > 0, 1.0, jnp.where(signed < 0, -1.0, 0.0))
+            tables[side] = jnp.where(flipped, value * sign, value).astype(tables.dtype)
+
+    halves = [shifted_ref, act_ref]
+
+    def up_step(half, i):
+        at = pl.ds(pl.multiple_of(i * tile, 128), tile)
+        value = jnp.dot(
+            norm_ref[...], weight_hold[half, :, at], preferred_element_type=jnp.float32
+        )
+        value = value + params[13 + half : 14 + half, at]
+        loss_ref[:, at] = value
+        halves[half][:, at] = jax.nn.gelu(value).astype(act_ref.dtype)
+
+    def down_step(half, i):
+        at = pl.ds(pl.multiple_of(i * tile, 128), tile)
+        value = total_ref[:, at]
+        for shard in range(groups):
+            source = (2 * shard + half) * rows
+            left = halves[source // columns][:, source % columns : source % columns + rows]
+            value = value + jnp.dot(
+                left,
+                weight_hold[half, shard * rows : (shard + 1) * rows, at],
+                preferred_element_type=jnp.float32,
+            )
+        if half == 0:
+            total_ref[:, at] = value + params[8:9, at]
+        else:
+            attended_ref[:, at] = value.astype(attended_ref.dtype)
+            limit = limits[:, 0:1]
+            norm_ref[:, at] = jnp.clip(value - target[0:1, at], -limit, limit).astype(
+                norm_ref.dtype
+            )
+
+    def over_tiles(fn):
+        def tile_body(i, carry):
+            fn(i)
+            return carry
+
+        lax.fori_loop(0, columns // tile, tile_body, 0)
+
+    def over_pairs(first):
+        def pair_body(i, carry):
+            pair_step(i)
+            return carry
+
+        lax.fori_loop(first, first + 2, pair_body, 0)
+
 
     def compute_list(n):
         if n == 2:
-            return [wait_smalls, unpack, activate, lambda: write_result(0).start()]
+            return [wait_smalls, unpack, activate, make_tables, lambda: write_result(0).start()]
         piece = n - 4
         if 0 <= piece < 5:
             work = [functools.partial(wait_weight, piece)]
             if piece != 2:
                 work.append(functools.partial(shift_tap, piece))
-            work += [functools.partial(conv_tap, piece, i) for i in tiles]
+            work += [functools.partial(over_tiles, functools.partial(conv_tap, piece))]
             return work
         if piece == 5:
             return [
@@ -514,44 +662,67 @@
             ]
         if piece == 6:
             work = [functools.partial(wait_weight, piece)]
-            work += [functools.partial(value_step, i) for i in tiles]
-            work += [lambda: write_result(6).start(), functools.partial(pair_step, 0)]
-            return work + [functools.partial(pair_step, 1)]
+            work += [functools.partial(over_tiles, value_step)]
+            return work + [lambda: write_result(6).start(), functools.partial(over_pairs, 0)]
         if piece == 7:
-            work = [functools.partial(pair_step, 2), functools.partial(pair_step, 3)]
+            work = [functools.partial(over_pairs, 2)]
             work += [lambda: [write_result(i).start() for i in (8, 9)]]
             work += [functools.partial(wait_weight, piece), lambda: write_result(1).wait()]
-            work += [functools.partial(out_step, i) for i in tiles]
+            work += [functools.partial(over_tiles, out_step)]
             work += [lambda: write_result(10).start(), lambda: write_result(2).wait()]
             return work + [
                 functools.partial(norm_step, 2, 7),
                 lambda: write_result(11).start(),
+                lambda: write_result(0).wait(),
             ]
+        if piece in (8, 9):
+            half = piece - 8
+            work = [functools.partial(wait_weight, piece)]
+            if half == 1:
+                work.append(lambda: write_pre(0).wait())
+            work += [functools.partial(over_tiles, functools.partial(up_step, half))]
+            work.append(lambda: [write_pre(half).start(), write_result(12 + half).start()])
+            return work
+        if piece in (10, 11):
+            half = piece - 10
+            work = [functools.partial(wait_weight, piece)]
+            if half == 0:
+                work.append(lambda: write_result(10).wait())
+            else:
+                work.append(lambda: [write_result(i).wait() for i in (9, 11)])
+            work += [functools.partial(over_tiles, functools.partial(down_step, half))]
+            if half == 1:
+                work.append(lambda: [write_result(i).start() for i in (14, 15)])
+            return work
         return []
 
     def send_list(n):
         work = []
-        if n + AHEAD < count:
+        if n + AHEAD < last:
             work.append(functools.partial(z_send, n + AHEAD))
+        if n in (0, 2, 4, 6):
+            work.append(functools.partial(part_send, n // 2))
         for shard in order:
-            if n < count:
+            if n < last:
                 work.append(functools.partial(stage_a, n, [shard]))
-            if 1 <= n <= count:
+            if 1 <= n <= last:
                 work.append(functools.partial(stage_b, n - 1, [shard]))
-            if 2 <= n < count + 2:
+            if 2 <= n < last + 2:
                 work.append(functools.partial(stage_c, n - 2, [shard]))
+            if n in (2, 4, 6, 8):
+                work.append(functools.partial(part_stage, n // 2 - 1, shard))
         return work
 
-    for step in summing[1:4]:
+    local_sums()
+    for step in summing[:4]:
         step()
 
-    for n in range(count + 3):
+    for n in range(count + 4):
         sends = send_list(n)
         work = compute_list(n)
         if 0 <= n - 3 < count:
             complete(n - 3)
-            if n - 3 < 8:
-                start_weight(n - 3)
+            start_weight(n - 3)
         slots = max(len(work), 1)
         for i in range(slots):
             for send in sends[len(sends) * i // slots : len(sends) * (i + 1) // slots]:
@@ -561,11 +732,24 @@
         if n < 2:
             summing[4 + n]()
 
-    for index in range(len(results)):
-        if index not in (1, 2):
-            write_result(index).wait()
-
-    for piece in range(count):
+    for index in (3, 4, 5, 6, 7, 8, 12, 13, 14, 15):
+        write_result(index).wait()
+    write_pre(1).wait()
+
+    for step in range(4):
+        for shard in range(groups):
+
+            @pl.when(jnp.logical_and(shard <= me, me + 1 < groups))
+            def _():
+                part_copy(step, shard, (me + 1) % groups, part_right).wait_send()
+
+            @pl.when(jnp.logical_and(shard >= me, me > 0))
+            def _():
+                part_copy(step, shard, (me + groups - 1) % groups, part_left).wait_send()
+
+    sent = pieces[last].at[pl.ds(0, others), pl.ds(0, 4 * part)]
+    remote(sent, sent, send_sem.at[last], sib_sem.at[last], (sib, me)).wait_send()
+    for piece in range(last):
         for shard in range(groups):
 
             @pl.when(jnp.logical_and(shard <= me, me + 1 < groups))
@@ -580,13 +764,14 @@
         remote(sent, sent, send_sem.at[piece], sib_sem.at[piece], (sib, me)).wait_send()
 
 
-def gather(groups, blocks, weights, small, stats, inputs, tables):
+def gather(groups, blocks, weights, small, inputs, target, limits):
     conv, query = weights[:2]
     rel = weights[7]
     taps, rows, columns = conv.shape
     width = query.shape[1]
     length = inputs.shape[0]
-    span = tables.shape[1]
+    span = 2 * length
+    stats_shape = (2 * columns // 128, 128)
     dtype = conv.dtype
     kept = pl.BlockSpec(memory_space=pl.ANY)
     inside = pl.BlockSpec(memory_space=pltpu.VMEM)
@@ -608,6 +793,10 @@
         jax.ShapeDtypeStruct(wide, dtype),
         jax.ShapeDtypeStruct(wide, jnp.float32),
         jax.ShapeDtypeStruct(wide, dtype),
+        jax.ShapeDtypeStruct((length, 2 * columns), jnp.float32),
+        jax.ShapeDtypeStruct((length, 2 * columns), dtype),
+        jax.ShapeDtypeStruct(wide, dtype),
+        jax.ShapeDtypeStruct(wide, dtype),
     ]
     return pl.pallas_call(
         functools.partial(gather_kernel, groups, blocks),
@@ -620,11 +809,12 @@
             jax.ShapeDtypeStruct((groups, 2 * rows, columns), dtype),
             jax.ShapeDtypeStruct((groups,) + rel.shape, dtype),
             jax.ShapeDtypeStruct((groups,) + small.shape, jnp.float32),
-            jax.ShapeDtypeStruct(stats.shape, jnp.float32),
+            jax.ShapeDtypeStruct(stats_shape, jnp.float32),
             *made,
+            jax.ShapeDtypeStruct((2, span, rel.shape[0]), dtype),
         ),
         in_specs=[kept] * 7 + [inside] * 5,
-        out_specs=[kept] * 6 + [inside] * 3 + [kept] * len(made),
+        out_specs=[kept] * 6 + [inside] * 3 + [kept] * len(made) + [inside],
         scratch_shapes=[
             pltpu.VMEM((count - 1, rows, columns), dtype),
             pltpu.VMEM((rows, 2 * width), dtype),
@@ -635,10 +825,10 @@
             pltpu.SemaphoreType.DMA((count,)),
             *grid_sems[:2],
             *([pltpu.SemaphoreType.DMA((groups,))] * 4),
-            *sum_scratch(groups, blocks, stats.shape),
+            *sum_scratch(groups, blocks, stats_shape),
             pltpu.VMEM((2, columns, columns), dtype),
             pltpu.SemaphoreType.DMA((2, groups)),
-            pltpu.SemaphoreType.DMA((len(made),)),
+            pltpu.SemaphoreType.DMA((len(made) + 2,)),
             pltpu.VMEM((16, columns), jnp.float32),
             pltpu.VMEM(wide, dtype),
             pltpu.VMEM(wide, jnp.float32),
@@ -651,12 +841,15 @@
             pltpu.VMEM((2, span, width), dtype),
             pltpu.VMEM((HEADS, length, length), dtype),
             pltpu.VMEM(wide, dtype),
+            pltpu.VMEM(stats_shape, jnp.float32),
+            pltpu.VMEM(wide, jnp.float32),
+            *([pltpu.SemaphoreType.DMA((4, groups))] * 3),
         ],
         compiler_params=pltpu.CompilerParams(
             collective_id=0, has_side_effects=True, vmem_limit_bytes=60 << 20
         ),
         name="gather",
-    )(*weights, small, stats, inputs, tables)
+    )(*weights, small, inputs, target, limits)
 
 
 def gelu_slope(value):
@@ -716,6 +909,7 @@
         probs_ref,
     ) = refs[85:99]
     tile_sem, host_sem, probs_sem, kept_sem = refs[99:103]
+    slab, slab_got, x_slab, y_slab, x_part, y_part, slab_credit = refs[103:110]
 
     dp = lax.axis_index("dp")
     me = lax.axis_index("fsdp")
@@ -738,10 +932,12 @@
     up_right = rights[1]
     rights[1:2] = [up_right.at[:, pl.ds(side * 2 * width, 2 * width)] for side in range(2)]
     lefts_got = [hidden_got] + [left_got.at[index] for index in range(4)]
-    left_of = [0, 0, 1, 1, 2, 3, 3] + [4] * taps
-    right_of = [0, 0, 1, 2, 3, 4, 5] + [6] * taps
-    mixed_piece = 6
-    first_tap = 7
+    left_of = [0, 1, 1, 2, 3, 3, 4, 4, 4, 4, 0, 4]
+    right_of = [0, 1, 2, 3, 4, 5, 6, 6, 6, 6, 0, 6]
+    tap_of = {6: 0, 7: 1, 8: 2, 9: 3, 11: 4}
+    mixed_piece = 5
+    normal = 10
+    extra_at = {0: 10, 6: 11}
     own_columns = pl.ds(pl.multiple_of(core * width, 128), width)
     sib_columns = pl.ds(pl.multiple_of((1 - core) * width, 128), width)
 
@@ -762,25 +958,24 @@
     def rel_copy():
         return remote(rel_grad, rel_got, rel_send.at[0], rel_recv.at[0], (sib, me))
 
-    def loads(piece, slot):
+    def loads(piece):
         left = left_of[piece]
         right = right_of[piece]
         pairs = [
-            (rights[right].at[:, own_columns], right_hold.at[slot, 0]),
-            (right_got.at[right], right_hold.at[slot, 1]),
+            (rights[right].at[:, own_columns], right_hold.at[0]),
+            (right_got.at[right], right_hold.at[1]),
         ]
         if left > 0:
-            pairs.append((lefts[left], left_hold.at[slot, 0]))
-            pairs.append((lefts_got[left], left_hold.at[slot, 1]))
+            pairs.append((lefts[left], left_hold.at[0]))
+            pairs.append((lefts_got[left], left_hold.at[1]))
         else:
             for shard in range(groups):
-                source = pl.ds((2 * shard + piece % 2) * rows, rows)
+                source = pl.ds((2 * shard + piece // normal) * rows, rows)
                 target = pl.ds(shard * rows, rows)
-                pairs.append((lefts[left].at[:, source], left_hold.at[slot, 0, :, target]))
-                pairs.append((lefts_got[left].at[:, source], left_hold.at[slot, 1, :, target]))
+                pairs.append((lefts[left].at[:, source], left_hold.at[0, :, target]))
+                pairs.append((lefts_got[left].at[:, source], left_hold.at[1, :, target]))
         return [
-            pltpu.make_async_copy(src, dst, load_sem.at[slot, i])
-            for i, (src, dst) in enumerate(pairs)
+            pltpu.make_async_copy(src, dst, load_sem.at[i]) for i, (src, dst) in enumerate(pairs)
         ]
 
     def start_loads(piece):
@@ -788,8 +983,14 @@
             left_copy(left_of[piece]).wait_recv()
         if right_of[piece] not in right_of[:piece]:
             right_copy(right_of[piece]).wait_recv()
-        for copy in loads(piece, piece % 2):
+        for copy in loads(piece):
             copy.start()
+
+    def wait_loads(piece):
+        for copy in loads(piece):
+            copy.wait()
+        if tap_of.get(piece, 2) != 2:
+            shift(tap_of[piece] - taps // 2)
 
     meet(near + shards + far)
 
@@ -804,7 +1005,7 @@
     ring = x_one.shape[0]
 
     def pay(piece, index, device):
-        @pl.when(piece < count - ring)
+        @pl.when(piece < normal - ring)
         def _():
             pl.semaphore_signal(
                 credit.at[index], inc=1, device_id=(device, me), device_id_type=MESH
@@ -907,25 +1108,26 @@
 
     diagonal = neighbours(along_x)[2]
 
-    def shift(piece):
-        move = piece - first_tap - taps // 2
+    def shift(move):
         for window in range(2):
-            value = right_hold[piece % 2, window].astype(jnp.float32)
+            value = right_hold[window].astype(jnp.float32)
             value = pltpu.roll(value, move % value.shape[0], 0)
             row = lax.broadcasted_iota(jnp.int32, value.shape, 0)
             inside = row >= move if move > 0 else row < value.shape[0] + move
             value = jnp.where(inside, value, 0.0)
-            right_hold[piece % 2, window] = value.astype(right_hold.dtype)
+            right_hold[window] = value.astype(right_hold.dtype)
+
+    def product(shard):
+        at = pl.ds(pl.multiple_of(shard * rows, 128), rows)
+        value = dot_leading(left_hold[0, :, at], right_hold[0])
+        value = value + dot_leading(left_hold[1, :, at], right_hold[1])
+        return value.astype(grad.dtype).reshape(2, 2, part, width)
 
     def produce(piece):
         slot = piece % slots
-        hold = piece % 2
 
         def shard_body(shard, carry):
-            columns = pl.ds(pl.multiple_of(shard * rows, 128), rows)
-            value = dot_leading(left_hold[hold, 0, :, columns], right_hold[hold, 0])
-            value = value + dot_leading(left_hold[hold, 1, :, columns], right_hold[hold, 1])
-            grad[slot, shard] = value.astype(grad.dtype).reshape(2, 2, part, width)
+            grad[slot, shard] = product(shard)
             return carry
 
         lax.fori_loop(0, groups, shard_body, 0)
@@ -941,6 +1143,147 @@
                 grad[slot, shard, 0, :, :, pl.ds(rel_at, rel_grad.shape[3])] = value.astype(
                     grad.dtype
                 )
+
+    def slab_copy(piece, j, arriving=False):
+        other = (me + 1 + j) % groups
+        at = j if arriving else groups - 2 - j
+        return remote(
+            slab.at[other],
+            slab_got.at[at],
+            shard_send.at[piece, j],
+            shard_recv.at[piece, at],
+            (dp, other),
+        )
+
+    def slab_one(piece, e):
+        return (
+            remote(
+                slab.at[me, :, 1 - at_x, :, first],
+                x_slab.at[e],
+                x1s.at[piece],
+                x1r.at[piece],
+                (along_x, me),
+            ),
+            remote(
+                slab.at[me, 1 - at_y, :, :, last],
+                y_slab.at[e],
+                y1s.at[piece],
+                y1r.at[piece],
+                (along_y, me),
+            ),
+        )
+
+    def slab_two(piece, e):
+        return (
+            remote(
+                slab.at[me, 1 - at_y, at_x, :, first],
+                y_part.at[e],
+                y2s.at[piece],
+                y2r.at[piece],
+                (along_y, me),
+            ),
+            remote(
+                slab.at[me, at_y, 1 - at_x, :, last],
+                x_part.at[e],
+                x2s.at[piece],
+                x2r.at[piece],
+                (along_x, me),
+            ),
+        )
+
+    def slab_sent(piece, e):
+        for j in range(others):
+            slab_copy(piece, j).wait_send()
+        for copy in slab_one(piece, e) + slab_two(piece, e):
+            copy.wait_send()
+
+    def extra_start(piece, e):
+        for copy in loads(piece):
+            copy.start()
+        if e > 0:
+            slab_sent(piece - 1, e - 1)
+        wait_loads(piece)
+
+        def shard_body(shard, carry):
+            slab[shard] = product(shard)
+            return carry
+
+        lax.fori_loop(0, groups, shard_body, 0)
+        for j in range(others):
+            if e > 0:
+                pl.semaphore_wait(slab_credit.at[(me + 1 + j) % groups], 1)
+            slab_copy(piece, j).start()
+
+    def extra_sum(piece, e):
+        for j in range(others):
+            slab_copy(piece, j, True).wait_recv()
+        for y in range(2):
+            for x in range(2):
+                value = slab[me, y, x].astype(jnp.float32)
+                for j in range(others):
+                    value = value + slab_got[j, y, x].astype(jnp.float32)
+                slab[me, y, x] = value.astype(slab.dtype)
+        if e == 0:
+            for j in range(others):
+                pl.semaphore_signal(
+                    slab_credit.at[me], inc=1, device_id=shards[j], device_id_type=MESH
+                )
+        for copy in slab_one(piece, e):
+            copy.start()
+
+    def extra_fold(piece, e):
+        for copy in slab_one(piece, e):
+            copy.wait_recv()
+        for other in range(2):
+            value = slab[me, other, at_x, :, first].astype(jnp.float32)
+            value = value + x_slab[e, other].astype(jnp.float32)
+            slab[me, other, at_x, :, first] = value.astype(slab.dtype)
+            value = slab[me, at_y, other, :, last].astype(jnp.float32)
+            value = value + y_slab[e, other].astype(jnp.float32)
+            slab[me, at_y, other, :, last] = value.astype(slab.dtype)
+        for copy in slab_two(piece, e):
+            copy.start()
+
+    def extra_done(piece, e):
+        for copy in slab_two(piece, e):
+            copy.wait_recv()
+        low = slab[me, at_y, at_x, :, first].astype(jnp.float32)
+        high = slab[me, at_y, at_x, :, last].astype(jnp.float32)
+        low = low + y_part[e].astype(jnp.float32)
+        high = high + x_part[e].astype(jnp.float32)
+        finish(piece, jnp.concatenate([low, high], 1))
+
+    def finish(piece, value):
+        if blocks > 1:
+            done[piece] = value.astype(done.dtype)
+            block_got[piece, block] = value.astype(done.dtype)
+            for j in range(blocks - 1):
+                block_copy(piece, j).start()
+            for j in range(blocks - 1):
+                block_copy(piece, j).wait_send()
+                block_arrival(piece, j).wait_recv()
+            value = block_got[piece, 0].astype(jnp.float32)
+            for other in range(1, blocks):
+                value = value + block_got[piece, other].astype(jnp.float32)
+        done[piece] = value.astype(done.dtype)
+        pltpu.make_async_copy(done.at[piece], place(piece, dp), write_sem.at[piece]).start()
+        spread(piece, done.at[piece], dp, ax.at[piece], along_x).start()
+        spread(piece, done.at[piece], dp, ay.at[piece], along_y).start()
+        spread(piece, done.at[piece], dp, sib_sem.at[piece], sib).start()
+
+    def cross(piece):
+        route = piece % 2
+        forward(piece, along_x, ax.at[piece], dp).wait_recv()
+        forward(piece, along_y, ay.at[piece], dp).wait_recv()
+        owner = route * along_x + (1 - route) * along_y
+        target = route * along_y + (1 - route) * along_x
+        forward(piece, owner, ad.at[piece], target).start()
+        forward(piece, along_x, sib_sem.at[piece], sib).start()
+        forward(piece, along_y, sib_sem.at[piece], sib).start()
+
+    def close(piece):
+        forward(piece, diagonal, ad.at[piece], dp).wait_recv()
+        forward(piece, diagonal, sib_sem.at[piece], sib).start()
 
     def add(piece_slot, ref, columns, *index):
         ahead = grad[(piece_slot,) + index + (slice(None), columns)]
@@ -1303,7 +1646,7 @@
         pl.when(n == 4 + taps)(step_last)
 
     def body(n, carry):
-        @pl.when(n < count)
+        @pl.when(n < normal)
         def _():
             @pl.when(n >= slots)
             def _():
@@ -1313,16 +1656,11 @@
                 for j in range(others):
                     shard_copy(old, j).wait_send()
 
-            for piece in range(count):
+            for piece in range(normal):
 
                 @pl.when(n == piece)
                 def _():
-                    for copy in loads(piece, piece % 2):
-                        copy.wait()
-                    if piece + 1 < count:
-                        start_loads(piece + 1)
-                    if piece >= first_tap and piece != first_tap + taps // 2:
-                        shift(piece)
+                    wait_loads(piece)
 
             produce(n)
             claim(n, 0)
@@ -1330,9 +1668,20 @@
             for copy in one(n):
                 copy.start()
 
+        for e, (at, piece) in enumerate(extra_at.items()):
+
+            @pl.when(n == at)
+            def _():
+                extra_start(piece, e)
+
         host(n)
-
-        @pl.when(jnp.logical_and(n >= 1, n < count + 1))
+        for piece in range(1, normal):
+
+            @pl.when(n == piece - 1)
+            def _():
+                start_loads(piece)
+
+        @pl.when(jnp.logical_and(n >= 1, n < normal + 1))
         def _():
             piece = n - 1
             slot = piece % slots
@@ -1355,7 +1704,7 @@
             for copy in two(piece):
                 copy.start()
 
-        @pl.when(jnp.logical_and(n >= 2, n < count + 2))
+        @pl.when(jnp.logical_and(n >= 2, n < normal + 2))
         def _():
             piece = n - 2
             slot = piece % slots
@@ -1380,7 +1729,7 @@
 
                 shard_copy(piece, j).start()
 
-        @pl.when(jnp.logical_and(n >= 3, n < count + 3))
+        @pl.when(jnp.logical_and(n >= 3, n < normal + 3))
         def _():
             piece = n - 3
             value = grad[piece % slots, me, at_y, at_x].astype(jnp.float32)
@@ -1388,61 +1737,47 @@
                 shard_arrival(piece, j).wait_recv()
                 value = value + shard_got[piece % ring, (me + 1 + j) % groups].astype(jnp.float32)
 
-            @pl.when(piece < count - ring)
+            @pl.when(piece < normal - ring)
             def _():
                 for j in range(others):
                     pl.semaphore_signal(
                         shard_credit.at[me], inc=1, device_id=shards[j], device_id_type=MESH
                     )
 
-            if blocks > 1:
-                done[piece] = value.astype(done.dtype)
-                block_got[piece, block] = value.astype(done.dtype)
-                for j in range(blocks - 1):
-                    block_copy(piece, j).start()
-                for j in range(blocks - 1):
-                    block_copy(piece, j).wait_send()
-                    block_arrival(piece, j).wait_recv()
-                value = block_got[piece, 0].astype(jnp.float32)
-                for other in range(1, blocks):
-                    value = value + block_got[piece, other].astype(jnp.float32)
-            done[piece] = value.astype(done.dtype)
-            pltpu.make_async_copy(done.at[piece], place(piece, dp), write_sem.at[piece]).start()
-            spread(piece, done.at[piece], dp, ax.at[piece], along_x).start()
-            spread(piece, done.at[piece], dp, ay.at[piece], along_y).start()
-            spread(piece, done.at[piece], dp, sib_sem.at[piece], sib).start()
-
-        @pl.when(jnp.logical_and(n >= 4, n < count + 4))
+            finish(piece, value)
+
+        @pl.when(jnp.logical_and(n >= 4, n < normal + 4))
         def _():
-            piece = n - 4
-            route = piece % 2
-            forward(piece, along_x, ax.at[piece], dp).wait_recv()
-            forward(piece, along_y, ay.at[piece], dp).wait_recv()
-            owner = route * along_x + (1 - route) * along_y
-            target = route * along_y + (1 - route) * along_x
-            forward(piece, owner, ad.at[piece], target).start()
-            forward(piece, along_x, sib_sem.at[piece], sib).start()
-            forward(piece, along_y, sib_sem.at[piece], sib).start()
+            cross(n - 4)
 
         @pl.when(n >= 5)
         def _():
-            piece = n - 5
-            forward(piece, diagonal, ad.at[piece], dp).wait_recv()
-            forward(piece, diagonal, sib_sem.at[piece], sib).start()
+            close(n - 5)
+
+        for e, (at, piece) in enumerate(extra_at.items()):
+            for later, action in (
+                (3, functools.partial(extra_sum, piece, e)),
+                (4, functools.partial(extra_fold, piece, e)),
+                (5, functools.partial(extra_done, piece, e)),
+                (6, functools.partial(cross, piece)),
+                (7, functools.partial(close, piece)),
+            ):
+                pl.when(n == at + later)(action)
 
         for step in range(len(summing)):
 
-            @pl.when(n == count + step - 1)
+            @pl.when(n == normal + step - 1)
             def _():
                 summing[step]()
 
         return carry
 
-    lax.fori_loop(0, count + 5, body, 0)
+    lax.fori_loop(0, normal + 5, body, 0)
+    slab_sent(11, 1)
     write_part().wait()
 
     def drain(piece, carry):
-        @pl.when(piece >= count - slots)
+        @pl.when(jnp.logical_and(piece >= normal - slots, piece < normal))
         def _():
             for copy in one(piece) + two(piece):
                 copy.wait_send()
@@ -1502,8 +1837,8 @@
         in_specs=[kept] * len(inputs) + [inside] * 2,
         out_specs=[kept, inside] + [kept] * 9,
         scratch_shapes=[
-            pltpu.VMEM((2, 2) + wide, dtype),
-            pltpu.VMEM((2, 2, length, width), dtype),
+            pltpu.VMEM((2,) + wide, dtype),
+            pltpu.VMEM((2, length, width), dtype),
             pltpu.VMEM((slots, groups, 2, 2, part, width), dtype),
             pltpu.VMEM(two_got, dtype),
             pltpu.VMEM(two_got, dtype),
@@ -1518,7 +1853,7 @@
             *([pltpu.SemaphoreType.DMA((5,))] * 2),
             *([pltpu.SemaphoreType.DMA((7,))] * 2),
             *([pltpu.SemaphoreType.DMA((1,))] * 2),
-            pltpu.SemaphoreType.DMA((2, 2 + 2 * groups)),
+            pltpu.SemaphoreType.DMA((2 + 2 * groups,)),
             *([each] * 8),
             *([pltpu.SemaphoreType.DMA((count, groups))] * 2),
             *([pltpu.SemaphoreType.DMA((count, blocks))] * 2),
@@ -1542,6 +1877,13 @@
             pltpu.SemaphoreType.DMA((14,)),
             pltpu.SemaphoreType.DMA((2,)),
             pltpu.SemaphoreType.DMA((hidden.shape[1] // 512 + 1,)),
+            pltpu.VMEM((groups, 2, 2, part, width), dtype),
+            pltpu.VMEM((groups - 1, 2, 2, part, width), dtype),
+            pltpu.VMEM((2, 2, part, width // 2), dtype),
+            pltpu.VMEM((2, 2, part, width // 2), dtype),
+            pltpu.VMEM((2, part, width // 2), dtype),
+            pltpu.VMEM((2, part, width // 2), dtype),
+            pltpu.SemaphoreType.REGULAR((groups,)),
         ],
         compiler_params=pltpu.CompilerParams(
             collective_id=1, has_side_effects=True, vmem_limit_bytes=VMEM_LIMIT
@@ -1551,29 +1893,6 @@
 
 
 EPSILON = 1e-05
-
-
-def position_table(length, features, direction):
-    basis_count = features // 6
-    offsets = jnp.arange(2 * length - 1, dtype=jnp.float32) - (length - 1)
-    offsets = offsets * direction
-    distance = jnp.abs(offsets)[:, None]
-    max_range = math.log(length) / math.log(2.0)
-    half_life = 2.0 ** jnp.linspace(3.0, max_range, basis_count, dtype=jnp.float32)
-    decaying = jnp.exp(-math.log(2.0) / half_life[None, :] * distance)
-    widths = 2.0 ** jnp.arange(1, basis_count + 1, dtype=jnp.float32) - 1.0
-    central = (widths[None, :] > distance).astype(jnp.float32)
-    stddev = length / (2.0 * basis_count)
-    centres = jnp.linspace(length / basis_count, length, basis_count, dtype=jnp.float32)
-    shape_par = (centres / stddev) ** 2
-    rate_par = centres / stddev**2
-    safe_dist = jnp.maximum(distance, 1.0)
-    log_prob = (shape_par - 1.0) * jnp.log(safe_dist) - rate_par * safe_dist
-    log_prob = log_prob - jnp.max(log_prob, axis=0, keepdims=True)
-    gamma_feat = jnp.where(distance > 0.5, jnp.exp(log_prob), 0.0)
-    symmetric = jnp.concatenate([decaying, central, gamma_feat], 1)
-    sign_row = jnp.sign(offsets)[:, None]
-    return jnp.concatenate([symmetric, sign_row * symmetric], 1)
 
 
 def normalize(values):
@@ -1635,13 +1954,11 @@
     small_parts = [gains, biases, up_bias, rel_bias]
     small = jnp.concatenate([part.reshape(-1) for part in small_parts])
     small = jnp.pad(small, (0, -small.shape[0] % 1024)).reshape(-1, 128)
-    stats = jnp.concatenate([jnp.sum(inputs, 0), jnp.sum(inputs * inputs, 0)]).reshape(-1, 128)
-    tables = jnp.stack(
-        [
-            jnp.pad(position_table(length, rel_rows, direction), ((0, 1), (0, 0)))
-            for direction in (1.0, -1.0)
-        ]
-    ).astype(jnp.bfloat16)
+    target_row = lax.dynamic_index_in_dim(target_table, window_ids[0], 0, keepdims=True)
+    levels = jnp.arange(clip_levels.shape[0], dtype=jnp.int32)
+    selector = (clip_index[0][:, None] == levels[None, :]).astype(jnp.float32)
+    limits = jnp.sum(selector * clip_levels[None, :], 1)[:, None]
+    limits = jnp.broadcast_to(limits, (length, 128))
     (
         conv_full,
         mixed_full,
@@ -1664,6 +1981,11 @@
         attended,
         after_attention,
         normed_two,
+        hidden_pre,
+        hidden,
+        outputs,
+        cotangent,
+        tables,
     ) = gather(
         groups,
         blocks,
@@ -1678,9 +2000,9 @@
             rel_weight,
         ],
         small,
-        stats,
         tokens[0],
-        tables,
+        target_row,
+        limits,
     )
     conv_full = conv_full.reshape(tap_count, model_width, model_width)
     mixed_full = mixed_full.reshape(model_width, -1)
@@ -1697,24 +2019,11 @@
         taken += part.size
     gain_rows = jnp.moveaxis(unpacked[0], 0, 1).reshape(gains.shape[0], -1)
     bias_rows = jnp.moveaxis(unpacked[1], 0, 1).reshape(biases.shape[0], -1)
-    up_offset = unpacked[2].reshape(-1)
     batch_sums = stats.reshape(2, -1)
     centre = batch_sums[0] / token_total
     variance = batch_sums[1] / token_total - centre * centre
     inverse = lax.rsqrt(variance + EPSILON)
     standard = (inputs - centre) * inverse
-    hidden_pre = jnp.dot(normed_two, up_full, preferred_element_type=jnp.float32) + up_offset
-    hidden = jax.nn.gelu(hidden_pre).astype(jnp.bfloat16)
-    outputs = (
-        after_attention
-        + jnp.dot(hidden, down_full, preferred_element_type=jnp.float32)
-        + bias_rows[5]
-    )
-    target_row = lax.dynamic_index_in_dim(target_table, window_ids[0], 0, keepdims=False)
-    levels = jnp.arange(clip_levels.shape[0], dtype=jnp.int32)
-    selector = (clip_index[0][:, None] == levels[None, :]).astype(jnp.float32)
-    limits = jnp.sum(selector * clip_levels[None, :], 1)[:, None]
-    cotangent = jnp.clip(outputs - target_row, -limits, limits).astype(jnp.bfloat16)
     params = jnp.concatenate([gain_rows, bias_rows[:1], centre[None], inverse[None]], 0)
     params = jnp.pad(params, ((0, 2), (0, 0)))
     pieces, sums, part_grad, *_ = reduce(
@@ -1738,20 +2047,20 @@
     up_sums = lax.dynamic_index_in_dim(up_sums, shard, 0, keepdims=False)
     rel_sums = sums[11, : 2 * key_width].reshape(2, groups, -1)
     rel_sums = lax.dynamic_index_in_dim(rel_sums, shard, 1, keepdims=False)
-    up_grad = jnp.concatenate([pieces[2], pieces[3]], 1)
-    mixed_sum = pieces[6].astype(jnp.float32)
+    up_grad = jnp.concatenate([pieces[1], pieces[2]], 1)
+    mixed_sum = pieces[5].astype(jnp.float32)
     rel_at = 2 * key_width
     return (
-        outputs.astype(jnp.bfloat16)[None],
+        outputs[None],
         input_grad.astype(jnp.bfloat16)[None],
-        pieces[7:12].astype(jnp.float32),
+        jnp.concatenate([pieces[6:10], pieces[11:12]], 0).astype(jnp.float32),
         mixed_sum[:, :key_width],
         mixed_sum[:, key_width:rel_at],
-        pieces[5].astype(jnp.float32),
         pieces[4].astype(jnp.float32),
+        pieces[3].astype(jnp.float32),
         mixed_sum[:rel_rows, rel_at : rel_at + rel_columns],
         up_grad.astype(jnp.float32),
-        pieces[:2].reshape(2 * piece_rows, -1).astype(jnp.float32),
+        jnp.concatenate([pieces[0], pieces[10]], 0).astype(jnp.float32),
         by_shard[:3],
         by_shard[3:9],
         up_sums,

time: 605 us -> 588 us (0.972)
  matrix products: 17.7 us -> 0 us
  Pallas kernels: 526 us -> 540 us
  other arithmetic: 38.2 us -> 24.9 us
    dot_general x2 -> x0, matrix products: 17.7 us -> none  [the longest x1 11 us: on_device(): jnp.dot(normed_two, up_full, preferred_element_type=jnp.float32) + up_offset]
    pallas_call x1, Pallas kernels: 201 us -> 216 us  [gather(): pl.pallas_call(functools.partial(gather_kernel, groups, blocks), out_shap...]
where the time goes in v6:
time: 588 us; the launch traced here: 583 us
  Pallas kernels  540 us (92%)
  other arithmetic  24.9 us (4%)
  local copies, waits for them, and re-layouts  16.3 us (3%)
    pallas_call x1, Pallas kernels, reduce(): pl.pallas_call(functools.partial(reduce_kernel, groups, blocks, rel_at),...  324 us
    pallas_call x1, Pallas kernels, gather(): pl.pallas_call(functools.partial(gather_kernel, groups, blocks), out_shap...  216 us

profile of v6, /device:TPU:0, one launch (start us, length us, event | category | flops | bytes accessed | tf_op | source)
XLA Modules:
  0.0 583.3 jit_solution(5736553061841087403)
XLA Ops:
  0.6 0.0 copy-start
  1.4 0.8 select_reduce_fusion
  2.2 0.0 copy-done
  2.2 0.6 constant_dynamic-slice_fusion.3.refs_10_
  2.8 0.7 reshape.154
  3.5 0.7 reshape.155
  4.2 1.3 fusion.1.refs_8_
  5.5 0.8 broadcast_in_dim.6.refs_11_
  6.3 216.2 %gather.1 = (bf16[5,4,384,1536]{3,2,1,0:T(8,128)(2,1)}, bf16[4,384,1024]{2,1,0:T(8,128)(2,1)}, bf16[4,384,1536]{2,1,0:T(8,128)(2,1)}, bf16[4,384,1536]{2,1,0:T(8...) custom-call(bf16[5,384,1536]{2,1,0:T(8,128)(2,1)} %refs_0_.1, ...), custom_call_target="tpu_custom_call" | custom-call | tf_op jit(solution)/shard_map/gather/pallas_call | solution.py:801
  222.5 0.8 fusion.4
  223.3 0.9 copy.47
  224.3 0.8 fusion.9
  225.1 0.7 select_maximum_fusion.refs_22_
  225.7 1.9 slice_bitcast_fusion.4.refs_23_
  227.6 0.0 copy-start.2
  227.6 324.3 %reduce.7 = (bf16[12,384,1536]{2,1,0:T(8,128)(2,1)}, f32[16,1536]{1,0:T(8,128)}, f32[512,1536]{1,0:T(8,128)}, bf16[512,3072]{1,0:T(8,128)(2,1)}, bf16[512,1536]{...) custom-call(bf16[512,3072]{1,0:T(8,128)(2,1)} %get-tuple-element.43., ...), custom_call_target="tpu_custom_call" | custom-call | tf_op jit(solution)/shard_map/reduce/pallas_call | solution.py:1822
  551.9 0.8 slice.118
  552.7 0.6 constant_dynamic-slice_fusion.1
  553.3 0.8 slice.117
  554.1 0.6 dynamic-slice_reduce_fusion
  554.7 0.9 slice_reduce_fusion.1
  555.6 0.0 copy-done.2
  555.6 0.0 copy-start.4
  555.6 4.0 fusion
  559.6 0.0 copy-done.4
  559.6 0.6 copy.49
  560.2 0.6 copy.48
  560.8 2.6 slice.100
  563.5 5.7 slice_bitcast_fusion.1
  569.2 0.7 slice.125
  569.8 1.3 fusion.11
  571.1 2.8 maximum_convert_fusion.2
  573.9 2.8 maximum_convert_fusion.1
  576.7 0.0 copy-start.3
  576.7 0.0 copy-start.1
  576.7 5.3 maximum_convert_fusion
  582.0 0.0 copy-done.3
  582.0 1.1 copy.52
  583.1 0.0 copy-done.1
  (12 shorter events, 0.1 us)
Async XLA Ops:
  0.6 1.5 copy-start
  227.6 328.0 %copy-start.2 = (bf16[1,512,1536]{2,1,0:T(8,128)(2,1)S(1)}, bf16[1,512,1536]{2,1,0:T(8,128)(2,1)}, u32[]{:S(2)}) copy-start(bf16[1,512,1536]{2,1,0:T(8,128)(2,1)} %param.17) | copy-start | bytes 4718596
  555.6 4.0 copy-start.4
  576.7 5.3 copy-start.3
  576.7 6.4 %copy-start.1 = (f32[64,1536]{1,0:T(8,128)S(1)}, f32[64,1536]{1,0:T(8,128)}, u32[]{:S(2)}) copy-start(f32[64,1536]{1,0:T(8,128)} %param.30) | copy-start | bytes 1179652

commit v7 on v6

--- a/solution.py
+++ b/solution.py
@@ -153,18 +153,18 @@
     results[12:12] = [
         hidden_out.at[:, pl.ds(side * conv.shape[2], conv.shape[2])] for side in range(2)
     ]
-    tables = refs[37]
-    refs = refs[38:]
+    tables, params = refs[37:39]
+    refs = refs[39:]
     hold, hold_mixed, local_sem, write_sem = refs[:4]
     z_sem, x_sem, y_sem, d_sem, sib_sem, send_sem, right_send, left_send = refs[4:12]
     rel_send, rel_recv, small_send, small_recv = refs[12:16]
     near_got, sums, shard_got, block_got = refs[16:20]
     sum_sems = refs[20:26]
     weight_hold, weight_sem, result_sem = refs[26:29]
-    params, shifted_ref, total_ref = refs[29:32]
-    act_ref, norm_ref, content_ref, position_ref, key_ref, value_ref = refs[32:38]
-    table_ref, probs_ref, attended_ref = refs[38:41]
-    stats, loss_ref, part_sem, part_right, part_left = refs[41:46]
+    shifted_ref, total_ref = refs[29:31]
+    act_ref, norm_ref, content_ref, position_ref, key_ref, value_ref = refs[31:37]
+    table_ref, probs_ref, attended_ref = refs[37:40]
+    stats, loss_ref, part_sem, part_right, part_left = refs[40:45]
     dp = lax.axis_index("dp")
     me = lax.axis_index("fsdp")
     near, shards, far = peers_of(groups, blocks)
@@ -250,10 +250,12 @@
             (dp, (me + groups - 1) % groups),
         )
 
-    last = count - 1
+    alone = count - 2
+    waves = [piece for piece in range(count) if piece != alone]
+    wave_count = len(waves)
 
     def part_copy(step, shard, device, sems, src=None):
-        dst = slice_of(last, shard, 2 * step + dp % 2)
+        dst = slice_of(alone, shard, 2 * step + dp % 2)
         return remote(
             dst if src is None else src,
             dst,
@@ -264,7 +266,7 @@
 
     def part_send(step):
         at = pl.ds(pl.multiple_of((2 * step + dp % 2) * part, 16), part)
-        src = holds[last].at[at]
+        src = holds[alone].at[at]
 
         @pl.when(me + 1 < groups)
         def _():
@@ -285,8 +287,8 @@
         def _():
             part_copy(step, shard, (me + groups - 1) % groups, part_left).start()
 
-        ref = slice_of(last, shard, 2 * step + dp % 2)
-        remote(ref, ref, send_sem.at[last], sib_sem.at[last], (sib, me)).start()
+        ref = slice_of(alone, shard, 2 * step + dp % 2)
+        remote(ref, ref, send_sem.at[alone], sib_sem.at[alone], (sib, me)).start()
 
     def z_send(piece):
         src = holds[piece].at[pl.ds(pl.multiple_of(dp % 8 * part, 16), part)]
@@ -641,7 +643,7 @@
     def compute_list(n):
         if n == 2:
             return [wait_smalls, unpack, activate, make_tables, lambda: write_result(0).start()]
-        piece = n - 4
+        piece = n - 3
         if 0 <= piece < 5:
             work = [functools.partial(wait_weight, piece)]
             if piece != 2:
@@ -698,17 +700,17 @@
 
     def send_list(n):
         work = []
-        if n + AHEAD < last:
-            work.append(functools.partial(z_send, n + AHEAD))
+        if n + AHEAD < wave_count:
+            work.append(functools.partial(z_send, waves[n + AHEAD]))
         if n in (0, 2, 4, 6):
             work.append(functools.partial(part_send, n // 2))
         for shard in order:
-            if n < last:
-                work.append(functools.partial(stage_a, n, [shard]))
-            if 1 <= n <= last:
-                work.append(functools.partial(stage_b, n - 1, [shard]))
-            if 2 <= n < last + 2:
-                work.append(functools.partial(stage_c, n - 2, [shard]))
+            if n < wave_count:
+                work.append(functools.partial(stage_a, waves[n], [shard]))
+            if 1 <= n <= wave_count:
+                work.append(functools.partial(stage_b, waves[n - 1], [shard]))
+            if 2 <= n < wave_count + 2:
+                work.append(functools.partial(stage_c, waves[n - 2], [shard]))
             if n in (2, 4, 6, 8):
                 work.append(functools.partial(part_stage, n // 2 - 1, shard))
         return work
@@ -717,12 +719,12 @@
     for step in summing[:4]:
         step()
 
-    for n in range(count + 4):
+    for n in range(count):
         sends = send_list(n)
         work = compute_list(n)
-        if 0 <= n - 3 < count:
-            complete(n - 3)
-            start_weight(n - 3)
+        if 0 <= n - 3 < wave_count - 2:
+            complete(waves[n - 3])
+            start_weight(waves[n - 3])
         slots = max(len(work), 1)
         for i in range(slots):
             for send in sends[len(sends) * i // slots : len(sends) * (i + 1) // slots]:
@@ -731,6 +733,15 @@
                 work[i]()
         if n < 2:
             summing[4 + n]()
+    for piece in (alone - 1, alone):
+        complete(piece)
+        start_weight(piece)
+    for work in compute_list(alone + 2) + send_list(count) + compute_list(alone + 3):
+        work()
+    complete(count - 1)
+    start_weight(count - 1)
+    for work in compute_list(count + 2):
+        work()
 
     for index in (3, 4, 5, 6, 7, 8, 12, 13, 14, 15):
         write_result(index).wait()
@@ -747,9 +758,9 @@
             def _():
                 part_copy(step, shard, (me + groups - 1) % groups, part_left).wait_send()
 
-    sent = pieces[last].at[pl.ds(0, others), pl.ds(0, 4 * part)]
-    remote(sent, sent, send_sem.at[last], sib_sem.at[last], (sib, me)).wait_send()
-    for piece in range(last):
+    sent = pieces[alone].at[pl.ds(0, others), pl.ds(0, 4 * part)]
+    remote(sent, sent, send_sem.at[alone], sib_sem.at[alone], (sib, me)).wait_send()
+    for piece in waves:
         for shard in range(groups):
 
             @pl.when(jnp.logical_and(shard <= me, me + 1 < groups))
@@ -812,9 +823,10 @@
             jax.ShapeDtypeStruct(stats_shape, jnp.float32),
             *made,
             jax.ShapeDtypeStruct((2, span, rel.shape[0]), dtype),
+            jax.ShapeDtypeStruct((16, columns), jnp.float32),
         ),
         in_specs=[kept] * 7 + [inside] * 5,
-        out_specs=[kept] * 6 + [inside] * 3 + [kept] * len(made) + [inside],
+        out_specs=[kept] * 6 + [inside] * 3 + [kept] * len(made) + [inside] * 2,
         scratch_shapes=[
             pltpu.VMEM((count - 1, rows, columns), dtype),
             pltpu.VMEM((rows, 2 * width), dtype),
@@ -829,7 +841,6 @@
             pltpu.VMEM((2, columns, columns), dtype),
             pltpu.SemaphoreType.DMA((2, groups)),
             pltpu.SemaphoreType.DMA((len(made) + 2,)),
-            pltpu.VMEM((16, columns), jnp.float32),
             pltpu.VMEM(wide, dtype),
             pltpu.VMEM(wide, jnp.float32),
             pltpu.VMEM(wide, dtype),
@@ -934,6 +945,7 @@
     lefts_got = [hidden_got] + [left_got.at[index] for index in range(4)]
     left_of = [0, 1, 1, 2, 3, 3, 4, 4, 4, 4, 0, 4]
     right_of = [0, 1, 2, 3, 4, 5, 6, 6, 6, 6, 0, 6]
+    sequence = [0, 10, 1, 2, 3, 4, 5, 6, 11, 7, 8, 9]
     tap_of = {6: 0, 7: 1, 8: 2, 9: 3, 11: 4}
     mixed_piece = 5
     normal = 10
@@ -979,9 +991,10 @@
         ]
 
     def start_loads(piece):
-        if left_of[piece] not in left_of[:piece]:
+        before = sequence[: sequence.index(piece)]
+        if left_of[piece] not in [left_of[other] for other in before]:
             left_copy(left_of[piece]).wait_recv()
-        if right_of[piece] not in right_of[:piece]:
+        if right_of[piece] not in [right_of[other] for other in before]:
             right_copy(right_of[piece]).wait_recv()
         for copy in loads(piece):
             copy.start()
@@ -1198,8 +1211,7 @@
             copy.wait_send()
 
     def extra_start(piece, e):
-        for copy in loads(piece):
-            copy.start()
+        start_loads(piece)
         if e > 0:
             slab_sent(piece - 1, e - 1)
         wait_loads(piece)
@@ -1519,7 +1531,7 @@
 
     def rel_step():
         for shard in range(groups):
-            value = dot_leading(table[...], table_grad_ref[:, shard * 128 : (shard + 1) * 128])
+            value = dot_leading(table[1], table_grad_ref[:, shard * 128 : (shard + 1) * 128])
             rel_grad[shard] = value.astype(rel_grad.dtype).reshape(rel_grad.shape[1:])
         rel_copy().start()
 
@@ -1565,12 +1577,12 @@
     def batch_back():
         def rows_fn(at):
             value = wide_hold[at, columns : 2 * columns].astype(jnp.float32)
-            standard = (value - params[4:5, :]) * params[5:6, :]
+            standard = (value - params[9:10, :]) * params[10:11, :]
             normed = standard * params[0:1, :] + params[3:4, :]
             value = total_ref[at, :] * gelu_slope(normed)
             put(0, value * standard)
             put(3, value)
-            attn_grad[at, :] += params[5:6, :] * params[0:1, :] * value
+            attn_grad[at, :] += params[10:11, :] * params[0:1, :] * value
 
         by_rows(rows_fn)
 
@@ -1809,12 +1821,12 @@
     slots = 4
     ring = 3 if blocks == 1 else 2
     narrow = heads[2].shape
-    span = table.shape[0]
+    span = table.shape[1]
     kept = pl.BlockSpec(memory_space=pl.ANY)
     inside = pl.BlockSpec(memory_space=pltpu.VMEM)
     each = pltpu.SemaphoreType.DMA((count,))
     wide = (length, columns)
-    rel_shape = (groups, 2, table.shape[1] // 2, 128)
+    rel_shape = (groups, 2, table.shape[2] // 2, 128)
     sums = (16, columns)
     inputs = [*lefts, *saved, *weights, *heads]
     half_got = (ring, groups, part, width // 2)
@@ -1967,8 +1979,8 @@
         up_full,
         down_full,
         _,
-        small_full,
-        stats,
+        _,
+        _,
         activated,
         after_conv,
         normed_one,
@@ -1986,6 +1998,7 @@
         outputs,
         cotangent,
         tables,
+        params,
     ) = gather(
         groups,
         blocks,
@@ -2010,22 +2023,6 @@
     out_full = out_full.reshape(model_width, -1)
     up_full = up_full.reshape(model_width, -1)
     down_full = down_full.reshape(-1, model_width)
-    flat = small_full.reshape(groups, -1)
-    taken = 0
-    unpacked = []
-    for part in small_parts:
-        chosen = flat[:, taken : taken + part.size].reshape((groups,) + part.shape)
-        unpacked.append(chosen)
-        taken += part.size
-    gain_rows = jnp.moveaxis(unpacked[0], 0, 1).reshape(gains.shape[0], -1)
-    bias_rows = jnp.moveaxis(unpacked[1], 0, 1).reshape(biases.shape[0], -1)
-    batch_sums = stats.reshape(2, -1)
-    centre = batch_sums[0] / token_total
-    variance = batch_sums[1] / token_total - centre * centre
-    inverse = lax.rsqrt(variance + EPSILON)
-    standard = (inputs - centre) * inverse
-    params = jnp.concatenate([gain_rows, bias_rows[:1], centre[None], inverse[None]], 0)
-    params = jnp.pad(params, ((0, 2), (0, 0)))
     pieces, sums, part_grad, *_ = reduce(
         groups,
         blocks,
@@ -2035,9 +2032,10 @@
         [down_full, up_full, out_full, value_full, mixed_full, conv_full],
         [probs, values, keys, content_query, position_query, mirrored_keys],
         params,
-        tables[1],
+        tables,
     )
-    input_grad = part_grad - inverse * gain_rows[0] * (
+    standard = (inputs - params[9]) * params[10]
+    input_grad = part_grad - params[10] * params[0] * (
         sums[3] + standard * sums[0]
     ) / token_total
     shard = lax.axis_index("fsdp")

time: 588 us -> 579 us (0.985)
  no operation moved by 1% of the time
where the time goes in v7:
time: 579 us; the launch traced here: 574 us
  Pallas kernels  538 us (93%)
  other arithmetic  23.6 us (4%)
  local copies, waits for them, and re-layouts  11.1 us (2%)
    pallas_call x1, Pallas kernels, reduce(): pl.pallas_call(functools.partial(reduce_kernel, groups, blocks, rel_at),...  324 us
    pallas_call x1, Pallas kernels, gather(): pl.pallas_call(functools.partial(gather_kernel, groups, blocks), out_shap...  213 us

profile of v7, /device:TPU:0, one launch (start us, length us, event | category | flops | bytes accessed | tf_op | source)
XLA Modules:
  0.0 573.9 jit_solution(9153238673802390035)
XLA Ops:
  0.6 0.0 copy-start
  0.7 0.8 reshape.76
  1.4 0.7 reshape.75
  2.1 1.3 fusion.1.refs_8_
  4.1 0.0 copy-done
  4.1 0.6 constant_dynamic-slice_fusion.3.refs_10_
  4.7 0.8 select_reduce_fusion
  5.5 0.8 broadcast_in_dim.6.refs_11_
  6.3 213.2 %gather.1 = (bf16[5,4,384,1536]{3,2,1,0:T(8,128)(2,1)}, bf16[4,384,1024]{2,1,0:T(8,128)(2,1)}, bf16[4,384,1536]{2,1,0:T(8,128)(2,1)}, bf16[4,384,1536]{2,1,0:T(8...) custom-call(bf16[5,384,1536]{2,1,0:T(8,128)(2,1)} %refs_0_.1, ...), custom_call_target="tpu_custom_call" | custom-call | tf_op jit(solution)/shard_map/gather/pallas_call | solution.py:812
  219.5 0.0 copy-start.2
  219.5 324.4 %reduce.13 = (bf16[12,384,1536]{2,1,0:T(8,128)(2,1)}, f32[16,1536]{1,0:T(8,128)}, f32[512,1536]{1,0:T(8,128)}, bf16[512,3072]{1,0:T(8,128)(2,1)}, bf16[512,1536]...) custom-call(bf16[512,3072]{1,0:T(8,128)(2,1)} %get-tuple-element.42., ...), custom_call_target="tpu_custom_call" | custom-call | tf_op jit(solution)/shard_map/reduce/pallas_call | solution.py:1834
  544.0 1.0 slice_reduce_fusion.2
  545.0 0.0 copy-done.2
  545.0 3.9 fusion
  548.9 5.7 slice_bitcast_fusion.1
  554.6 2.6 slice.78
  557.2 5.3 maximum_convert_fusion
  562.5 1.3 fusion.2
  563.8 0.7 slice.99
  564.4 2.8 maximum_convert_fusion.1
  567.2 0.0 copy-start.4
  567.2 0.0 copy-start.3
  567.2 0.0 copy-start.1
  567.2 2.8 maximum_convert_fusion.2
  570.0 0.0 copy-done.4
  570.1 0.6 copy.39
  570.7 0.6 copy.38
  571.3 0.6 dynamic-slice_reduce_fusion
  571.9 0.6 constant_dynamic-slice_fusion.1
  572.5 0.0 copy-done.3
  572.5 1.1 copy.42
  573.6 0.0 copy-done.1
  (6 shorter events, 0.1 us)
Async XLA Ops:
  0.6 3.5 copy-start
  219.5 325.5 %copy-start.2 = (bf16[1,512,1536]{2,1,0:T(8,128)(2,1)S(1)}, bf16[1,512,1536]{2,1,0:T(8,128)(2,1)}, u32[]{:S(2)}) copy-start(bf16[1,512,1536]{2,1,0:T(8,128)(2,1)} %param.17) | copy-start | bytes 4718596
  567.2 2.8 copy-start.4
  567.2 5.3 copy-start.3
  567.2 6.5 %copy-start.1 = (f32[64,1536]{1,0:T(8,128)S(1)}, f32[64,1536]{1,0:T(8,128)}, u32[]{:S(2)}) copy-start(f32[64,1536]{1,0:T(8,128)} %param.30) | copy-start | bytes 1179652

commit v8 on v7

--- a/solution.py
+++ b/solution.py
@@ -381,7 +381,7 @@
 
     length = inputs.shape[0]
     block_rows = 128
-    tile = 256
+    tile = 512
     per_row = rows // 128
     token_total = length * 8 * blocks * groups
 

time: 579 us -> 578 us (level)
  no operation moved by 1% of the time
where the time goes in v8:
time: 578 us; the launch traced here: 573 us
  Pallas kernels  536 us (93%)
  other arithmetic  23.6 us (4%)
  local copies, waits for them, and re-layouts  11.1 us (2%)
    pallas_call x1, Pallas kernels, reduce(): pl.pallas_call(functools.partial(reduce_kernel, groups, blocks, rel_at),...  324 us
    pallas_call x1, Pallas kernels, gather(): pl.pallas_call(functools.partial(gather_kernel, groups, blocks), out_shap...  212 us

profile of v8, /device:TPU:0, one launch (start us, length us, event | category | flops | bytes accessed | tf_op | source)
XLA Modules:
  0.0 572.5 jit_solution(17917035789106379520)
XLA Ops:
  0.6 0.0 copy-start
  0.7 0.8 reshape.76
  1.4 0.7 reshape.75
  2.1 1.3 fusion.1.refs_8_
  4.1 0.0 copy-done
  4.1 0.6 constant_dynamic-slice_fusion.3.refs_10_
  4.7 0.8 select_reduce_fusion
  5.5 0.8 broadcast_in_dim.6.refs_11_
  6.3 211.9 %gather.1 = (bf16[5,4,384,1536]{3,2,1,0:T(8,128)(2,1)}, bf16[4,384,1024]{2,1,0:T(8,128)(2,1)}, bf16[4,384,1536]{2,1,0:T(8,128)(2,1)}, bf16[4,384,1536]{2,1,0:T(8...) custom-call(bf16[5,384,1536]{2,1,0:T(8,128)(2,1)} %refs_0_.1, ...), custom_call_target="tpu_custom_call" | custom-call | tf_op jit(solution)/shard_map/gather/pallas_call | solution.py:812
  218.3 0.0 copy-start.2
  218.3 324.3 %reduce.13 = (bf16[12,384,1536]{2,1,0:T(8,128)(2,1)}, f32[16,1536]{1,0:T(8,128)}, f32[512,1536]{1,0:T(8,128)}, bf16[512,3072]{1,0:T(8,128)(2,1)}, bf16[512,1536]...) custom-call(bf16[512,3072]{1,0:T(8,128)(2,1)} %get-tuple-element.42., ...), custom_call_target="tpu_custom_call" | custom-call | tf_op jit(solution)/shard_map/reduce/pallas_call | solution.py:1834
  542.6 1.0 slice_reduce_fusion.2
  543.6 0.0 copy-done.2
  543.6 3.9 fusion
  547.5 5.7 slice_bitcast_fusion.1
  553.2 2.6 slice.78
  555.9 5.3 maximum_convert_fusion
  561.1 1.3 fusion.2
  562.4 0.7 slice.99
  563.0 2.8 maximum_convert_fusion.1
  565.8 0.0 copy-start.4
  565.8 0.0 copy-start.3
  565.8 0.0 copy-start.1
  565.8 2.8 maximum_convert_fusion.2
  568.6 0.0 copy-done.4
  568.7 0.6 copy.39
  569.3 0.6 copy.38
  569.9 0.6 dynamic-slice_reduce_fusion
  570.6 0.6 constant_dynamic-slice_fusion.1
  571.1 0.0 copy-done.3
  571.1 1.1 copy.42
  572.3 0.0 copy-done.1
  (6 shorter events, 0.1 us)
Async XLA Ops:
  0.6 3.5 copy-start
  218.3 325.3 %copy-start.2 = (bf16[1,512,1536]{2,1,0:T(8,128)(2,1)S(1)}, bf16[1,512,1536]{2,1,0:T(8,128)(2,1)}, u32[]{:S(2)}) copy-start(bf16[1,512,1536]{2,1,0:T(8,128)(2,1)} %param.17) | copy-start | bytes 4718596
  565.8 2.8 copy-start.4
  565.8 5.3 copy-start.3
  565.8 6.5 %copy-start.1 = (f32[64,1536]{1,0:T(8,128)S(1)}, f32[64,1536]{1,0:T(8,128)}, u32[]{:S(2)}) copy-start(f32[64,1536]{1,0:T(8,128)} %param.30) | copy-start | bytes 1179652
